TPU v7x, 128 devices: a whole 4x4x4 slice. The times are simulated.
128 devices in a mesh: dp: 8 (over x, core), blk: 16 (over y, z).
Axes of the slice: x: 4, y: 4, z: 4, core: 2. Of those that a mesh axis runs over, the one named last changes fastest.
Arguments:
- embedding: bfloat16 [512, 256, 1024], P(('dp', 'blk')), may hold values from -6 to 6
- subspace: float32 [512, 256, 64], P(('dp', 'blk')), may hold values from -6 to 6
- degree: float32 [512, 256], P(('dp', 'blk')), may hold values from 300 to 3000
- neighbours: int32 [512, 16], P(('dp', 'blk')), may hold values from 0 to 63, as said below
- counts: int32 [512], P(('dp', 'blk')), may hold values from 1 to 16, as said below
Outputs:
- basis_next: float32 [512, 256, 64], P(('dp', 'blk'))
Inputs may be any that keep to these rules, and one draw needn't show every extreme that they name: `neighbours`: block g's slots name blocks of its own group by index inside the group, never g itself; the used slots of a block name distinct blocks; slots from counts[g] on are unused. `counts`: some block uses all 16 slots in every draw.
All inputs are finite; a program needn't handle non-finite values.
Results may differ from a plain program's by a relative error of at most 0.0042.
Values may be sent and summed in bfloat16 or wider, within the bound.
No kernel may reach another device: no remote copies, remote signals or barrier semaphores. Data moves between devices by JAX's collectives and lax.ppermute only.
A program may use at most 128 MiB of HBM per device.

v0:
```python
import math

import jax
import jax.numpy as jnp
from jax import lax
from jax.sharding import PartitionSpec as P


def affinity(left, right, left_sq, right_sq):
    feature = left.shape[-1]
    cross = lax.dot_general(
        left, right, (((1,), (1,)), ((), ())), preferred_element_type=jnp.float32
    )
    distance = left_sq[:, None] + right_sq[None, :] - 2.0 * cross
    return jnp.exp((2.0 * feature - distance) / (4.0 * math.sqrt(feature))).astype(jnp.bfloat16)


def transposed(tile, values):
    return lax.dot_general(
        tile, values, (((0,), (0,)), ((), ())), preferred_element_type=jnp.float32
    )


def own_term(packed):
    block_x, block_sq, block_u = packed
    diagonal_mask = jnp.eye(block_x.shape[0], dtype=bool)
    tile = jnp.where(
        diagonal_mask, jnp.zeros((), jnp.bfloat16), affinity(block_x, block_x, block_sq, block_sq)
    )
    return jnp.dot(tile, block_u, preferred_element_type=jnp.float32)


def per_device(embedding, subspace, degree, neighbours, counts):
    own_blocks, block_rows, feature = embedding.shape
    columns = subspace.shape[-1]
    devices_blk = lax.axis_size("blk")
    position = lax.axis_index("blk")
    group = own_blocks * devices_blk
    offset_own = position * own_blocks
    slot_total = neighbours.shape[1]
    inv_root = 1.0 / jnp.sqrt(degree)
    scaled = (subspace * inv_root[..., None]).astype(jnp.bfloat16)
    squares = jnp.sum(jnp.square(embedding.astype(jnp.float32)), axis=-1)
    self_part = lax.map(own_term, (embedding, squares, scaled))
    initial = jnp.zeros((group, block_rows, columns), jnp.float32)
    running = initial
    start = jnp.int32(0)
    piece_x = lax.all_gather(embedding, "blk", axis=0, tiled=True)
    piece_u = lax.all_gather(scaled, "blk", axis=0, tiled=True)
    piece_len = piece_x.shape[0]
    piece_sq = jnp.sum(jnp.square(piece_x.astype(jnp.float32)), axis=-1)

    def own_slot(counter, running):
        source = counter // slot_total
        slot_id = counter % slot_total
        target = neighbours[source, slot_id]
        inside = (slot_id < counts[source]) & (target >= start) & (target < start + piece_len)

        def compute(running):
            local = jnp.clip(target, 0, piece_len - 1)
            tile = affinity(embedding[source], piece_x[local], squares[source], piece_sq[local])
            forward = jnp.dot(tile, piece_u[local], preferred_element_type=jnp.float32)
            running = running.at[offset_own + source].add(forward)
            return running.at[target].add(transposed(tile, scaled[source]))

        return lax.cond(inside, compute, lambda kept: kept, running)

    running = lax.fori_loop(0, own_blocks * slot_total, own_slot, running)
    mine = lax.psum_scatter(running, "blk", scatter_dimension=0, tiled=True)
    product = mine + self_part
    image = product * inv_root[..., None]
    flat = image.reshape(-1, columns)
    local_gram = jnp.dot(flat.T, flat, precision=lax.Precision.HIGHEST)
    gram = lax.psum(local_gram, ("dp", "blk")) / (flat.shape[0] * lax.axis_size("dp") * devices_blk)
    lower = jnp.linalg.cholesky(gram)
    solved = jax.scipy.linalg.solve_triangular(lower, flat.T, lower=True)
    return solved.T.reshape(image.shape)


def solution(mesh):
    placed = (
        P(("dp", "blk"), None, None),
        P(("dp", "blk"), None, None),
        P(("dp", "blk"), None),
        P(("dp", "blk"), None),
        P(("dp", "blk")),
    )
    return jax.shard_map(
        per_device,
        mesh=mesh,
        in_specs=placed,
        out_specs=P(("dp", "blk"), None, None),
        check_vma=False,
    )
```

profile of v0, /device:TPU:0, one launch (start us, length us, event | category | flops | bytes accessed | tf_op | source)
XLA Modules:
  0.0 1325.0 jit_solution(9574203510479591794)
XLA Ops:
  7.4 1.6 multiply_convert_fusion
  11.4 45.9 %all-gather.5.cloned.1.call-done = bf16[64,256,64]{1,2,0:T(8,128)(2,1)} async-done(((bf16[4,256,64]{1,2,0:T(8,128)(2,1)}), bf16[64,256,64]{1,2,0:T(8,128)(2,1)}) %all-gather.5.cloned.1.call-update) | async-done | bytes 2097168 | tf_op jit(solution)/shard_map/all_gather | solution.py:49
  57.3 4.8 copy.12
  62.1 193.8 %all-gather.3.cloned.1.call-done = bf16[64,256,1024]{2,1,0:T(8,128)(2,1)} async-done(((bf16[4,256,1024]{2,1,0:T(8,128)(2,1)}), bf16[64,256,1024]{2,1,0:T(8,128)(2,1)}) %all-gather.3.cloned.1.call-update) | async-done | bytes 33554448 | tf_op jit(solution)/shard_map/all_gather | solution.py:48
  255.9 11.3 multiply_reduce_fusion
  267.3 2.5 broadcast_in_dim.22
  269.7 378.5 %while.30 = (s32[]{:T(128)}, f32[64,256,64]{1,2,0:T(8,128)}, s32[4]{0:T(128)S(1)}, s32[4,16]{1,0:T(4,128)}, s32[]{:T(128)}, /*index=5*/f32[4,256]{1,0:T(4,128)S(...) while((s32[]{:T(128)}, f32[64,256,64]{1,2,0:T(8,128)}, ...), condition=%wide.region_7.8_spmd, body=%wide.region_2.7_spmd.sunk | while | flops 151453776 | bytes 1843886 | solution.py:68
  273.5 10.1 conditional.2
  277.5 1.5 and_reduce_fusion
  278.9 2.4 fusion.10
  281.3 2.4 fusion.7
  287.5 10.1 conditional.2
  291.4 1.5 and_reduce_fusion
  292.9 2.4 fusion.10
  295.3 2.4 fusion.7
  301.4 10.1 conditional.2
  305.4 1.5 and_reduce_fusion
  306.8 2.4 fusion.10
  309.2 2.3 fusion.7
  365.7 10.1 conditional.2
  369.7 1.5 and_reduce_fusion
  371.1 2.4 fusion.10
  373.5 2.3 fusion.7
  379.6 10.1 conditional.2
  383.6 1.5 and_reduce_fusion
  385.0 2.4 fusion.10
  387.4 2.4 fusion.7
  393.6 10.1 conditional.2
  397.5 1.5 and_reduce_fusion
  399.0 2.4 fusion.10
  401.3 2.3 fusion.7
  407.5 10.1 conditional.2
  411.5 1.5 and_reduce_fusion
  412.9 2.4 fusion.10
  415.3 2.3 fusion.7
  467.9 10.1 conditional.2
  471.8 1.5 and_reduce_fusion
  473.3 2.4 fusion.10
  475.6 2.3 fusion.7
  481.8 10.1 conditional.2
  485.8 1.5 and_reduce_fusion
  487.2 2.4 fusion.10
  489.6 2.3 fusion.7
  495.7 10.1 conditional.2
  499.7 1.5 and_reduce_fusion
  501.1 2.4 fusion.10
  503.5 2.3 fusion.7
  560.0 10.1 conditional.2
  563.9 1.5 and_reduce_fusion
  565.4 2.4 fusion.10
  567.8 2.3 fusion.7
  573.9 10.1 conditional.2
  579.3 2.4 fusion.10
  581.7 2.4 fusion.7
  587.9 10.1 conditional.2
  591.8 1.5 and_reduce_fusion
  593.3 2.4 fusion.10
  595.6 2.3 fusion.7
  648.3 2.0 while.31
  650.3 587.7 %reduce-scatter.2.cloned.1.call-done = f32[4,256,64]{1,2,0:T(8,128)} async-done(((f32[64,256,64]{1,2,0:T(8,128)}), f32[4,256,64]{1,2,0:T(8,128)}) %reduce-scatter.2.cloned.1.call-update) | async-done | bytes 262160 | tf_op jit(solution)/shard_map/reduce_scatter | solution.py:69
  1239.4 64.8 %psum.7 = f32[64,64]{0,1:T(8,128)S(1)} all-reduce(f32[64,64]{0,1:T(8,128)S(1)} %convolution_bitcast_fusion.2), channel_id=1, replica_groups=mesh['dp'=8,'blk'=16] {'dp','blk'}, use_global_device_ids=true, to_apply=%region_11.12 | all-reduce | flops 4096 | bytes 32768 | tf_op jit(solution)/shard_map/psum | solution.py:74
  1304.3 5.8 cholesky.16
  1311.5 4.9 custom-call.7
  1316.4 2.1 fusion.50
  (235 shorter events, 151.5 us)
Async XLA Ops:
  6.5 4.4 copy-start
  6.5 50.8 %all-gather.5.cloned.1.call-start = ((), (), s32[]{:S(2)}) async-start(), calls=%async_computation.2 | async-start | bytes 2228224 | tf_op jit(solution)/shard_map/all_gather | solution.py:49
  9.0 246.9 %all-gather.3.cloned.1.call-start = ((), (), s32[]{:S(2)}) async-start(), calls=%async_computation.1 | async-start | bytes 35651584 | tf_op jit(solution)/shard_map/all_gather | solution.py:48
  9.8 1228.2 %reduce-scatter.2.cloned.1.call-start = ((), (), s32[]{:S(2)}) async-start(), calls=%async_computation.3 | async-start | bytes 4456448 | tf_op jit(solution)/shard_map/reduce_scatter | solution.py:69
  267.2 2.5 copy-start.1
Sparse Core Ops, SparseCore 0:
  9.5 47.7 all-gather.4
  59.4 196.4 all-gather.2
  648.4 589.5 reduce-scatter.1
where the time goes:
time: 1340 us; the launch traced here: 1320 us
  waiting for transfers between devices  828 us (62%)
  loops' own time  157 us (12%)
  local copies, waits for them, and re-layouts  133 us (10%)
  matrix products  84.9 us (6%)
  blocking collectives  64.8 us (5%)
  other arithmetic  44.4 us (3%)
    reduce_scatter x1, waiting for transfers between devices, per_device(): mine = lax.psum_scatter(running, 'blk', scatter_dimension=0, tiled=True)  588 us
    all_gather x1, waiting for transfers between devices, per_device(): piece_x = lax.all_gather(embedding, 'blk', axis=0, tiled=True)  194 us
    another operation x1, loops' own time, per_device(): running = lax.fori_loop(0, own_blocks * slot_total, own_slot, running)  123 us
    dynamic_slice x64, local copies, waits for them, and re-layouts, own_slot(): target = neighbours[source, slot_id]  84.5 us
    psum x1, blocking collectives, per_device(): lax.psum(local_gram, ('dp', 'blk'))  64.8 us
    all_gather x1, waiting for transfers between devices, per_device(): piece_u = lax.all_gather(scaled, 'blk', axis=0, tiled=True)  45.9 us
    dynamic_slice x64, local copies, waits for them, and re-layouts, own_slot(): counts[source]  38.7 us
    another operation x64, loops' own time, own_slot(): return lax.cond(inside, compute, lambda kept: kept, running)  33.7 us
  transfers between devices with their start and end apart: 3, of which 3 were waited for; matrix products, arithmetic and copies ran while one was open for 1% of the time, Pallas kernels for 0%

commit v1 on v0

v1 whole, which is shorter than its diff:
```python
import functools
import math

import jax
import jax.numpy as jnp
from jax import lax
from jax.experimental import pallas as pl
from jax.experimental.pallas import tpu as pltpu
from jax.sharding import PartitionSpec as P

ROWS = 256
FEAT = 1024
COLS = 64
OWN = 4
SIDE = 4
HALF = OWN // 2 * ROWS
DOCS = OWN * ROWS
META = 16
SCALED = 32
Z_ROWS = META + DOCS
Z_CUT = META + HALF
Y_X = SCALED + META
Y_ROWS = Y_X + DOCS + SCALED
Y_CUT = Y_X + HALF
LOG2E = 1.4426950408889634
GAIN = 2.0 * LOG2E / (4.0 * math.sqrt(FEAT))
BIAS = 2.0 * FEAT * LOG2E / (4.0 * math.sqrt(FEAT))
SQ_GAIN = -LOG2E / (4.0 * math.sqrt(FEAT))

NT = (((1,), (1,)), ((), ()))
NN = (((1,), (0,)), ((), ()))


def dot(a, b, dims):
    return lax.dot_general(a, b, dims, preferred_element_type=jnp.float32)


def prep_kernel(nbr_ref, cnt_ref, x_ref, sub_ref, deg_ref, py_ref, pz_ref, small, sems):
    copies = [
        pltpu.make_async_copy(x_ref, pz_ref.at[pl.ds(META, DOCS)], sems.at[0]),
        pltpu.make_async_copy(x_ref, py_ref.at[pl.ds(Y_X, DOCS)], sems.at[1]),
    ]
    for copy in copies:
        copy.start()
    lane = lax.broadcasted_iota(jnp.int32, (1, 128), 1)
    ones = jnp.ones((META, FEAT), jnp.bfloat16)
    squares = []
    adjacency = []
    for b in range(OWN):
        x = x_ref[b * ROWS:(b + 1) * ROWS, :].astype(jnp.float32)
        sq = x * x
        high = sq.astype(jnp.bfloat16)
        low = (sq - high.astype(jnp.float32)).astype(jnp.bfloat16)
        squares.append(dot(ones, high, NT) + dot(ones, low, NT))
        row = jnp.zeros((1, 128), jnp.float32)
        for k in range(nbr_ref.shape[1]):
            used = (k < cnt_ref[b]).astype(jnp.float32)
            row = row + jnp.where(lane == nbr_ref[b, k], used, 0.0)
        adjacency.append(row)
        inv = 1.0 / jnp.sqrt(deg_ref[b:b + 1, :])
        scaled = (sub_ref[b].T * inv).astype(jnp.bfloat16)
        packed = jnp.concatenate([scaled[16 * g:16 * (g + 1), :] for g in range(4)], axis=1)
        place = 16 * b if b < 2 else SCALED + META + 16 * (b - 2)
        small[place:place + 16, :] = packed
    total = jnp.concatenate(squares, axis=1)
    s_high = total.astype(jnp.bfloat16).astype(jnp.float32)
    rest = total - s_high
    s_mid = rest.astype(jnp.bfloat16).astype(jnp.float32)
    s_low = rest - s_mid
    which = lax.broadcasted_iota(jnp.int32, (META, FEAT), 0)
    meta = jnp.where(which == 0, s_high, jnp.where(which == 1, s_mid, jnp.where(which == 2, s_low, 0.0)))
    pad = jnp.zeros((1, FEAT - 128), jnp.float32)
    for b in range(OWN):
        wide = jnp.concatenate([adjacency[b], pad], axis=1)
        meta = jnp.where(which == 4 + b, wide, meta)
    small[SCALED:SCALED + META, :] = meta.astype(jnp.bfloat16)
    tail = [
        pltpu.make_async_copy(small.at[pl.ds(0, Y_X)], py_ref.at[pl.ds(0, Y_X)], sems.at[2]),
        pltpu.make_async_copy(small.at[pl.ds(Y_X, SCALED)], py_ref.at[pl.ds(Y_X + DOCS, SCALED)], sems.at[3]),
        pltpu.make_async_copy(small.at[pl.ds(SCALED, META)], pz_ref.at[pl.ds(0, META)], sems.at[4]),
    ]
    for copy in tail:
        copy.start()
    for copy in copies + tail:
        copy.wait()


def prepare(embedding, subspace, degree, neighbours, counts):
    smem = pl.BlockSpec(memory_space=pltpu.SMEM)
    vmem = pl.BlockSpec(memory_space=pltpu.VMEM)
    hbm = pl.BlockSpec(memory_space=pl.ANY)
    return pl.pallas_call(
        prep_kernel,
        out_shape=(
            jax.ShapeDtypeStruct((Y_ROWS, FEAT), jnp.bfloat16),
            jax.ShapeDtypeStruct((Z_ROWS, FEAT), jnp.bfloat16),
        ),
        in_specs=[smem, smem, vmem, vmem, vmem],
        out_specs=(hbm, hbm),
        scratch_shapes=[
            pltpu.VMEM((2 * SCALED + META, FEAT), jnp.bfloat16),
            pltpu.SemaphoreType.DMA((5,)),
        ],
        compiler_params=pltpu.CompilerParams(vmem_limit_bytes=24 * 2**20),
        name="prepare",
    )(neighbours, counts, embedding.reshape(DOCS, FEAT), subspace, degree)


def stage_kernel(second, *refs):
    slots = 16 if second else 12
    groups = slots // OWN
    n_side = 5 if second else 3
    idx_ref = refs[0]
    z_refs = refs[1:1 + n_side]
    y_refs = refs[1 + n_side:1 + 2 * n_side]
    rest = refs[1 + 2 * n_side:]
    if second:
        acc_in, rest = rest[0], rest[1:]
        outs, rest = rest[:4], rest[4:]
    else:
        acc_out, rest = rest[0], rest[1:]
    (r_x, c_x, c_s, c_pack, meta_r, meta_c, sq_r, sq_c, col, adj_vmem, adj_r, adj_c, acc,
     sem_r, sem_c, sem_s, sem_m, sem_a) = rest

    def source_z(group, half):
        if group < 3:
            return z_refs[group], META + half * HALF
        return (z_refs[3], META) if half == 0 else (z_refs[4], 0)

    def source_y(group, half):
        if group < 3:
            return y_refs[group], Y_X + half * HALF
        return (y_refs[3], Y_X) if half == 0 else (y_refs[4], 0)

    copies_m = []
    copies_s = []
    for g in range(groups):
        copies_m.append(pltpu.make_async_copy(z_refs[g].at[pl.ds(0, META)], meta_r.at[g], sem_m.at[g]))
        copies_m.append(pltpu.make_async_copy(y_refs[g].at[pl.ds(SCALED, META)], meta_c.at[g], sem_m.at[4 + g]))
        copies_s.append(pltpu.make_async_copy(y_refs[g].at[pl.ds(0, SCALED)], c_pack.at[g, pl.ds(0, SCALED)], sem_s.at[g]))
        far, start = (y_refs[g], Y_X + DOCS) if g < 3 else (y_refs[4], HALF)
        copies_s.append(pltpu.make_async_copy(far.at[pl.ds(start, SCALED)], c_pack.at[g, pl.ds(SCALED, SCALED)], sem_s.at[4 + g]))

    def copy_r(s):
        ref, start = source_z(s // OWN, s % OWN // 2)
        return pltpu.make_async_copy(ref.at[pl.ds(start + s % 2 * ROWS, ROWS)], r_x.at[s], sem_r.at[s])

    def copy_c(s):
        ref, start = source_y(s // OWN, s % OWN // 2)
        return pltpu.make_async_copy(ref.at[pl.ds(start + s % 2 * ROWS, ROWS)], c_x.at[s], sem_c.at[s])

    if second:
        pltpu.make_async_copy(acc_in, acc, sem_a.at[2]).start()
    for copy in copies_m:
        copy.start()
    first_r = range(12, 16) if second else range(12)
    for s in first_r:
        copy_r(s).start()
    copy_c(0).start()
    for copy in copies_s:
        copy.start()
    for s in range(1, slots):
        copy_c(s).start()
    if second:
        for s in range(12):
            copy_r(s).start()

    for copy in copies_m:
        copy.wait()
    for side, (meta, keep, adj) in enumerate(((meta_r, sq_r, adj_r), (meta_c, sq_c, adj_c))):
        for g in range(groups):
            m = meta[g].astype(jnp.float32)
            total = (m[0:1, :] + m[1:2, :] + m[2:3, :]) * SQ_GAIN
            if side == 0:
                total = total + BIAS
            for b in range(OWN):
                keep[g * OWN + b] = total[:, b * ROWS:(b + 1) * ROWS]
            adj_vmem[side, g * OWN:(g + 1) * OWN, :] = m[4:4 + OWN, 0:128].astype(jnp.int32)
        pltpu.make_async_copy(adj_vmem.at[side], adj, sem_a.at[side]).start()
    for copy in copies_s:
        copy.wait()
    for g in range(groups):
        for b in range(OWN):
            p = c_pack[g, 16 * b:16 * (b + 1), :]
            c_s[g * OWN + b] = jnp.concatenate([p[:, ROWS * k:ROWS * (k + 1)] for k in range(4)], axis=0)
    if second:
        pltpu.make_async_copy(acc_in, acc, sem_a.at[2]).wait()
    else:
        acc[...] = jnp.zeros_like(acc)
    for side, adj in enumerate((adj_r, adj_c)):
        pltpu.make_async_copy(adj_vmem.at[side], adj, sem_a.at[side]).wait()

    def body(c, r, weight, own):
        cross = dot(c_x[c], r_x[r], NT)
        tile = jnp.exp2(cross * GAIN + (jnp.concatenate([col[...], col[...]], axis=1) + sq_r[r])).astype(jnp.bfloat16)
        if own:
            row_id = lax.broadcasted_iota(jnp.int32, (ROWS, ROWS), 0)
            col_id = lax.broadcasted_iota(jnp.int32, (ROWS, ROWS), 1)
            tile = jnp.where(row_id == col_id, jnp.zeros_like(tile), tile)
        acc[r] = acc[r] + weight * dot(c_s[c], tile, NN)

    def sweep(c_lo, c_hi, r_lo, r_hi, wait_r):
        def per_c(c, carry):
            pltpu.make_async_copy(c_x.at[c], c_x.at[c], sem_c.at[c]).wait()
            col[...] = jnp.transpose(jnp.broadcast_to(sq_c[c], (128, ROWS)))
            block_c = idx_ref[1, c]

            def per_r(r, carry):
                @pl.when((c == c_lo) & (r >= wait_r[0]) & (r < wait_r[1]))
                def _():
                    pltpu.make_async_copy(r_x.at[r], r_x.at[r], sem_r.at[r]).wait()

                block_r = idx_ref[0, r]
                edges = adj_r[r, block_c] + adj_c[c, block_r]

                @pl.when(edges > 0)
                def _():
                    body(c, r, edges.astype(jnp.float32), False)

                if not second:
                    @pl.when(block_r == block_c)
                    def _():
                        body(c, r, 1.0, True)
                return carry

            return lax.fori_loop(r_lo, r_hi, per_r, carry)

        lax.fori_loop(c_lo, c_hi, per_c, 0)

    if second:
        sweep(0, 12, 12, 16, (12, 16))
        sweep(12, 16, 0, 16, (0, 12))
        for g in range(4):
            outs[g][...] = acc[g * OWN:(g + 1) * OWN]
    else:
        sweep(0, 12, 0, 12, (0, 12))
        acc_out[...] = acc[...]


def stage(second, index, z_parts, y_parts, acc=None):
    smem = pl.BlockSpec(memory_space=pltpu.SMEM)
    vmem = pl.BlockSpec(memory_space=pltpu.VMEM)
    hbm = pl.BlockSpec(memory_space=pl.ANY)
    slots = 16 if second else 12
    groups = slots // OWN
    operands = [index, *z_parts, *y_parts]
    in_specs = [smem] + [hbm] * (len(z_parts) + len(y_parts))
    if second:
        operands.append(acc)
        in_specs.append(hbm)
        out_shape = tuple(jax.ShapeDtypeStruct((OWN, COLS, ROWS), jnp.float32) for _ in range(4))
        out_specs = (vmem,) * 4
    else:
        out_shape = jax.ShapeDtypeStruct((16, COLS, ROWS), jnp.float32)
        out_specs = vmem
    return pl.pallas_call(
        functools.partial(stage_kernel, second),
        out_shape=out_shape,
        in_specs=in_specs,
        out_specs=out_specs,
        scratch_shapes=[
            pltpu.VMEM((slots, ROWS, FEAT), jnp.bfloat16),
            pltpu.VMEM((slots, ROWS, FEAT), jnp.bfloat16),
            pltpu.VMEM((slots, COLS, ROWS), jnp.bfloat16),
            pltpu.VMEM((groups, 2 * SCALED, FEAT), jnp.bfloat16),
            pltpu.VMEM((groups, META, FEAT), jnp.bfloat16),
            pltpu.VMEM((groups, META, FEAT), jnp.bfloat16),
            pltpu.VMEM((slots, 1, ROWS), jnp.float32),
            pltpu.VMEM((slots, 1, ROWS), jnp.float32),
            pltpu.VMEM((ROWS, 128), jnp.float32),
            pltpu.VMEM((2, 16, 128), jnp.int32),
            pltpu.SMEM((16, 128), jnp.int32),
            pltpu.SMEM((16, 128), jnp.int32),
            pltpu.VMEM((16, COLS, ROWS), jnp.float32),
            pltpu.SemaphoreType.DMA((16,)),
            pltpu.SemaphoreType.DMA((16,)),
            pltpu.SemaphoreType.DMA((8,)),
            pltpu.SemaphoreType.DMA((8,)),
            pltpu.SemaphoreType.DMA((3,)),
        ],
        compiler_params=pltpu.CompilerParams(vmem_limit_bytes=32 * 2**20),
        cost_estimate=pl.CostEstimate(flops=6 * 10**9, bytes_accessed=16 * 2**20, transcendentals=10**6),
        name="stage_two" if second else "stage_one",
    )(*operands)


def finish_kernel(deg_ref, own_ref, a_ref, b_ref, c_ref, image_ref, gram_ref):
    parts = []
    for b in range(OWN):
        inv = 1.0 / jnp.sqrt(deg_ref[b:b + 1, :])
        parts.append((own_ref[b] + a_ref[b] + (b_ref[b] + c_ref[b])) * inv)
    image = jnp.concatenate(parts, axis=1)
    image_ref[...] = image
    gram_ref[...] = lax.dot_general(
        image, image, NT, precision=lax.Precision.HIGHEST, preferred_element_type=jnp.float32
    )


def finish(degree, own, a, b, c):
    return pl.pallas_call(
        finish_kernel,
        out_shape=(
            jax.ShapeDtypeStruct((COLS, DOCS), jnp.float32),
            jax.ShapeDtypeStruct((COLS, COLS), jnp.float32),
        ),
        name="finish",
    )(degree, own, a, b, c)


def shift_z(k):
    return [(y * SIDE + z, y * SIDE + (z + k) % SIDE) for y in range(SIDE) for z in range(SIDE)]


def shift_y(k):
    return [(y * SIDE + z, (y + k) % SIDE * SIDE + z) for y in range(SIDE) for z in range(SIDE)]


def per_device(embedding, subspace, degree, neighbours, counts):
    position = lax.axis_index("blk")
    y, z = position // SIDE, position % SIDE
    order = (0, SIDE - 1, 1, 2)
    row_ids = jnp.stack([(y * SIDE + (z + k) % SIDE) * OWN + b for k in order for b in range(OWN)])
    col_ids = jnp.stack([((y + k) % SIDE * SIDE + z) * OWN + b for k in order for b in range(OWN)])
    index = jnp.stack([row_ids, col_ids]).astype(jnp.int32)

    pack_y, pack_z = prepare(embedding, subspace, degree, neighbours, counts)
    z_minus = lax.ppermute(pack_z, "blk", shift_z(1))
    z_plus = lax.ppermute(pack_z, "blk", shift_z(-1))
    y_minus = lax.ppermute(pack_y, "blk", shift_y(1))
    y_plus = lax.ppermute(pack_y, "blk", shift_y(-1))
    z_far_a = lax.ppermute(z_minus[:Z_CUT], "blk", shift_z(1))
    z_far_b = lax.ppermute(z_plus[Z_CUT:], "blk", shift_z(-1))
    y_far_a = lax.ppermute(y_minus[:Y_CUT], "blk", shift_y(1))
    y_far_b = lax.ppermute(y_plus[Y_CUT:], "blk", shift_y(-1))

    near_z = (pack_z, z_minus, z_plus)
    near_y = (pack_y, y_minus, y_plus)
    acc = stage(False, index, near_z, near_y)
    own, to_minus, to_plus, to_far = stage(
        True, index, near_z + (z_far_a, z_far_b), near_y + (y_far_a, y_far_b), acc
    )
    back_a = lax.ppermute(to_minus, "blk", shift_z(-1))
    back_b = lax.ppermute(to_plus, "blk", shift_z(1))
    back_c = lax.ppermute(to_far, "blk", shift_z(2))
    image, gram = finish(degree, own, back_a, back_b, back_c)

    devices_blk = lax.axis_size("blk")
    devices_dp = lax.axis_size("dp")
    step = 1
    while step < devices_blk:
        gram = gram + lax.ppermute(gram, "blk", [(i, i ^ step) for i in range(devices_blk)])
        step *= 2
    step = 1
    while step < devices_dp:
        gram = gram + lax.ppermute(gram, "dp", [(i, i ^ step) for i in range(devices_dp)])
        step *= 2
    gram = gram / (DOCS * devices_blk * devices_dp)
    lower = jnp.linalg.cholesky(gram)
    solved = jax.scipy.linalg.solve_triangular(lower, image, lower=True)
    return solved.T.reshape(OWN, ROWS, COLS)


def solution(mesh):
    placed = (
        P(("dp", "blk"), None, None),
        P(("dp", "blk"), None, None),
        P(("dp", "blk"), None),
        P(("dp", "blk"), None),
        P(("dp", "blk")),
    )
    return jax.shard_map(
        per_device,
        mesh=mesh,
        in_specs=placed,
        out_specs=P(("dp", "blk"), None, None),
        check_vma=False,
    )
```

time: 1340 us -> 193 us (0.14); the launches traced: 1320 us -> 193 us
  waiting for transfers between devices: 828 us -> 79 us
  loops' own time: 157 us -> 0 us
  local copies, waits for them, and re-layouts: 133 us -> 21.1 us
  matrix products: 84.9 us -> 2.09 us
  blocking collectives: 64.8 us -> 0 us
  Pallas kernels: 0 us -> 49 us
  other arithmetic: 44.4 us -> 12.1 us
  starting transfers between devices: 0.08 us -> 28.9 us
    reduce_scatter x1 -> x0, waiting for transfers between devices: 588 us -> none  [per_device(): mine = lax.psum_scatter(running, 'blk', scatter_dimension=0, tiled=True)]
    all_gather x2 -> x0, waiting for transfers between devices: 240 us -> none  [the longest x1 194 us: per_device(): piece_x = lax.all_gather(embedding, 'blk', axis=0, tiled=True)]
    another operation x66 -> x0, loops' own time: 157 us -> none  [the longest x1 123 us: per_device(): running = lax.fori_loop(0, own_blocks * slot_total, own_slot, running)]
    dynamic_slice x145 -> x0, local copies, waits for them, and re-layouts: 123 us -> none  [the longest x64 84.5 us: own_slot(): target = neighbours[source, slot_id]]
    dot_general x44 -> x0, matrix products: 82.8 us -> none  [the longest x13 30.8 us: compute(): forward = jnp.dot(tile, piece_u[local], preferred_element_type=jnp.float32)]
    ppermute x0 -> x18, waiting for transfers between devices: none -> 79 us  [the longest x1 44.9 us: per_device(): y_minus = lax.ppermute(pack_y, 'blk', shift_y(1))]
    psum x1 -> x0, blocking collectives: 64.8 us -> none  [per_device(): lax.psum(local_gram, ('dp', 'blk'))]
    pallas_call x0 -> x4, Pallas kernels: none -> 49 us  [the longest x2 44.3 us: stage(): pl.pallas_call(functools.partial(stage_kernel, second), out_shape=out_sha...]
  transfers between devices with their start and end apart: 3 -> 18, of which waited for: 3 -> 10; matrix products, arithmetic and copies ran while one was open for 1% -> 2% of each run, Pallas kernels for 0% -> 12%
where the time goes in v1:
time: 193 us
  waiting for transfers between devices  79 us (41%)
  Pallas kernels  49 us (25%)
  starting transfers between devices  28.9 us (15%)
  local copies, waits for them, and re-layouts  21.1 us (11%)
  other arithmetic  12.1 us (6%)
  matrix products  2.09 us (1%)
    ppermute x1, waiting for transfers between devices, per_device(): y_minus = lax.ppermute(pack_y, 'blk', shift_y(1))  44.9 us
    pallas_call x2, Pallas kernels, stage(): pl.pallas_call(functools.partial(stage_kernel, second), out_shape=out_sha...  44.3 us
    ppermute x4, waiting for transfers between devices, per_device(): lax.ppermute(gram, 'blk', [(i, i ^ step) for i in range(devices_blk)])  16 us
    unnamed x37, local copies, waits for them, and re-layouts  15.6 us
    ppermute x3, waiting for transfers between devices, per_device(): lax.ppermute(gram, 'dp', [(i, i ^ step) for i in range(devices_dp)])  10.3 us
    another operation x3, other arithmetic, per_device(): lower = jnp.linalg.cholesky(gram)  6.52 us
    ppermute x1, starting transfers between devices, per_device(): back_a = lax.ppermute(to_minus, 'blk', shift_z(-1))  5.6 us
    another operation x2, other arithmetic, per_device(): solved = jax.scipy.linalg.solve_triangular(lower, image, lower=True)  5.55 us
  transfers between devices with their start and end apart: 18, of which 10 were waited for; matrix products, arithmetic and copies ran while one was open for 2% of the time, Pallas kernels for 12%

profile of v1, /device:TPU:0, one launch (start us, length us, event | category | flops | bytes accessed | tf_op | source)
XLA Modules:
  0.0 192.5 jit_solution(9836060623559845654)
XLA Ops:
  0.0 1.1 copy.6.sub_ref
  1.2 0.0 copy-start
  1.2 1.6 copy-done
  2.8 0.7 copy-done.8
  3.4 0.7 copy-done.9
  4.1 0.7 copy-done.10
  4.8 2.6 %prepare.1 = (bf16[1104,1024]{1,0:T(8,128)(2,1)S(1)}, bf16[1040,1024]{1,0:T(8,128)(2,1)S(1)}) custom-call(s32[4,16]{1,0:T(4,128)S(1)} %copy-done.9, s32[4]{0:T(128)S(1)} %copy-done.10, bf16[1024,1024]{1,0:T(8,128)(2,1)S(1)} %bitcast.51, f32[4,256,64]{2,1,0:T(8,128)S(1)} %copy.6.sub_ref, f32[4,256]{1,0:T(4,128)S(1)} %copy-done.8), custom_call_target="tpu_custom_call" | custom-call | tf_op jit(solution)/shard_map/prepare/pallas_call | solution.py:92
  7.4 1.7 collective-permute-start.4
  9.1 1.6 collective-permute-start.5
  10.7 2.0 %collective-permute-start = (bf16[1040,1024]{1,0:T(8,128)(2,1)S(1)}, bf16[1040,1024]{1,0:T(8,128)(2,1)S(1)}, u32[]{:S(2)}, u32[]{:S(2)}) collective-permute-start(bf16[1040,1024]{1,0:T(8,128)(2,1)S(1)} %get-tuple-element.13.refs_1_), channel_id=1, source_target_pairs={{0,1},{1,2},{2,3},{3,0},{4,5},{5,6},{6,7},{7,4},{8,9},{9,10},{10,1... | collective-permute-start | bytes 6389768 | tf_op jit(solution)/shard_map/ppermute | solution.py:327
  12.7 2.1 %collective-permute-start.1 = (bf16[1040,1024]{1,0:T(8,128)(2,1)S(1)}, bf16[1040,1024]{1,0:T(8,128)(2,1)S(1)}, u32[]{:S(2)}, u32[]{:S(2)}) collective-permute-start(bf16[1040,1024]{1,0:T(8,128)(2,1)S(1)} %get-tuple-element.13.refs_1_), channel_id=1, source_target_pairs={{0,3},{1,0},{2,1},{3,2},{4,7},{5,4},{6,5},{7,6},{8,11},{9,8},{10,9... | collective-permute-start | bytes 6389768 | tf_op jit(solution)/shard_map/ppermute | solution.py:328
  14.8 44.9 %collective-permute-done.4.refs_5_.refs_7_ = bf16[1104,1024]{1,0:T(8,128)(2,1)S(1)} collective-permute-done((bf16[1104,1024]{1,0:T(8,128)(2,1)S(1)}, bf16[1104,1024]{1,0:T(8,128)(2,1)S(1)}, u32[]{:S(2)}, u32[]{:S(2)}) %collective-permute-start.4) | collective-permute-done | bytes 2261024 | tf_op jit(solution)/shard_map/ppermute | solution.py:329
  59.7 1.1 slice.30
  60.7 0.3 collective-permute-start.6
  61.0 0.0 collective-permute-done.5.refs_6_.refs_8_
  61.0 1.1 slice.31
  62.2 2.9 %collective-permute-start.7 = (bf16[544,1024]{1,0:T(8,128)(2,1)}, bf16[544,1024]{1,0:T(8,128)(2,1)}, u32[]{:S(2)}, u32[]{:S(2)}) collective-permute-start(bf16[544,1024]{1,0:T(8,128)(2,1)} %slice.31), channel_id=1, source_target_pairs={{0,12},{1,13},{2,14},{3,15},{4,0},{5,1},{6,2},{7,3},{8,4},{9,5},{1... | collective-permute-start | bytes 3342344 | tf_op jit(solution)/shard_map/ppermute | solution.py:334
  65.1 0.0 collective-permute-done.refs_2_
  65.1 1.1 slice.28
  66.2 1.9 collective-permute-start.2
  68.2 0.0 collective-permute-done.1.refs_3_
  68.2 1.1 slice.29
  69.2 1.3 copy-done.5
  70.6 2.1 %collective-permute-start.3 = (bf16[512,1024]{1,0:T(8,128)(2,1)}, bf16[512,1024]{1,0:T(8,128)(2,1)}, u32[]{:S(2)}, u32[]{:S(2)}) collective-permute-start(bf16[512,1024]{1,0:T(8,128)(2,1)} %slice.29), channel_id=1, source_target_pairs={{0,3},{1,0},{2,1},{3,2},{4,7},{5,4},{6,5},{7,6},{8,11},{9,8},{10,9... | collective-permute-start | bytes 3145736 | tf_op jit(solution)/shard_map/ppermute | solution.py:332
  72.7 0.1 stack.145
  72.8 0.1 stack.127
  72.9 1.6 copy-done.2
  74.5 1.6 copy-done.4
  76.2 1.6 copy-done.6
  77.8 1.6 copy-done.12
  79.4 1.6 copy-done.14
  81.0 22.8 %stage_one.1.refs_11_ = f32[16,64,256]{2,1,0:T(8,128)S(1)} custom-call(s32[2,16]{1,0:T(2,128)S(1)} %pad_add_fusion.refs_0_, bf16[1040,1024]{1,0:T(8,128)(2,1)S(1)} %copy-done.14, bf16[1040,1024]{1,0:T(8,128)(2,1)S(1)} %copy-done.2, bf16[1040,1024]{1,0:T(8,128)(2,1)S(1)} %copy-done.6, bf16[1104,1024]{1,0:T(8,128)(2,1)S(1)} %copy-done.12, ...), custom_call_target="tpu_custom_call" | custom-call | flops 6000000000 | bytes 16777216 | tf_op jit(solution)/shard_map/stage_one/pallas_call | solution.py:256
  103.8 0.0 collective-permute-done.3.refs_5_
  103.8 0.0 collective-permute-done.2.refs_4_
  103.8 0.0 collective-permute-done.6.refs_9_
  103.8 21.5 %stage_two.1 = (f32[4,64,256]{2,1,0:T(8,128)S(1)}, f32[4,64,256]{2,1,0:T(8,128)S(1)}, f32[4,64,256]{2,1,0:T(8,128)S(1)}, f32[4,64,256]{2,1,0:T(8,128)S(1)}) custom-call(s32[2,16]{1,0:T(2,128)S(1)} %pad_add_fusion.refs_0_, bf16[1040,1024]{1,0:T(8,128)(2,1)S(1)} %copy-done.14, bf16[1040,1024]{1,0:T(8,128)(2,1)S(1)} %copy-done.2, ...), custom_call_target="tpu_custom_call" | custom-call | flops 6000000000 | bytes 16777216 | tf_op jit(solution)/shard_map/stage_two/pallas_call | solution.py:256
  125.3 0.0 copy-start.7
  125.4 0.7 copy-done.7
  126.1 5.6 %collective-permute-start.8 = (f32[4,64,256]{2,1,0:T(8,128)S(1)}, f32[4,64,256]{2,1,0:T(8,128)S(1)}, u32[]{:S(2)}, u32[]{:S(2)}) collective-permute-start(f32[4,64,256]{2,1,0:T(8,128)S(1)} %get-tuple-element.16), channel_id=1, source_target_pairs={{0,3},{1,0},{2,1},{3,2},{4,7},{5,4},{6,5},{7,6},{8,11},{9,8},{10,9... | collective-permute-start | bytes 786440 | tf_op jit(solution)/shard_map/ppermute | solution.py:342
  131.6 0.0 collective-permute-start.9
  131.7 4.9 %collective-permute-start.10 = (f32[4,64,256]{2,1,0:T(8,128)S(1)}, f32[4,64,256]{2,1,0:T(8,128)S(1)}, u32[]{:S(2)}, u32[]{:S(2)}) collective-permute-start(f32[4,64,256]{2,1,0:T(8,128)S(1)} %get-tuple-element.18), channel_id=1, source_target_pairs={{0,2},{1,3},{2,0},{3,1},{4,6},{5,7},{6,4},{7,5},{8,10},{9,11},{10,... | collective-permute-start | bytes 786440 | tf_op jit(solution)/shard_map/ppermute | solution.py:344
  136.6 2.9 %collective-permute-done.9.b_ref = f32[4,64,256]{2,1,0:T(8,128)S(1)} collective-permute-done((f32[4,64,256]{2,1,0:T(8,128)S(1)}, f32[4,64,256]{2,1,0:T(8,128)S(1)}, u32[]{:S(2)}, u32[]{:S(2)}) %collective-permute-start.9) | collective-permute-done | bytes 262176 | tf_op jit(solution)/shard_map/ppermute | solution.py:343
  139.5 5.0 %collective-permute-done.10.c_ref = f32[4,64,256]{2,1,0:T(8,128)S(1)} collective-permute-done((f32[4,64,256]{2,1,0:T(8,128)S(1)}, f32[4,64,256]{2,1,0:T(8,128)S(1)}, u32[]{:S(2)}, u32[]{:S(2)}) %collective-permute-start.10) | collective-permute-done | bytes 262176 | tf_op jit(solution)/shard_map/ppermute | solution.py:344
  144.4 0.7 copy-done.17
  145.1 2.2 %finish.1 = (f32[64,1024]{1,0:T(8,128)}, f32[64,64]{1,0:T(8,128)}) custom-call(f32[4,256]{1,0:T(4,128)} %deg_ref.3, f32[4,64,256]{2,1,0:T(8,128)} %copy-done.7, f32[4,64,256]{2,1,0:T(8,128)} %copy-done.15, f32[4,64,256]{2,1,0:T(8,128)} %copy-done.16, f32[4,64,256]{2,1,0:T(8,128)} %copy-done.17), custom_call_target="tpu_custom_call" | custom-call | tf_op jit(solution)/shard_map/finish/pallas_call | solution.py:300
  147.3 0.8 copy.8
  148.2 0.1 collective-permute-start.11
  148.2 3.9 %collective-permute-done.11 = f32[64,64]{0,1:T(8,128)S(1)} collective-permute-done((f32[64,64]{0,1:T(8,128)S(1)}, f32[64,64]{0,1:T(8,128)S(1)}, u32[]{:S(2)}, u32[]{:S(2)}) %collective-permute-start.11) | collective-permute-done | bytes 16416 | tf_op jit(solution)/shard_map/ppermute | solution.py:351
  152.2 0.0 collective-permute-start.12
  152.2 5.4 %collective-permute-done.12 = f32[64,64]{0,1:T(8,128)S(1)} collective-permute-done((f32[64,64]{0,1:T(8,128)S(1)}, f32[64,64]{0,1:T(8,128)S(1)}, u32[]{:S(2)}, u32[]{:S(2)}) %collective-permute-start.12) | collective-permute-done | bytes 16416 | tf_op jit(solution)/shard_map/ppermute | solution.py:351
  157.6 2.8 %collective-permute-start.13 = (f32[64,64]{0,1:T(8,128)S(1)}, f32[64,64]{0,1:T(8,128)S(1)}, u32[]{:S(2)}, u32[]{:S(2)}) collective-permute-start(f32[64,64]{0,1:T(8,128)S(1)} %add.290), channel_id=1, source_target_pairs={{0,4},{1,5},{2,6},{3,7},{4,0},{5,1},{6,2},{7,3},{8,12},{9,13},{10,... | collective-permute-start | bytes 49160 | tf_op jit(solution)/shard_map/ppermute | solution.py:351
  160.4 1.9 collective-permute-done.13
  162.3 0.6 collective-permute-start.14
  162.8 4.8 %collective-permute-done.14 = f32[64,64]{0,1:T(8,128)S(1)} collective-permute-done((f32[64,64]{0,1:T(8,128)S(1)}, f32[64,64]{0,1:T(8,128)S(1)}, u32[]{:S(2)}, u32[]{:S(2)}) %collective-permute-start.14) | collective-permute-done | bytes 16416 | tf_op jit(solution)/shard_map/ppermute | solution.py:351
  167.7 1.2 collective-permute-done.15
  168.9 3.9 %collective-permute-done.16 = f32[64,64]{0,1:T(8,128)S(1)} collective-permute-done((f32[64,64]{0,1:T(8,128)S(1)}, f32[64,64]{0,1:T(8,128)S(1)}, u32[]{:S(2)}, u32[]{:S(2)}) %collective-permute-start.16) | collective-permute-done | bytes 16416 | tf_op jit(solution)/shard_map/ppermute | solution.py:355
  172.8 0.3 collective-permute-start.17
  173.1 5.2 %collective-permute-done.17 = f32[64,64]{0,1:T(8,128)S(1)} collective-permute-done((f32[64,64]{0,1:T(8,128)S(1)}, f32[64,64]{0,1:T(8,128)S(1)}, u32[]{:S(2)}, u32[]{:S(2)}) %collective-permute-start.17) | collective-permute-done | bytes 16416 | tf_op jit(solution)/shard_map/ppermute | solution.py:355
  178.2 0.1 copy.9
  178.3 5.8 %cholesky.16 = f32[64,64]{1,0:T(8,128)S(1)} custom-call(f32[64,64]{1,0:T(8,128)S(1)} %fusion.5), custom_call_target="Cholesky" | custom-call | tf_op jit(solution)/shard_map/jit(cholesky)/cholesky | solution.py:358
  184.2 0.6 compare_reduce_fusion
  184.9 0.7 fusion.3
  185.5 4.9 %custom-call.7 = f32[1,64,64]{1,2,0:T(8,128)S(1)} custom-call(f32[1,64,64]{2,1,0:T(8,128)S(1)} %fusion.3), custom_call_target="InvertDiagBlocksLowerTriangular" | custom-call | tf_op jit(solution)/shard_map/jit(_solve_triangular)/triangular_solve | solution.py:359
  190.4 2.1 %fusion = f32[4,256,64]{1,2,0:T(8,128)} fusion(f32[8,4,8,256]{3,2,1,0:T(8,128)} %bitcast.52, f32[1,64,64]{1,2,0:T(8,128)S(1)} %custom-call.7), kind=kOutput, calls=%fused_computation | convolution fusion | flops 50331648 | bytes 540672 | tf_op jit(solution)/shard_map/jit(_solve_triangular)/triangular_solve | solution.py:359
  (36 shorter events, 0.1 us)
Async XLA Ops:
  1.2 1.6 copy-start
  2.7 0.7 copy-start.8
  3.4 0.7 copy-start.9
  4.1 0.7 copy-start.10
  7.3 54.9 %copy-start.11 = (bf16[1104,1024]{1,0:T(8,128)(2,1)}, bf16[1104,1024]{1,0:T(8,128)(2,1)S(1)}, u32[]{:S(2)}) copy-start(bf16[1104,1024]{1,0:T(8,128)(2,1)S(1)} %get-tuple-element.14.refs_4_.refs_6_) | copy-start | bytes 6782980
  7.3 54.8 %copy-start.13 = (bf16[1040,1024]{1,0:T(8,128)(2,1)}, bf16[1040,1024]{1,0:T(8,128)(2,1)S(1)}, u32[]{:S(2)}) copy-start(bf16[1040,1024]{1,0:T(8,128)(2,1)S(1)} %get-tuple-element.13.refs_1_) | copy-start | bytes 6389764
  7.4 52.3 %collective-permute-start.4 = (bf16[1104,1024]{1,0:T(8,128)(2,1)S(1)}, bf16[1104,1024]{1,0:T(8,128)(2,1)S(1)}, u32[]{:S(2)}, u32[]{:S(2)}) collective-permute-start(bf16[1104,1024]{1,0:T(8,128)(2,1)S(1)} %get-tuple-element.14.refs_4_.refs_6_), channel_id=1, source_target_pairs={{0,4},{1,5},{2,6},{3,7},{4,8},{5,9},{6,10},{7,11},{8,12},{9,13},{1... | collective-permute-start | bytes 6782984 | tf_op jit(solution)/shard_map/ppermute | solution.py:329
  9.1 52.0 %collective-permute-start.5 = (bf16[1104,1024]{1,0:T(8,128)(2,1)S(1)}, bf16[1104,1024]{1,0:T(8,128)(2,1)S(1)}, u32[]{:S(2)}, u32[]{:S(2)}) collective-permute-start(bf16[1104,1024]{1,0:T(8,128)(2,1)S(1)} %get-tuple-element.14.refs_4_.refs_6_), channel_id=1, source_target_pairs={{0,12},{1,13},{2,14},{3,15},{4,0},{5,1},{6,2},{7,3},{8,4},{9,5},{1... | collective-permute-start | bytes 6782984 | tf_op jit(solution)/shard_map/ppermute | solution.py:330
  10.7 54.5 %collective-permute-start = (bf16[1040,1024]{1,0:T(8,128)(2,1)S(1)}, bf16[1040,1024]{1,0:T(8,128)(2,1)S(1)}, u32[]{:S(2)}, u32[]{:S(2)}) collective-permute-start(bf16[1040,1024]{1,0:T(8,128)(2,1)S(1)} %get-tuple-element.13.refs_1_), channel_id=1, source_target_pairs={{0,1},{1,2},{2,3},{3,0},{4,5},{5,6},{6,7},{7,4},{8,9},{9,10},{10,1... | collective-permute-start | bytes 6389768 | tf_op jit(solution)/shard_map/ppermute | solution.py:327
  12.7 55.5 %collective-permute-start.1 = (bf16[1040,1024]{1,0:T(8,128)(2,1)S(1)}, bf16[1040,1024]{1,0:T(8,128)(2,1)S(1)}, u32[]{:S(2)}, u32[]{:S(2)}) collective-permute-start(bf16[1040,1024]{1,0:T(8,128)(2,1)S(1)} %get-tuple-element.13.refs_1_), channel_id=1, source_target_pairs={{0,3},{1,0},{2,1},{3,2},{4,7},{5,4},{6,5},{7,6},{8,11},{9,8},{10,9... | collective-permute-start | bytes 6389768 | tf_op jit(solution)/shard_map/ppermute | solution.py:328
  60.7 43.1 %collective-permute-start.6 = (bf16[560,1024]{1,0:T(8,128)(2,1)}, bf16[560,1024]{1,0:T(8,128)(2,1)S(1)}, u32[]{:S(2)}, u32[]{:S(2)}) collective-permute-start(bf16[560,1024]{1,0:T(8,128)(2,1)} %slice.30), channel_id=1, source_target_pairs={{0,4},{1,5},{2,6},{3,7},{4,8},{5,9},{6,10},{7,11},{8,12},{9,13},{1... | collective-permute-start | bytes 3440648 | tf_op jit(solution)/shard_map/ppermute | solution.py:333
  61.0 5.2 %copy-start.3 = (bf16[1104,1024]{1,0:T(8,128)(2,1)}, bf16[1104,1024]{1,0:T(8,128)(2,1)S(1)}, u32[]{:S(2)}) copy-start(bf16[1104,1024]{1,0:T(8,128)(2,1)S(1)} %collective-permute-done.5.refs_6_.refs_8_) | copy-start | bytes 6782980
  62.2 41.6 %collective-permute-start.7 = (bf16[544,1024]{1,0:T(8,128)(2,1)}, bf16[544,1024]{1,0:T(8,128)(2,1)}, u32[]{:S(2)}, u32[]{:S(2)}) collective-permute-start(bf16[544,1024]{1,0:T(8,128)(2,1)} %slice.31), channel_id=1, source_target_pairs={{0,12},{1,13},{2,14},{3,15},{4,0},{5,1},{6,2},{7,3},{8,4},{9,5},{1... | collective-permute-start | bytes 3342344 | tf_op jit(solution)/shard_map/ppermute | solution.py:334
  65.1 4.1 %copy-start.1 = (bf16[1040,1024]{1,0:T(8,128)(2,1)}, bf16[1040,1024]{1,0:T(8,128)(2,1)S(1)}, u32[]{:S(2)}) copy-start(bf16[1040,1024]{1,0:T(8,128)(2,1)S(1)} %collective-permute-done.refs_2_) | copy-start | bytes 6389764
  66.2 37.6 %collective-permute-start.2 = (bf16[528,1024]{1,0:T(8,128)(2,1)}, bf16[528,1024]{1,0:T(8,128)(2,1)}, u32[]{:S(2)}, u32[]{:S(2)}) collective-permute-start(bf16[528,1024]{1,0:T(8,128)(2,1)} %slice.28), channel_id=1, source_target_pairs={{0,1},{1,2},{2,3},{3,0},{4,5},{5,6},{6,7},{7,4},{8,9},{9,10},{10,1... | collective-permute-start | bytes 3244040 | tf_op jit(solution)/shard_map/ppermute | solution.py:331
  69.2 1.3 copy-start.5
  70.6 33.2 %collective-permute-start.3 = (bf16[512,1024]{1,0:T(8,128)(2,1)}, bf16[512,1024]{1,0:T(8,128)(2,1)}, u32[]{:S(2)}, u32[]{:S(2)}) collective-permute-start(bf16[512,1024]{1,0:T(8,128)(2,1)} %slice.29), channel_id=1, source_target_pairs={{0,3},{1,0},{2,1},{3,2},{4,7},{5,4},{6,5},{7,6},{8,11},{9,8},{10,9... | collective-permute-start | bytes 3145736 | tf_op jit(solution)/shard_map/ppermute | solution.py:332
  72.9 1.6 copy-start.2
  74.5 1.6 copy-start.4
  76.2 1.6 copy-start.6
  77.8 1.6 copy-start.12
  79.4 1.6 copy-start.14
  125.3 0.7 copy-start.7
  126.1 10.5 %collective-permute-start.8 = (f32[4,64,256]{2,1,0:T(8,128)S(1)}, f32[4,64,256]{2,1,0:T(8,128)S(1)}, u32[]{:S(2)}, u32[]{:S(2)}) collective-permute-start(f32[4,64,256]{2,1,0:T(8,128)S(1)} %get-tuple-element.16), channel_id=1, source_target_pairs={{0,3},{1,0},{2,1},{3,2},{4,7},{5,4},{6,5},{7,6},{8,11},{9,8},{10,9... | collective-permute-start | bytes 786440 | tf_op jit(solution)/shard_map/ppermute | solution.py:342
  131.6 7.8 %collective-permute-start.9 = (f32[4,64,256]{2,1,0:T(8,128)S(1)}, f32[4,64,256]{2,1,0:T(8,128)S(1)}, u32[]{:S(2)}, u32[]{:S(2)}) collective-permute-start(f32[4,64,256]{2,1,0:T(8,128)S(1)} %get-tuple-element.17), channel_id=1, source_target_pairs={{0,1},{1,2},{2,3},{3,0},{4,5},{5,6},{6,7},{7,4},{8,9},{9,10},{10,1... | collective-permute-start | bytes 786440 | tf_op jit(solution)/shard_map/ppermute | solution.py:343
  131.7 12.8 %collective-permute-start.10 = (f32[4,64,256]{2,1,0:T(8,128)S(1)}, f32[4,64,256]{2,1,0:T(8,128)S(1)}, u32[]{:S(2)}, u32[]{:S(2)}) collective-permute-start(f32[4,64,256]{2,1,0:T(8,128)S(1)} %get-tuple-element.18), channel_id=1, source_target_pairs={{0,2},{1,3},{2,0},{3,1},{4,6},{5,7},{6,4},{7,5},{8,10},{9,11},{10,... | collective-permute-start | bytes 786440 | tf_op jit(solution)/shard_map/ppermute | solution.py:344
  136.6 7.9 %copy-start.15 = (f32[4,64,256]{2,1,0:T(8,128)}, f32[4,64,256]{2,1,0:T(8,128)S(1)}, u32[]{:S(2)}) copy-start(f32[4,64,256]{2,1,0:T(8,128)S(1)} %collective-permute-done.8.a_ref) | copy-start | bytes 786436
  139.5 5.0 %copy-start.16 = (f32[4,64,256]{2,1,0:T(8,128)}, f32[4,64,256]{2,1,0:T(8,128)S(1)}, u32[]{:S(2)}) copy-start(f32[4,64,256]{2,1,0:T(8,128)S(1)} %collective-permute-done.9.b_ref) | copy-start | bytes 786436
  144.4 0.7 copy-start.17
  148.2 4.0 %collective-permute-start.11 = (f32[64,64]{0,1:T(8,128)S(1)}, f32[64,64]{0,1:T(8,128)S(1)}, u32[]{:S(2)}, u32[]{:S(2)}) collective-permute-start(f32[64,64]{0,1:T(8,128)S(1)} %copy.8), channel_id=1, source_target_pairs={{0,1},{1,0},{2,3},{3,2},{4,5},{5,4},{6,7},{7,6},{8,9},{9,8},{10,11... | collective-permute-start | bytes 49160 | tf_op jit(solution)/shard_map/ppermute | solution.py:351
  152.2 5.4 %collective-permute-start.12 = (f32[64,64]{0,1:T(8,128)S(1)}, f32[64,64]{0,1:T(8,128)S(1)}, u32[]{:S(2)}, u32[]{:S(2)}) collective-permute-start(f32[64,64]{0,1:T(8,128)S(1)} %add.289), channel_id=1, source_target_pairs={{0,2},{1,3},{2,0},{3,1},{4,6},{5,7},{6,4},{7,5},{8,10},{9,11},{10,... | collective-permute-start | bytes 49160 | tf_op jit(solution)/shard_map/ppermute | solution.py:351
  157.6 4.7 %collective-permute-start.13 = (f32[64,64]{0,1:T(8,128)S(1)}, f32[64,64]{0,1:T(8,128)S(1)}, u32[]{:S(2)}, u32[]{:S(2)}) collective-permute-start(f32[64,64]{0,1:T(8,128)S(1)} %add.290), channel_id=1, source_target_pairs={{0,4},{1,5},{2,6},{3,7},{4,0},{5,1},{6,2},{7,3},{8,12},{9,13},{10,... | collective-permute-start | bytes 49160 | tf_op jit(solution)/shard_map/ppermute | solution.py:351
  162.3 5.4 %collective-permute-start.14 = (f32[64,64]{0,1:T(8,128)S(1)}, f32[64,64]{0,1:T(8,128)S(1)}, u32[]{:S(2)}, u32[]{:S(2)}) collective-permute-start(f32[64,64]{0,1:T(8,128)S(1)} %add.291), channel_id=1, source_target_pairs={{0,8},{1,9},{2,10},{3,11},{4,12},{5,13},{6,14},{7,15},{8,0},{9,1},... | collective-permute-start | bytes 49160 | tf_op jit(solution)/shard_map/ppermute | solution.py:351
  167.7 1.2 collective-permute-start.15
  168.9 3.9 %collective-permute-start.16 = (f32[64,64]{0,1:T(8,128)S(1)}, f32[64,64]{0,1:T(8,128)S(1)}, u32[]{:S(2)}, u32[]{:S(2)}) collective-permute-start(f32[64,64]{0,1:T(8,128)S(1)} %add.293), channel_id=1, source_target_pairs={{0,32},{16,48},{32,0},{48,16},{64,96},{80,112},{96,64},{112,80},{1... | collective-permute-start | bytes 49160 | tf_op jit(solution)/shard_map/ppermute | solution.py:355
  172.8 5.4 %collective-permute-start.17 = (f32[64,64]{0,1:T(8,128)S(1)}, f32[64,64]{0,1:T(8,128)S(1)}, u32[]{:S(2)}, u32[]{:S(2)}) collective-permute-start(f32[64,64]{0,1:T(8,128)S(1)} %add.294), channel_id=1, source_target_pairs={{0,64},{16,80},{32,96},{48,112},{64,0},{80,16},{96,32},{112,48},{1... | collective-permute-start | bytes 49160 | tf_op jit(solution)/shard_map/ppermute | solution.py:355

commit v2 on v0

v2 whole, which is shorter than its diff:
```python
import functools
import math

import jax
import jax.numpy as jnp
from jax import lax
from jax.experimental import pallas as pl
from jax.experimental.pallas import tpu as pltpu
from jax.sharding import PartitionSpec as P

ROWS = 256
FEAT = 1024
COLS = 64
OWN = 4
SIDE = 4
HALF = OWN // 2 * ROWS
DOCS = OWN * ROWS
META = 16
SCALED = 32
UNIT = 2
UNITS = 2 * SIDE
Z_ROWS = META + HALF
Y_X = SCALED + META
Y_ROWS = Y_X + HALF
GROUPED = 4
VMEM_LIMIT = 62 * 2**20
ARRIVAL = ((0, 0), (0, 1), (-1, 0), (1, 1), (-1, 1), (1, 0), (2, 0), (2, 1))
LOG2E = 1.4426950408889634
GAIN = 2.0 * LOG2E / (4.0 * math.sqrt(FEAT))
BIAS = 2.0 * FEAT * LOG2E / (4.0 * math.sqrt(FEAT))
SQ_GAIN = -LOG2E / (4.0 * math.sqrt(FEAT))

NT = (((1,), (1,)), ((), ()))
NN = (((1,), (0,)), ((), ()))


def dot(a, b, dims):
    return lax.dot_general(a, b, dims, preferred_element_type=jnp.float32)


def prep_kernel(nbr_hbm, cnt_hbm, x_hbm, sub_hbm, deg_hbm, za_ref, zb_ref, ya_ref, yb_ref,
                nbr_ref, cnt_ref, x_ref, sub_ref, deg_ref, small, sems):
    loads = [
        pltpu.make_async_copy(x_hbm.at[pl.ds(b * ROWS, ROWS)], x_ref.at[pl.ds(b * ROWS, ROWS)], sems.at[b])
        for b in range(OWN)
    ]
    extra = [
        pltpu.make_async_copy(nbr_hbm, nbr_ref, sems.at[4]),
        pltpu.make_async_copy(cnt_hbm, cnt_ref, sems.at[5]),
        pltpu.make_async_copy(deg_hbm, deg_ref, sems.at[6]),
        pltpu.make_async_copy(sub_hbm, sub_ref, sems.at[7]),
    ]
    for copy in loads + extra:
        copy.start()
    stores = []

    def store(source, target, which):
        copy = pltpu.make_async_copy(source, target, sems.at[which])
        copy.start()
        stores.append(copy)

    ones = jnp.ones((META, FEAT), jnp.bfloat16)
    squares = []
    for b in range(OWN):
        half, place = b // UNIT, b % UNIT * ROWS
        loads[b].wait()
        source = x_ref.at[pl.ds(b * ROWS, ROWS)]
        store(source, (za_ref, zb_ref)[half].at[pl.ds(META + place, ROWS)], 8 + b)
        store(source, (ya_ref, yb_ref)[half].at[pl.ds(Y_X + place, ROWS)], 12 + b)
        x = x_ref[b * ROWS:(b + 1) * ROWS, :].astype(jnp.float32)
        sq = x * x
        high = sq.astype(jnp.bfloat16)
        low = (sq - high.astype(jnp.float32)).astype(jnp.bfloat16)
        squares.append(dot(ones, high, NT) + dot(ones, low, NT))
    for copy in extra:
        copy.wait()
    lane = lax.broadcasted_iota(jnp.int32, (1, 128), 1)
    which = lax.broadcasted_iota(jnp.int32, (META, FEAT), 0)
    pad = jnp.zeros((1, FEAT - 128), jnp.float32)
    for half in range(2):
        total = jnp.concatenate(squares[half * UNIT:(half + 1) * UNIT] + [jnp.zeros((META, FEAT - HALF), jnp.float32)], axis=1)
        s_high = total.astype(jnp.bfloat16).astype(jnp.float32)
        rest = total - s_high
        s_mid = rest.astype(jnp.bfloat16).astype(jnp.float32)
        s_low = rest - s_mid
        meta = jnp.where(which == 0, s_high, jnp.where(which == 1, s_mid, jnp.where(which == 2, s_low, 0.0)))
        for i in range(UNIT):
            b = half * UNIT + i
            row = jnp.zeros((1, 128), jnp.float32)
            for k in range(nbr_ref.shape[1]):
                used = (k < cnt_ref[b]).astype(jnp.float32)
                row = row + jnp.where(lane == nbr_ref[b, k], used, 0.0)
            meta = jnp.where(which == 4 + i, jnp.concatenate([row, pad], axis=1), meta)
            inv = 1.0 / jnp.sqrt(deg_ref[b:b + 1, :])
            scaled = (sub_ref[b] * inv).astype(jnp.bfloat16)
            small[half, 16 * i:16 * (i + 1), :] = jnp.concatenate(
                [scaled[16 * g:16 * (g + 1), :] for g in range(4)], axis=1
            )
        small[half, SCALED:Y_X, :] = meta.astype(jnp.bfloat16)
        store(small.at[half], (ya_ref, yb_ref)[half].at[pl.ds(0, Y_X)], 16 + half)
        store(small.at[half, pl.ds(SCALED, META)], (za_ref, zb_ref)[half].at[pl.ds(0, META)], 18 + half)
    for copy in stores:
        copy.wait()


def prepare(embedding, subspace, degree, neighbours, counts):
    hbm = pl.BlockSpec(memory_space=pltpu.HBM)
    return pl.pallas_call(
        prep_kernel,
        out_shape=(jax.ShapeDtypeStruct((Z_ROWS, FEAT), jnp.bfloat16),) * 2
        + (jax.ShapeDtypeStruct((Y_ROWS, FEAT), jnp.bfloat16),) * 2,
        in_specs=[hbm] * 5,
        out_specs=(hbm,) * 4,
        scratch_shapes=[
            pltpu.SMEM(neighbours.shape, jnp.int32),
            pltpu.SMEM(counts.shape, jnp.int32),
            pltpu.VMEM((DOCS, FEAT), jnp.bfloat16),
            pltpu.VMEM((OWN, COLS, ROWS), jnp.float32),
            pltpu.VMEM((OWN, ROWS), jnp.float32),
            pltpu.VMEM((2, Y_X, FEAT), jnp.bfloat16),
            pltpu.SemaphoreType.DMA((20,)),
        ],
        compiler_params=pltpu.CompilerParams(vmem_limit_bytes=VMEM_LIMIT),
        name="prepare",
    )(neighbours, counts, embedding.reshape(DOCS, FEAT), jnp.swapaxes(subspace, 1, 2), degree)


def stage_kernel(old, new, last, *refs):
    idx_ref = refs[0]
    z_refs = refs[1:1 + new]
    y_refs = refs[1 + new:1 + 2 * new]
    rest = refs[1 + 2 * new:]
    if old:
        acc_in, rest = rest[0], rest[1:]
    if last:
        outs, rest = rest[:4], rest[4:]
    else:
        acc_out, rest = rest[0], rest[1:]
    (r_x, c_x, c_s, c_pack, meta_r, meta_c, sq_r, sq_c, col, adj_vmem, adj_r, adj_c, codes, edge_list, acc,
     sem_r, sem_c, sem_s, sem_m, sem_n, sem_a) = rest
    old_slots, slots = UNIT * old, UNIT * new

    meta_copies = []
    pack_copies = []
    r_copies = []
    c_copies = []
    for u in range(new):
        meta_copies.append(pltpu.make_async_copy(z_refs[u].at[pl.ds(0, META)], meta_r.at[u], sem_m.at[u]))
        meta_copies.append(pltpu.make_async_copy(y_refs[u].at[pl.ds(SCALED, META)], meta_c.at[u], sem_n.at[u]))
        pack_copies.append(pltpu.make_async_copy(y_refs[u].at[pl.ds(0, SCALED)], c_pack.at[u], sem_s.at[u]))
        r_copies.append(pltpu.make_async_copy(z_refs[u].at[pl.ds(META, HALF)], r_x.at[u], sem_r.at[u]))
        c_copies.append(pltpu.make_async_copy(y_refs[u].at[pl.ds(Y_X, HALF)], c_x.at[u], sem_c.at[u]))
    if old:
        acc_copy = pltpu.make_async_copy(acc_in, acc, sem_a.at[2])
    for copy in meta_copies:
        copy.start()
    for copy in r_copies[old:] + c_copies[:old] + pack_copies:
        copy.start()
    if old:
        acc_copy.start()
    for copy in c_copies[old:] + r_copies[:old]:
        copy.start()

    for copy in meta_copies:
        copy.wait()
    for side, (meta, keep, adj) in enumerate(((meta_r, sq_r, adj_r), (meta_c, sq_c, adj_c))):
        for u in range(new):
            m = meta[u].astype(jnp.float32)
            total = (m[0:1, 0:HALF] + m[1:2, 0:HALF] + m[2:3, 0:HALF]) * SQ_GAIN
            for i in range(UNIT):
                piece = total[:, i * ROWS:(i + 1) * ROWS]
                if side == 0:
                    keep[u * UNIT + i] = piece + BIAS
                else:
                    keep[u * UNIT + i:u * UNIT + i + 1, :] = piece
            adj_vmem[side, u * UNIT:(u + 1) * UNIT, :] = m[4:4 + UNIT, 0:128].astype(jnp.int32)
        pltpu.make_async_copy(adj_vmem.at[side], adj, sem_a.at[side]).start()
    columns = jnp.transpose(sq_c[...])
    for s in range(slots):
        col[s] = jnp.broadcast_to(columns[:, s:s + 1], (ROWS, 128))
    for copy in pack_copies:
        copy.wait()
    for s in range(slots):
        p = c_pack[s // UNIT, 16 * (s % UNIT):16 * (s % UNIT + 1), :]
        c_s[s] = jnp.concatenate([p[:, ROWS * k:ROWS * (k + 1)] for k in range(4)], axis=0)
    for side, adj in enumerate((adj_r, adj_c)):
        pltpu.make_async_copy(adj_vmem.at[side], adj, sem_a.at[side]).wait()

    def form(pairs, diagonal):
        cross = [
            dot(c_x[c // UNIT, pl.ds(c % UNIT * ROWS, ROWS), :], r_x[r // UNIT, pl.ds(r % UNIT * ROWS, ROWS), :], NT)
            for c, r, _ in pairs
        ]
        terms = []
        for (c, r, weight), value in zip(pairs, cross):
            bias = jnp.concatenate([col[c], col[c]], axis=1) + sq_r[r]
            tile = jnp.exp2(value * GAIN + bias)
            if diagonal:
                row_id = lax.broadcasted_iota(jnp.int32, (ROWS, ROWS), 0)
                col_id = lax.broadcasted_iota(jnp.int32, (ROWS, ROWS), 1)
                tile = jnp.where(row_id == col_id, 0.0, tile)
            term = dot(c_s[c], tile.astype(jnp.bfloat16), NN)
            terms.append(term if diagonal else term * weight)
        for (c, r, _), term in zip(pairs, terms):
            acc[r] = acc[r] + term

    def list_tiles(c_lo, c_hi, r_lo, r_hi):
        def per_c(c, count):
            block_c = idx_ref[1, c]
            for r in range(r_lo, r_hi):
                edges = adj_r[r, block_c] + adj_c[c, idx_ref[0, r]]
                codes[count] = c * 16 + r
                edge_list[count] = edges
                count = count + (edges > 0).astype(jnp.int32)
            return count

        count = lax.fori_loop(c_lo, c_hi, per_c, 0)
        for i in range(GROUPED - 1):
            codes[count + i] = codes[0]
            edge_list[count + i] = 0
        return count

    def run_tiles(count):
        def step(t, carry):
            pairs = []
            for i in range(GROUPED):
                code = codes[t * GROUPED + i]
                pairs.append((code // 16, code % 16, edge_list[t * GROUPED + i].astype(jnp.float32)))
            form(pairs, False)
            return carry

        lax.fori_loop(0, (count + GROUPED - 1) // GROUPED, step, 0)

    if old:
        count = list_tiles(0, old_slots, old_slots, slots)
        for copy in [acc_copy] + r_copies[old:] + c_copies[:old]:
            copy.wait()
        run_tiles(count)
        count = list_tiles(old_slots, slots, 0, slots)
        for copy in c_copies[old:] + r_copies[:old]:
            copy.wait()
        run_tiles(count)
    else:
        acc[...] = jnp.zeros_like(acc)
        count = list_tiles(0, slots, 0, slots)
        for copy in c_copies + r_copies:
            copy.wait()
        form([(s, s, None) for s in range(OWN)], True)
        run_tiles(count)
    if last:
        for out, order in zip(outs, ((0, 1, 2, 3), (4, 5, 8, 9), (10, 11, 6, 7), (12, 13, 14, 15))):
            for k, s in enumerate(order):
                out[k] = acc[s]
    else:
        acc_out[...] = acc[...]


def stage(old, new, index, z_parts, y_parts, acc=None):
    smem = pl.BlockSpec(memory_space=pltpu.SMEM)
    vmem = pl.BlockSpec(memory_space=pltpu.VMEM)
    hbm = pl.BlockSpec(memory_space=pltpu.HBM)
    last = new == UNITS
    operands = [index, *z_parts[:new], *y_parts[:new]]
    in_specs = [smem] + [hbm] * (2 * new)
    if old:
        operands.append(acc)
        in_specs.append(hbm)
    if last:
        out_shape = tuple(jax.ShapeDtypeStruct((OWN, COLS, ROWS), jnp.float32) for _ in range(4))
        out_specs = (vmem,) * 4
    else:
        out_shape = jax.ShapeDtypeStruct((16, COLS, ROWS), jnp.float32)
        out_specs = vmem
    slots = UNIT * new
    return pl.pallas_call(
        functools.partial(stage_kernel, old, new, last),
        out_shape=out_shape,
        in_specs=in_specs,
        out_specs=out_specs,
        scratch_shapes=[
            pltpu.VMEM((new, HALF, FEAT), jnp.bfloat16),
            pltpu.VMEM((new, HALF, FEAT), jnp.bfloat16),
            pltpu.VMEM((slots, COLS, ROWS), jnp.bfloat16),
            pltpu.VMEM((new, SCALED, FEAT), jnp.bfloat16),
            pltpu.VMEM((new, META, FEAT), jnp.bfloat16),
            pltpu.VMEM((new, META, FEAT), jnp.bfloat16),
            pltpu.VMEM((slots, 1, ROWS), jnp.float32),
            pltpu.VMEM((128, ROWS), jnp.float32),
            pltpu.VMEM((slots, ROWS, 128), jnp.float32),
            pltpu.VMEM((2, 16, 128), jnp.int32),
            pltpu.SMEM((16, 128), jnp.int32),
            pltpu.SMEM((16, 128), jnp.int32),
            pltpu.SMEM((264,), jnp.int32),
            pltpu.SMEM((264,), jnp.int32),
            pltpu.VMEM((16, COLS, ROWS), jnp.float32),
            pltpu.SemaphoreType.DMA((new,)),
            pltpu.SemaphoreType.DMA((new,)),
            pltpu.SemaphoreType.DMA((new,)),
            pltpu.SemaphoreType.DMA((new,)),
            pltpu.SemaphoreType.DMA((new,)),
            pltpu.SemaphoreType.DMA((3,)),
        ],
        compiler_params=pltpu.CompilerParams(vmem_limit_bytes=VMEM_LIMIT),
        cost_estimate=pl.CostEstimate(flops=6 * 10**9, bytes_accessed=16 * 2**20, transcendentals=10**6),
        name="stage_%d" % new,
    )(*operands)


def finish_kernel(deg_ref, own_ref, a_ref, b_ref, c_ref, image_ref, gram_ref):
    parts = []
    for b in range(OWN):
        inv = 1.0 / jnp.sqrt(deg_ref[b:b + 1, :])
        parts.append((own_ref[b] + a_ref[b] + (b_ref[b] + c_ref[b])) * inv)
    image = jnp.concatenate(parts, axis=1)
    image_ref[...] = image
    gram_ref[...] = lax.dot_general(
        image, image, NT, precision=lax.Precision.HIGHEST, preferred_element_type=jnp.float32
    )


def finish(degree, own, a, b, c):
    return pl.pallas_call(
        finish_kernel,
        out_shape=(
            jax.ShapeDtypeStruct((COLS, DOCS), jnp.float32),
            jax.ShapeDtypeStruct((COLS, COLS), jnp.float32),
        ),
        compiler_params=pltpu.CompilerParams(vmem_limit_bytes=VMEM_LIMIT),
        name="finish",
    )(degree, own, a, b, c)


def shift_z(k):
    return [(y * SIDE + z, y * SIDE + (z + k) % SIDE) for y in range(SIDE) for z in range(SIDE)]


def shift_y(k):
    return [(y * SIDE + z, (y + k) % SIDE * SIDE + z) for y in range(SIDE) for z in range(SIDE)]


def per_device(embedding, subspace, degree, neighbours, counts):
    position = lax.axis_index("blk")
    y, z = position // SIDE, position % SIDE
    row_ids = jnp.stack([(y * SIDE + (z + k) % SIDE) * OWN + UNIT * h + i for k, h in ARRIVAL for i in range(UNIT)])
    col_ids = jnp.stack([((y + k) % SIDE * SIDE + z) * OWN + UNIT * h + i for k, h in ARRIVAL for i in range(UNIT)])
    index = jnp.stack([row_ids, col_ids]).astype(jnp.int32)

    z_a, z_b, y_a, y_b = prepare(embedding, subspace, degree, neighbours, counts)

    def gather(a, b, shift):
        minus_a = lax.ppermute(a, "blk", shift(1))
        plus_b = lax.ppermute(b, "blk", shift(-1))
        b_next, minus_a = lax.optimization_barrier((b, minus_a))
        a_next, plus_b = lax.optimization_barrier((a, plus_b))
        minus_b = lax.ppermute(b_next, "blk", shift(1))
        plus_a = lax.ppermute(a_next, "blk", shift(-1))
        minus_next, minus_b = lax.optimization_barrier((minus_a, minus_b))
        plus_next, plus_a = lax.optimization_barrier((plus_b, plus_a))
        far_a = lax.ppermute(minus_next, "blk", shift(1))
        far_b = lax.ppermute(plus_next, "blk", shift(-1))
        return a, b, minus_a, plus_b, minus_b, plus_a, far_a, far_b

    z_parts = gather(z_a, z_b, shift_z)
    y_parts = gather(y_a, y_b, shift_y)
    acc = stage(0, 4, index, z_parts, y_parts)
    acc = stage(4, 6, index, z_parts, y_parts, acc)
    own, to_minus, to_plus, to_far = stage(6, 8, index, z_parts, y_parts, acc)
    back_a = lax.ppermute(to_minus, "blk", shift_z(-1))
    back_b = lax.ppermute(to_plus, "blk", shift_z(1))
    back_c = lax.ppermute(to_far, "blk", shift_z(2))
    image, gram = finish(degree, own, back_a, back_b, back_c)

    devices_blk = lax.axis_size("blk")
    devices_dp = lax.axis_size("dp")
    step = 1
    while step < devices_blk:
        gram = gram + lax.ppermute(gram, "blk", [(i, i ^ step) for i in range(devices_blk)])
        step *= 2
    step = 1
    while step < devices_dp:
        gram = gram + lax.ppermute(gram, "dp", [(i, i ^ step) for i in range(devices_dp)])
        step *= 2
    gram = gram / (DOCS * devices_blk * devices_dp)
    lower = jnp.linalg.cholesky(gram)
    solved = jax.scipy.linalg.solve_triangular(lower, image, lower=True)
    return solved.T.reshape(OWN, ROWS, COLS)


def solution(mesh):
    placed = (
        P(("dp", "blk"), None, None),
        P(("dp", "blk"), None, None),
        P(("dp", "blk"), None),
        P(("dp", "blk"), None),
        P(("dp", "blk")),
    )
    return jax.shard_map(
        per_device,
        mesh=mesh,
        in_specs=placed,
        out_specs=P(("dp", "blk"), None, None),
        check_vma=False,
    )
```

time: 1340 us -> 172 us (0.13); the launches traced: 1320 us -> 172 us
  waiting for transfers between devices: 828 us -> 73.2 us
  loops' own time: 157 us -> 0 us
  local copies, waits for them, and re-layouts: 133 us -> 1.94 us
  matrix products: 84.9 us -> 1.12 us
  blocking collectives: 64.8 us -> 0 us
  starting transfers between devices: 0.08 us -> 41.3 us
  Pallas kernels: 0 us -> 41.2 us
  other arithmetic: 44.4 us -> 12.7 us
    reduce_scatter x1 -> x0, waiting for transfers between devices: 588 us -> none  [per_device(): mine = lax.psum_scatter(running, 'blk', scatter_dimension=0, tiled=True)]
    all_gather x2 -> x0, waiting for transfers between devices: 240 us -> none  [the longest x1 194 us: per_device(): piece_x = lax.all_gather(embedding, 'blk', axis=0, tiled=True)]
    another operation x66 -> x0, loops' own time: 157 us -> none  [the longest x1 123 us: per_device(): running = lax.fori_loop(0, own_blocks * slot_total, own_slot, running)]
    dynamic_slice x145 -> x0, local copies, waits for them, and re-layouts: 123 us -> none  [the longest x64 84.5 us: own_slot(): target = neighbours[source, slot_id]]
    dot_general x44 -> x0, matrix products: 82.8 us -> none  [the longest x13 30.8 us: compute(): forward = jnp.dot(tile, piece_u[local], preferred_element_type=jnp.float32)]
    ppermute x0 -> x22, waiting for transfers between devices: none -> 73.2 us  [the longest x2 21.2 us: gather(): minus_a = lax.ppermute(a, 'blk', shift(1))]
    psum x1 -> x0, blocking collectives: 64.8 us -> none  [per_device(): lax.psum(local_gram, ('dp', 'blk'))]
    ppermute x0 -> x22, starting transfers between devices: none -> 41.3 us  [the longest x3 9.69 us: per_device(): lax.ppermute(gram, 'dp', [(i, i ^ step) for i in range(devices_dp)])]
  transfers between devices with their start and end apart: 3 -> 22, of which waited for: 3 -> 12; matrix products, arithmetic and copies ran while one was open for 1% -> 0% of each run, Pallas kernels for 0% -> 12%
where the time goes in v2:
time: 172 us
  waiting for transfers between devices  73.2 us (43%)
  starting transfers between devices  41.3 us (24%)
  Pallas kernels  41.2 us (24%)
  other arithmetic  12.7 us (7%)
  local copies, waits for them, and re-layouts  1.94 us (1%)
    pallas_call x3, Pallas kernels, stage(): pl.pallas_call(functools.partial(stage_kernel, old, new, last), out_shape...  34.4 us
    ppermute x2, waiting for transfers between devices, gather(): minus_a = lax.ppermute(a, 'blk', shift(1))  21.2 us
    ppermute x2, waiting for transfers between devices, gather(): minus_b = lax.ppermute(b_next, 'blk', shift(1))  20.3 us
    ppermute x4, waiting for transfers between devices, per_device(): lax.ppermute(gram, 'blk', [(i, i ^ step) for i in range(devices_blk)])  16.5 us
    ppermute x3, starting transfers between devices, per_device(): lax.ppermute(gram, 'dp', [(i, i ^ step) for i in range(devices_dp)])  9.69 us
    another operation x3, other arithmetic, per_device(): lower = jnp.linalg.cholesky(gram)  6.52 us
    ppermute x1, starting transfers between devices, per_device(): back_a = lax.ppermute(to_minus, 'blk', shift_z(-1))  5.83 us
    another operation x2, other arithmetic, per_device(): solved = jax.scipy.linalg.solve_triangular(lower, image, lower=True)  5.55 us
  transfers between devices with their start and end apart: 22, of which 12 were waited for; matrix products, arithmetic and copies ran while one was open for 0% of the time, Pallas kernels for 12%

profile of v2, /device:TPU:0, one launch (start us, length us, event | category | flops | bytes accessed | tf_op | source)
XLA Modules:
  0.0 171.6 jit_solution(6445105849548510056)
XLA Ops:
  0.0 4.6 %prepare.1 = (bf16[528,1024]{1,0:T(8,128)(2,1)}, bf16[528,1024]{1,0:T(8,128)(2,1)}, bf16[560,1024]{1,0:T(8,128)(2,1)}, bf16[560,1024]{1,0:T(8,128)(2,1)}) custom-call(s32[4,16]{1,0:T(4,128)} %nbr_hbm.1, s32[4]{0:T(128)} %cnt_hbm.1, bf16[1024,1024]{1,0:T(8,128)(2,1)} %bitcast.52, f32[4,64,256]{2,1,0:T(8,128)} %bitcast.53, f32[4,256]{1,0:T(4,128)} %deg_ref.1), custom_call_target="tpu_custom_call" | custom-call | tf_op jit(solution)/shard_map/prepare/pallas_call | solution.py:108
  4.6 1.7 %collective-permute-start.6 = (bf16[560,1024]{1,0:T(8,128)(2,1)}, bf16[560,1024]{1,0:T(8,128)(2,1)S(1)}, u32[]{:S(2)}, u32[]{:S(2)}) collective-permute-start(bf16[560,1024]{1,0:T(8,128)(2,1)} %get-tuple-element.47.refs_5_.refs_7_.refs_9_), channel_id=1, source_target_pairs={{0,4},{1,5},{2,6},{3,7},{4,8},{5,9},{6,10},{7,11},{8,12},{9,13},{1... | collective-permute-start | bytes 3440648 | tf_op jit(solution)/shard_map/ppermute | solution.py:351
  6.4 1.6 collective-permute-start.7
  7.9 2.0 %collective-permute-start = (bf16[528,1024]{1,0:T(8,128)(2,1)}, bf16[528,1024]{1,0:T(8,128)(2,1)}, u32[]{:S(2)}, u32[]{:S(2)}) collective-permute-start(bf16[528,1024]{1,0:T(8,128)(2,1)} %get-tuple-element.37.refs_1_), channel_id=1, source_target_pairs={{0,1},{1,2},{2,3},{3,0},{4,5},{5,6},{6,7},{7,4},{8,9},{9,10},{10,1... | collective-permute-start | bytes 3244040 | tf_op jit(solution)/shard_map/ppermute | solution.py:351
  9.9 2.1 %collective-permute-start.1 = (bf16[528,1024]{1,0:T(8,128)(2,1)}, bf16[528,1024]{1,0:T(8,128)(2,1)}, u32[]{:S(2)}, u32[]{:S(2)}) collective-permute-start(bf16[528,1024]{1,0:T(8,128)(2,1)} %get-tuple-element.35.refs_2_), channel_id=1, source_target_pairs={{0,3},{1,0},{2,1},{3,2},{4,7},{5,4},{6,5},{7,6},{8,11},{9,8},{10,9... | collective-permute-start | bytes 3244040 | tf_op jit(solution)/shard_map/ppermute | solution.py:352
  12.1 21.2 %collective-permute-done.6.refs_7_.refs_9_.refs_11_ = bf16[560,1024]{1,0:T(8,128)(2,1)S(1)} collective-permute-done((bf16[560,1024]{1,0:T(8,128)(2,1)}, bf16[560,1024]{1,0:T(8,128)(2,1)S(1)}, u32[]{:S(2)}, u32[]{:S(2)}) %collective-permute-start.6) | collective-permute-done | bytes 1146912 | tf_op jit(solution)/shard_map/ppermute | solution.py:351
  33.3 0.3 collective-permute-start.8
  33.6 0.0 collective-permute-done.7.refs_8_.refs_10_.refs_12_
  33.6 2.9 %collective-permute-start.9 = (bf16[560,1024]{1,0:T(8,128)(2,1)}, bf16[560,1024]{1,0:T(8,128)(2,1)}, u32[]{:S(2)}, u32[]{:S(2)}) collective-permute-start(bf16[560,1024]{1,0:T(8,128)(2,1)} %get-tuple-element.47.refs_5_.refs_7_.refs_9_), channel_id=1, source_target_pairs={{0,12},{1,13},{2,14},{3,15},{4,0},{5,1},{6,2},{7,3},{8,4},{9,5},{1... | collective-permute-start | bytes 3440648 | tf_op jit(solution)/shard_map/ppermute | solution.py:356
  36.5 0.0 collective-permute-done.refs_3_
  36.5 1.9 %collective-permute-start.2 = (bf16[528,1024]{1,0:T(8,128)(2,1)}, bf16[528,1024]{1,0:T(8,128)(2,1)}, u32[]{:S(2)}, u32[]{:S(2)}) collective-permute-start(bf16[528,1024]{1,0:T(8,128)(2,1)} %get-tuple-element.35.refs_2_), channel_id=1, source_target_pairs={{0,1},{1,2},{2,3},{3,0},{4,5},{5,6},{6,7},{7,4},{8,9},{9,10},{10,1... | collective-permute-start | bytes 3244040 | tf_op jit(solution)/shard_map/ppermute | solution.py:355
  38.4 0.0 collective-permute-done.1.refs_4_
  38.4 2.2 %collective-permute-start.3 = (bf16[528,1024]{1,0:T(8,128)(2,1)}, bf16[528,1024]{1,0:T(8,128)(2,1)}, u32[]{:S(2)}, u32[]{:S(2)}) collective-permute-start(bf16[528,1024]{1,0:T(8,128)(2,1)} %get-tuple-element.37.refs_1_), channel_id=1, source_target_pairs={{0,3},{1,0},{2,1},{3,2},{4,7},{5,4},{6,5},{7,6},{8,11},{9,8},{10,9... | collective-permute-start | bytes 3244040 | tf_op jit(solution)/shard_map/ppermute | solution.py:356
  40.6 0.1 stack.127
  40.7 0.1 stack.145
  40.8 20.3 %collective-permute-done.8.refs_11_.refs_13_ = bf16[560,1024]{1,0:T(8,128)(2,1)S(1)} collective-permute-done((bf16[560,1024]{1,0:T(8,128)(2,1)}, bf16[560,1024]{1,0:T(8,128)(2,1)S(1)}, u32[]{:S(2)}, u32[]{:S(2)}) %collective-permute-start.8) | collective-permute-done | bytes 1146912 | tf_op jit(solution)/shard_map/ppermute | solution.py:355
  61.1 0.0 collective-permute-start.10
  61.1 0.0 collective-permute-done.9.refs_12_.refs_14_
  61.1 3.2 %collective-permute-start.11 = (bf16[560,1024]{1,0:T(8,128)(2,1)}, bf16[560,1024]{1,0:T(8,128)(2,1)}, u32[]{:S(2)}, u32[]{:S(2)}) collective-permute-start(bf16[560,1024]{1,0:T(8,128)(2,1)} %collective-permute-done.7.refs_8_.refs_10_.refs_12_), channel_id=1, source_target_pairs={{0,12},{1,13},{2,14},{3,15},{4,0},{5,1},{6,2},{7,3},{8,4},{9,5},{1... | collective-permute-start | bytes 3440648 | tf_op jit(solution)/shard_map/ppermute | solution.py:360
  64.4 0.6 pad_add_fusion.refs_0_
  65.0 0.0 copy-done.5
  65.0 0.0 collective-permute-done.2.refs_5_
  65.0 1.7 %collective-permute-start.4 = (bf16[528,1024]{1,0:T(8,128)(2,1)}, bf16[528,1024]{1,0:T(8,128)(2,1)}, u32[]{:S(2)}, u32[]{:S(2)}) collective-permute-start(bf16[528,1024]{1,0:T(8,128)(2,1)} %collective-permute-done.refs_3_), channel_id=1, source_target_pairs={{0,1},{1,2},{2,3},{3,0},{4,5},{5,6},{6,7},{7,4},{8,9},{9,10},{10,1... | collective-permute-start | bytes 3244040 | tf_op jit(solution)/shard_map/ppermute | solution.py:359
  66.7 0.0 collective-permute-done.3.refs_6_
  66.7 2.3 %collective-permute-start.5 = (bf16[528,1024]{1,0:T(8,128)(2,1)}, bf16[528,1024]{1,0:T(8,128)(2,1)}, u32[]{:S(2)}, u32[]{:S(2)}) collective-permute-start(bf16[528,1024]{1,0:T(8,128)(2,1)} %collective-permute-done.1.refs_4_), channel_id=1, source_target_pairs={{0,3},{1,0},{2,1},{3,2},{4,7},{5,4},{6,5},{7,6},{8,11},{9,8},{10,9... | collective-permute-start | bytes 3244040 | tf_op jit(solution)/shard_map/ppermute | solution.py:360
  69.0 0.0 copy-done.4
  69.0 9.2 %stage_4.1.refs_13_ = f32[16,64,256]{2,1,0:T(8,128)} custom-call(s32[2,16]{1,0:T(2,128)} %pad_add_fusion.refs_0_, bf16[528,1024]{1,0:T(8,128)(2,1)} %get-tuple-element.37.refs_1_, bf16[528,1024]{1,0:T(8,128)(2,1)} %get-tuple-element.35.refs_2_, bf16[528,1024]{1,0:T(8,128)(2,1)} %collective-permute-done.refs_3_, ...), custom_call_target="tpu_custom_call" | custom-call | flops 6000000000 | bytes 16777216 | tf_op jit(solution)/shard_map/stage_4/pallas_call | solution.py:275
  78.2 11.7 %stage_6.1.refs_17_ = f32[16,64,256]{2,1,0:T(8,128)} custom-call(s32[2,16]{1,0:T(2,128)} %pad_add_fusion.refs_0_, bf16[528,1024]{1,0:T(8,128)(2,1)} %get-tuple-element.37.refs_1_, bf16[528,1024]{1,0:T(8,128)(2,1)} %get-tuple-element.35.refs_2_, bf16[528,1024]{1,0:T(8,128)(2,1)} %collective-permute-done.refs_3_, ...), custom_call_target="tpu_custom_call" | custom-call | flops 6000000000 | bytes 16777216 | tf_op jit(solution)/shard_map/stage_6/pallas_call | solution.py:275
  89.9 1.1 collective-permute-done.4.refs_7_
  91.0 0.0 collective-permute-done.5.refs_8_
  91.0 0.0 collective-permute-done.10.refs_15_
  91.0 0.0 collective-permute-done.11.refs_16_
  91.0 13.5 %stage_8.1 = (f32[4,64,256]{2,1,0:T(8,128)}, f32[4,64,256]{2,1,0:T(8,128)}, f32[4,64,256]{2,1,0:T(8,128)}, f32[4,64,256]{2,1,0:T(8,128)}) custom-call(s32[2,16]{1,0:T(2,128)} %pad_add_fusion.refs_0_, bf16[528,1024]{1,0:T(8,128)(2,1)} %get-tuple-element.37.refs_1_, bf16[528,1024]{1,0:T(8,128)(2,1)} %get-tuple-element.35.refs_2_, ...), custom_call_target="tpu_custom_call" | custom-call | flops 6000000000 | bytes 16777216 | tf_op jit(solution)/shard_map/stage_8/pallas_call | solution.py:275
  104.5 5.8 %collective-permute-start.12 = (f32[4,64,256]{2,1,0:T(8,128)}, f32[4,64,256]{2,1,0:T(8,128)S(1)}, u32[]{:S(2)}, u32[]{:S(2)}) collective-permute-start(f32[4,64,256]{2,1,0:T(8,128)} %get-tuple-element.52), channel_id=1, source_target_pairs={{0,3},{1,0},{2,1},{3,2},{4,7},{5,4},{6,5},{7,6},{8,11},{9,8},{10,9... | collective-permute-start | bytes 786440 | tf_op jit(solution)/shard_map/ppermute | solution.py:368
  110.3 0.0 collective-permute-start.13
  110.4 1.5 collective-permute-start.14
  111.9 3.6 %collective-permute-done.12.a_ref = f32[4,64,256]{2,1,0:T(8,128)S(1)} collective-permute-done((f32[4,64,256]{2,1,0:T(8,128)}, f32[4,64,256]{2,1,0:T(8,128)S(1)}, u32[]{:S(2)}, u32[]{:S(2)}) %collective-permute-start.12) | collective-permute-done | bytes 262176 | tf_op jit(solution)/shard_map/ppermute | solution.py:368
  115.5 5.5 %collective-permute-done.13.b_ref = f32[4,64,256]{2,1,0:T(8,128)S(1)} collective-permute-done((f32[4,64,256]{2,1,0:T(8,128)}, f32[4,64,256]{2,1,0:T(8,128)S(1)}, u32[]{:S(2)}, u32[]{:S(2)}) %collective-permute-start.13) | collective-permute-done | bytes 262176 | tf_op jit(solution)/shard_map/ppermute | solution.py:369
  121.0 0.0 collective-permute-done.14.c_ref
  121.0 0.7 copy-done.2
  121.7 0.1 copy-done.3
  121.7 2.2 %finish.1 = (f32[64,1024]{1,0:T(8,128)}, f32[64,64]{1,0:T(8,128)}) custom-call(f32[4,256]{1,0:T(4,128)} %deg_ref.1, f32[4,64,256]{2,1,0:T(8,128)} %get-tuple-element.51.own_ref, f32[4,64,256]{2,1,0:T(8,128)} %copy-done.1, f32[4,64,256]{2,1,0:T(8,128)} %copy-done.2, f32[4,64,256]{2,1,0:T(8,128)} %copy-done.3), custom_call_target="tpu_custom_call" | custom-call | tf_op jit(solution)/shard_map/finish/pallas_call | solution.py:322
  123.9 0.9 copy.7
  124.8 0.1 collective-permute-start.15
  124.9 3.9 %collective-permute-done.15 = f32[64,64]{0,1:T(8,128)S(1)} collective-permute-done((f32[64,64]{0,1:T(8,128)S(1)}, f32[64,64]{0,1:T(8,128)S(1)}, u32[]{:S(2)}, u32[]{:S(2)}) %collective-permute-start.15) | collective-permute-done | bytes 16416 | tf_op jit(solution)/shard_map/ppermute | solution.py:377
  128.8 0.2 collective-permute-start.16
  129.0 5.2 %collective-permute-done.16 = f32[64,64]{0,1:T(8,128)S(1)} collective-permute-done((f32[64,64]{0,1:T(8,128)S(1)}, f32[64,64]{0,1:T(8,128)S(1)}, u32[]{:S(2)}, u32[]{:S(2)}) %collective-permute-start.16) | collective-permute-done | bytes 16416 | tf_op jit(solution)/shard_map/ppermute | solution.py:377
  134.2 0.0 collective-permute-start.17
  134.2 3.9 %collective-permute-done.17 = f32[64,64]{0,1:T(8,128)S(1)} collective-permute-done((f32[64,64]{0,1:T(8,128)S(1)}, f32[64,64]{0,1:T(8,128)S(1)}, u32[]{:S(2)}, u32[]{:S(2)}) %collective-permute-start.17) | collective-permute-done | bytes 16416 | tf_op jit(solution)/shard_map/ppermute | solution.py:377
  138.1 1.9 %collective-permute-start.18 = (f32[64,64]{0,1:T(8,128)S(1)}, f32[64,64]{0,1:T(8,128)S(1)}, u32[]{:S(2)}, u32[]{:S(2)}) collective-permute-start(f32[64,64]{0,1:T(8,128)S(1)} %add.315), channel_id=1, source_target_pairs={{0,8},{1,9},{2,10},{3,11},{4,12},{5,13},{6,14},{7,15},{8,0},{9,1},... | collective-permute-start | bytes 49160 | tf_op jit(solution)/shard_map/ppermute | solution.py:377
  140.0 3.5 %collective-permute-done.18 = f32[64,64]{0,1:T(8,128)S(1)} collective-permute-done((f32[64,64]{0,1:T(8,128)S(1)}, f32[64,64]{0,1:T(8,128)S(1)}, u32[]{:S(2)}, u32[]{:S(2)}) %collective-permute-start.18) | collective-permute-done | bytes 16416 | tf_op jit(solution)/shard_map/ppermute | solution.py:377
  143.6 0.0 collective-permute-start.19
  143.6 1.2 collective-permute-done.19
  144.8 3.7 %collective-permute-start.20 = (f32[64,64]{0,1:T(8,128)S(1)}, f32[64,64]{0,1:T(8,128)S(1)}, u32[]{:S(2)}, u32[]{:S(2)}) collective-permute-start(f32[64,64]{0,1:T(8,128)S(1)} %add.317), channel_id=1, source_target_pairs={{0,32},{16,48},{32,0},{48,16},{64,96},{80,112},{96,64},{112,80},{1... | collective-permute-start | bytes 49160 | tf_op jit(solution)/shard_map/ppermute | solution.py:381
  148.5 1.9 %collective-permute-done.20 = f32[64,64]{0,1:T(8,128)S(1)} collective-permute-done((f32[64,64]{0,1:T(8,128)S(1)}, f32[64,64]{0,1:T(8,128)S(1)}, u32[]{:S(2)}, u32[]{:S(2)}) %collective-permute-start.20) | collective-permute-done | bytes 16416 | tf_op jit(solution)/shard_map/ppermute | solution.py:381
  150.4 6.0 %collective-permute-start.21 = (f32[64,64]{0,1:T(8,128)S(1)}, f32[64,64]{0,1:T(8,128)S(1)}, u32[]{:S(2)}, u32[]{:S(2)}) collective-permute-start(f32[64,64]{0,1:T(8,128)S(1)} %add.318), channel_id=1, source_target_pairs={{0,64},{16,80},{32,96},{48,112},{64,0},{80,16},{96,32},{112,48},{1... | collective-permute-start | bytes 49160 | tf_op jit(solution)/shard_map/ppermute | solution.py:381
  156.4 1.9 %collective-permute-done.21 = f32[64,64]{0,1:T(8,128)S(1)} collective-permute-done((f32[64,64]{0,1:T(8,128)S(1)}, f32[64,64]{0,1:T(8,128)S(1)}, u32[]{:S(2)}, u32[]{:S(2)}) %collective-permute-start.21) | collective-permute-done | bytes 16416 | tf_op jit(solution)/shard_map/ppermute | solution.py:381
  158.3 0.1 copy.8
  158.4 5.8 %cholesky.16 = f32[64,64]{1,0:T(8,128)S(1)} custom-call(f32[64,64]{1,0:T(8,128)S(1)} %fusion.5), custom_call_target="Cholesky" | custom-call | tf_op jit(solution)/shard_map/jit(cholesky)/cholesky | solution.py:384
  164.2 0.6 compare_reduce_fusion
  164.9 0.7 fusion.3
  165.5 4.9 %custom-call.7 = f32[1,64,64]{1,2,0:T(8,128)S(1)} custom-call(f32[1,64,64]{2,1,0:T(8,128)S(1)} %fusion.3), custom_call_target="InvertDiagBlocksLowerTriangular" | custom-call | tf_op jit(solution)/shard_map/jit(_solve_triangular)/triangular_solve | solution.py:385
  170.4 0.0 copy-done
  170.5 1.1 fusion
  (16 shorter events, 0.1 us)
Async XLA Ops:
  4.6 28.6 %collective-permute-start.6 = (bf16[560,1024]{1,0:T(8,128)(2,1)}, bf16[560,1024]{1,0:T(8,128)(2,1)S(1)}, u32[]{:S(2)}, u32[]{:S(2)}) collective-permute-start(bf16[560,1024]{1,0:T(8,128)(2,1)} %get-tuple-element.47.refs_5_.refs_7_.refs_9_), channel_id=1, source_target_pairs={{0,4},{1,5},{2,6},{3,7},{4,8},{5,9},{6,10},{7,11},{8,12},{9,13},{1... | collective-permute-start | bytes 3440648 | tf_op jit(solution)/shard_map/ppermute | solution.py:351
  6.4 27.2 %collective-permute-start.7 = (bf16[560,1024]{1,0:T(8,128)(2,1)}, bf16[560,1024]{1,0:T(8,128)(2,1)}, u32[]{:S(2)}, u32[]{:S(2)}) collective-permute-start(bf16[560,1024]{1,0:T(8,128)(2,1)} %get-tuple-element.45.refs_6_.refs_8_.refs_10_), channel_id=1, source_target_pairs={{0,12},{1,13},{2,14},{3,15},{4,0},{5,1},{6,2},{7,3},{8,4},{9,5},{1... | collective-permute-start | bytes 3440648 | tf_op jit(solution)/shard_map/ppermute | solution.py:352
  7.9 28.6 %collective-permute-start = (bf16[528,1024]{1,0:T(8,128)(2,1)}, bf16[528,1024]{1,0:T(8,128)(2,1)}, u32[]{:S(2)}, u32[]{:S(2)}) collective-permute-start(bf16[528,1024]{1,0:T(8,128)(2,1)} %get-tuple-element.37.refs_1_), channel_id=1, source_target_pairs={{0,1},{1,2},{2,3},{3,0},{4,5},{5,6},{6,7},{7,4},{8,9},{9,10},{10,1... | collective-permute-start | bytes 3244040 | tf_op jit(solution)/shard_map/ppermute | solution.py:351
  9.9 28.5 %collective-permute-start.1 = (bf16[528,1024]{1,0:T(8,128)(2,1)}, bf16[528,1024]{1,0:T(8,128)(2,1)}, u32[]{:S(2)}, u32[]{:S(2)}) collective-permute-start(bf16[528,1024]{1,0:T(8,128)(2,1)} %get-tuple-element.35.refs_2_), channel_id=1, source_target_pairs={{0,3},{1,0},{2,1},{3,2},{4,7},{5,4},{6,5},{7,6},{8,11},{9,8},{10,9... | collective-permute-start | bytes 3244040 | tf_op jit(solution)/shard_map/ppermute | solution.py:352
  33.3 35.7 %copy-start.4 = (bf16[560,1024]{1,0:T(8,128)(2,1)}, bf16[560,1024]{1,0:T(8,128)(2,1)S(1)}, u32[]{:S(2)}) copy-start(bf16[560,1024]{1,0:T(8,128)(2,1)S(1)} %collective-permute-done.6.refs_7_.refs_9_.refs_11_) | copy-start | bytes 3440644
  33.3 27.8 %collective-permute-start.8 = (bf16[560,1024]{1,0:T(8,128)(2,1)}, bf16[560,1024]{1,0:T(8,128)(2,1)S(1)}, u32[]{:S(2)}, u32[]{:S(2)}) collective-permute-start(bf16[560,1024]{1,0:T(8,128)(2,1)} %get-tuple-element.45.refs_6_.refs_8_.refs_10_), channel_id=1, source_target_pairs={{0,4},{1,5},{2,6},{3,7},{4,8},{5,9},{6,10},{7,11},{8,12},{9,13},{1... | collective-permute-start | bytes 3440648 | tf_op jit(solution)/shard_map/ppermute | solution.py:355
  33.6 27.5 %collective-permute-start.9 = (bf16[560,1024]{1,0:T(8,128)(2,1)}, bf16[560,1024]{1,0:T(8,128)(2,1)}, u32[]{:S(2)}, u32[]{:S(2)}) collective-permute-start(bf16[560,1024]{1,0:T(8,128)(2,1)} %get-tuple-element.47.refs_5_.refs_7_.refs_9_), channel_id=1, source_target_pairs={{0,12},{1,13},{2,14},{3,15},{4,0},{5,1},{6,2},{7,3},{8,4},{9,5},{1... | collective-permute-start | bytes 3440648 | tf_op jit(solution)/shard_map/ppermute | solution.py:356
  36.5 28.4 %collective-permute-start.2 = (bf16[528,1024]{1,0:T(8,128)(2,1)}, bf16[528,1024]{1,0:T(8,128)(2,1)}, u32[]{:S(2)}, u32[]{:S(2)}) collective-permute-start(bf16[528,1024]{1,0:T(8,128)(2,1)} %get-tuple-element.35.refs_2_), channel_id=1, source_target_pairs={{0,1},{1,2},{2,3},{3,0},{4,5},{5,6},{6,7},{7,4},{8,9},{9,10},{10,1... | collective-permute-start | bytes 3244040 | tf_op jit(solution)/shard_map/ppermute | solution.py:355
  38.4 28.2 %collective-permute-start.3 = (bf16[528,1024]{1,0:T(8,128)(2,1)}, bf16[528,1024]{1,0:T(8,128)(2,1)}, u32[]{:S(2)}, u32[]{:S(2)}) collective-permute-start(bf16[528,1024]{1,0:T(8,128)(2,1)} %get-tuple-element.37.refs_1_), channel_id=1, source_target_pairs={{0,3},{1,0},{2,1},{3,2},{4,7},{5,4},{6,5},{7,6},{8,11},{9,8},{10,9... | collective-permute-start | bytes 3244040 | tf_op jit(solution)/shard_map/ppermute | solution.py:356
  61.1 3.8 %copy-start.5 = (bf16[560,1024]{1,0:T(8,128)(2,1)}, bf16[560,1024]{1,0:T(8,128)(2,1)S(1)}, u32[]{:S(2)}) copy-start(bf16[560,1024]{1,0:T(8,128)(2,1)S(1)} %collective-permute-done.8.refs_11_.refs_13_) | copy-start | bytes 3440644
  61.1 29.9 %collective-permute-start.10 = (bf16[560,1024]{1,0:T(8,128)(2,1)S(1)}, bf16[560,1024]{1,0:T(8,128)(2,1)}, u32[]{:S(2)}, u32[]{:S(2)}) collective-permute-start(bf16[560,1024]{1,0:T(8,128)(2,1)S(1)} %collective-permute-done.6.refs_7_.refs_9_.refs_11_), channel_id=1, source_target_pairs={{0,4},{1,5},{2,6},{3,7},{4,8},{5,9},{6,10},{7,11},{8,12},{9,13},{1... | collective-permute-start | bytes 3440648 | tf_op jit(solution)/shard_map/ppermute | solution.py:359
  61.1 29.9 %collective-permute-start.11 = (bf16[560,1024]{1,0:T(8,128)(2,1)}, bf16[560,1024]{1,0:T(8,128)(2,1)}, u32[]{:S(2)}, u32[]{:S(2)}) collective-permute-start(bf16[560,1024]{1,0:T(8,128)(2,1)} %collective-permute-done.7.refs_8_.refs_10_.refs_12_), channel_id=1, source_target_pairs={{0,12},{1,13},{2,14},{3,15},{4,0},{5,1},{6,2},{7,3},{8,4},{9,5},{1... | collective-permute-start | bytes 3440648 | tf_op jit(solution)/shard_map/ppermute | solution.py:360
  65.0 26.0 %collective-permute-start.4 = (bf16[528,1024]{1,0:T(8,128)(2,1)}, bf16[528,1024]{1,0:T(8,128)(2,1)}, u32[]{:S(2)}, u32[]{:S(2)}) collective-permute-start(bf16[528,1024]{1,0:T(8,128)(2,1)} %collective-permute-done.refs_3_), channel_id=1, source_target_pairs={{0,1},{1,2},{2,3},{3,0},{4,5},{5,6},{6,7},{7,4},{8,9},{9,10},{10,1... | collective-permute-start | bytes 3244040 | tf_op jit(solution)/shard_map/ppermute | solution.py:359
  66.7 24.3 %collective-permute-start.5 = (bf16[528,1024]{1,0:T(8,128)(2,1)}, bf16[528,1024]{1,0:T(8,128)(2,1)}, u32[]{:S(2)}, u32[]{:S(2)}) collective-permute-start(bf16[528,1024]{1,0:T(8,128)(2,1)} %collective-permute-done.1.refs_4_), channel_id=1, source_target_pairs={{0,3},{1,0},{2,1},{3,2},{4,7},{5,4},{6,5},{7,6},{8,11},{9,8},{10,9... | collective-permute-start | bytes 3244040 | tf_op jit(solution)/shard_map/ppermute | solution.py:360
  104.5 11.0 %collective-permute-start.12 = (f32[4,64,256]{2,1,0:T(8,128)}, f32[4,64,256]{2,1,0:T(8,128)S(1)}, u32[]{:S(2)}, u32[]{:S(2)}) collective-permute-start(f32[4,64,256]{2,1,0:T(8,128)} %get-tuple-element.52), channel_id=1, source_target_pairs={{0,3},{1,0},{2,1},{3,2},{4,7},{5,4},{6,5},{7,6},{8,11},{9,8},{10,9... | collective-permute-start | bytes 786440 | tf_op jit(solution)/shard_map/ppermute | solution.py:368
  110.3 10.6 %collective-permute-start.13 = (f32[4,64,256]{2,1,0:T(8,128)}, f32[4,64,256]{2,1,0:T(8,128)S(1)}, u32[]{:S(2)}, u32[]{:S(2)}) collective-permute-start(f32[4,64,256]{2,1,0:T(8,128)} %get-tuple-element.53), channel_id=1, source_target_pairs={{0,1},{1,2},{2,3},{3,0},{4,5},{5,6},{6,7},{7,4},{8,9},{9,10},{10,1... | collective-permute-start | bytes 786440 | tf_op jit(solution)/shard_map/ppermute | solution.py:369
  110.4 10.6 %collective-permute-start.14 = (f32[4,64,256]{2,1,0:T(8,128)}, f32[4,64,256]{2,1,0:T(8,128)S(1)}, u32[]{:S(2)}, u32[]{:S(2)}) collective-permute-start(f32[4,64,256]{2,1,0:T(8,128)} %get-tuple-element.54), channel_id=1, source_target_pairs={{0,2},{1,3},{2,0},{3,1},{4,6},{5,7},{6,4},{7,5},{8,10},{9,11},{10,... | collective-permute-start | bytes 786440 | tf_op jit(solution)/shard_map/ppermute | solution.py:370
  115.5 5.5 %copy-start.1 = (f32[4,64,256]{2,1,0:T(8,128)}, f32[4,64,256]{2,1,0:T(8,128)S(1)}, u32[]{:S(2)}) copy-start(f32[4,64,256]{2,1,0:T(8,128)S(1)} %collective-permute-done.12.a_ref) | copy-start | bytes 786436
  121.0 0.7 copy-start.2
  121.0 0.8 copy-start.3
  123.9 46.5 %copy-start = (f32[64,1024]{1,0:T(8,128)S(1)}, f32[64,1024]{1,0:T(8,128)}, u32[]{:S(2)}) copy-start(f32[64,1024]{1,0:T(8,128)} %get-tuple-element.55) | copy-start | bytes 786436
  124.8 4.0 %collective-permute-start.15 = (f32[64,64]{0,1:T(8,128)S(1)}, f32[64,64]{0,1:T(8,128)S(1)}, u32[]{:S(2)}, u32[]{:S(2)}) collective-permute-start(f32[64,64]{0,1:T(8,128)S(1)} %copy.7), channel_id=1, source_target_pairs={{0,1},{1,0},{2,3},{3,2},{4,5},{5,4},{6,7},{7,6},{8,9},{9,8},{10,11... | collective-permute-start | bytes 49160 | tf_op jit(solution)/shard_map/ppermute | solution.py:377
  128.8 5.4 %collective-permute-start.16 = (f32[64,64]{0,1:T(8,128)S(1)}, f32[64,64]{0,1:T(8,128)S(1)}, u32[]{:S(2)}, u32[]{:S(2)}) collective-permute-start(f32[64,64]{0,1:T(8,128)S(1)} %add.313), channel_id=1, source_target_pairs={{0,2},{1,3},{2,0},{3,1},{4,6},{5,7},{6,4},{7,5},{8,10},{9,11},{10,... | collective-permute-start | bytes 49160 | tf_op jit(solution)/shard_map/ppermute | solution.py:377
  134.2 3.9 %collective-permute-start.17 = (f32[64,64]{0,1:T(8,128)S(1)}, f32[64,64]{0,1:T(8,128)S(1)}, u32[]{:S(2)}, u32[]{:S(2)}) collective-permute-start(f32[64,64]{0,1:T(8,128)S(1)} %add.314), channel_id=1, source_target_pairs={{0,4},{1,5},{2,6},{3,7},{4,0},{5,1},{6,2},{7,3},{8,12},{9,13},{10,... | collective-permute-start | bytes 49160 | tf_op jit(solution)/shard_map/ppermute | solution.py:377
  138.1 5.4 %collective-permute-start.18 = (f32[64,64]{0,1:T(8,128)S(1)}, f32[64,64]{0,1:T(8,128)S(1)}, u32[]{:S(2)}, u32[]{:S(2)}) collective-permute-start(f32[64,64]{0,1:T(8,128)S(1)} %add.315), channel_id=1, source_target_pairs={{0,8},{1,9},{2,10},{3,11},{4,12},{5,13},{6,14},{7,15},{8,0},{9,1},... | collective-permute-start | bytes 49160 | tf_op jit(solution)/shard_map/ppermute | solution.py:377
  143.6 1.2 collective-permute-start.19
  144.8 5.6 %collective-permute-start.20 = (f32[64,64]{0,1:T(8,128)S(1)}, f32[64,64]{0,1:T(8,128)S(1)}, u32[]{:S(2)}, u32[]{:S(2)}) collective-permute-start(f32[64,64]{0,1:T(8,128)S(1)} %add.317), channel_id=1, source_target_pairs={{0,32},{16,48},{32,0},{48,16},{64,96},{80,112},{96,64},{112,80},{1... | collective-permute-start | bytes 49160 | tf_op jit(solution)/shard_map/ppermute | solution.py:381
  150.4 7.9 %collective-permute-start.21 = (f32[64,64]{0,1:T(8,128)S(1)}, f32[64,64]{0,1:T(8,128)S(1)}, u32[]{:S(2)}, u32[]{:S(2)}) collective-permute-start(f32[64,64]{0,1:T(8,128)S(1)} %add.318), channel_id=1, source_target_pairs={{0,64},{16,80},{32,96},{48,112},{64,0},{80,16},{96,32},{112,48},{1... | collective-permute-start | bytes 49160 | tf_op jit(solution)/shard_map/ppermute | solution.py:381

commit v3 on v2

--- a/solution.py
+++ b/solution.py
@@ -24,6 +24,8 @@
 Y_ROWS = Y_X + HALF
 GROUPED = 4
 VMEM_LIMIT = 62 * 2**20
+SMALL_LIMIT = 16 * 2**20
+PANEL = 8
 ARRIVAL = ((0, 0), (0, 1), (-1, 0), (1, 1), (-1, 1), (1, 0), (2, 0), (2, 1))
 LOG2E = 1.4426950408889634
 GAIN = 2.0 * LOG2E / (4.0 * math.sqrt(FEAT))
@@ -330,6 +332,39 @@
     )(degree, own, a, b, c)
 
 
+def solve_kernel(documents, gram_ref, other_ref, image_ref, out_ref):
+    gram = (gram_ref[...] + other_ref[...]) / documents
+    row_id = lax.broadcasted_iota(jnp.int32, (COLS, 2 * COLS), 0)
+    lane_id = lax.broadcasted_iota(jnp.int32, (COLS, 2 * COLS), 1)
+    unit = (row_id[:, :COLS] == lane_id[:, :COLS]).astype(jnp.float32)
+    work = jnp.concatenate([gram, unit], axis=1)
+    for start in range(0, COLS, PANEL):
+        columns = [jnp.broadcast_to(work[:, start + j:start + j + 1], work.shape) for j in range(PANEL)]
+        for j in range(PANEL):
+            k = start + j
+            factor = columns[j] * (1.0 / columns[j][k:k + 1, :])
+            factor = jnp.where(row_id > k, factor, 0.0)
+            for i in range(j + 1, PANEL):
+                columns[i] = columns[i] - factor * columns[j][start + i:start + i + 1, :]
+            work = work - factor * work[k:k + 1, :]
+    pivots = jnp.sum(jnp.where(row_id == lane_id, work, 0.0), axis=1, keepdims=True)
+    inverse = work[:, COLS:] / jnp.sqrt(pivots)
+    for b in range(OWN):
+        out_ref[b] = lax.dot_general(
+            inverse, image_ref[:, b * ROWS:(b + 1) * ROWS], NN,
+            precision=lax.Precision.HIGHEST, preferred_element_type=jnp.float32,
+        )
+
+
+def solve(documents, gram, other, image):
+    return pl.pallas_call(
+        functools.partial(solve_kernel, float(documents)),
+        out_shape=jax.ShapeDtypeStruct((OWN, COLS, ROWS), jnp.float32),
+        compiler_params=pltpu.CompilerParams(vmem_limit_bytes=SMALL_LIMIT),
+        name="solve",
+    )(gram, other, image)
+
+
 def shift_z(k):
     return [(y * SIDE + z, y * SIDE + (z + k) % SIDE) for y in range(SIDE) for z in range(SIDE)]
 
@@ -372,18 +407,15 @@
 
     devices_blk = lax.axis_size("blk")
     devices_dp = lax.axis_size("dp")
-    step = 1
-    while step < devices_blk:
-        gram = gram + lax.ppermute(gram, "blk", [(i, i ^ step) for i in range(devices_blk)])
-        step *= 2
-    step = 1
-    while step < devices_dp:
-        gram = gram + lax.ppermute(gram, "dp", [(i, i ^ step) for i in range(devices_dp)])
-        step *= 2
-    gram = gram / (DOCS * devices_blk * devices_dp)
-    lower = jnp.linalg.cholesky(gram)
-    solved = jax.scipy.linalg.solve_triangular(lower, image, lower=True)
-    return solved.T.reshape(OWN, ROWS, COLS)
+    other = lax.ppermute(gram, "dp", [(i, i ^ 1) for i in range(devices_dp)])
+    for axis, size, first in (("dp", devices_dp, 2), ("blk", devices_blk, 1)):
+        step = first
+        while step < size:
+            gram = gram + other
+            other = lax.ppermute(gram, axis, [(i, i ^ step) for i in range(size)])
+            step *= 2
+    solved = solve(DOCS * devices_blk * devices_dp, gram, other, image)
+    return jnp.swapaxes(solved, 1, 2)
 
 
 def solution(mesh):

time: 172 us -> 161 us (0.936)
  other arithmetic: 12.7 us -> 1.39 us
  Pallas kernels: 41.2 us -> 47 us
  starting transfers between devices: 41.3 us -> 38.6 us
  waiting for transfers between devices: 73.2 us -> 71.3 us
    another operation x5 -> x0, other arithmetic: 12.1 us -> none  [the longest x3 6.52 us: per_device(): lower = jnp.linalg.cholesky(gram)]
    ppermute x1, waiting for transfers between devices: 3.6 us -> 7.43 us  [per_device(): back_a = lax.ppermute(to_minus, 'blk', shift_z(-1))]
    ppermute x1, waiting for transfers between devices: 5.46 us -> 1.62 us  [per_device(): back_b = lax.ppermute(to_plus, 'blk', shift_z(1))]
    pallas_call x0 -> x1, Pallas kernels: none -> 2.99 us  [solve(): pl.pallas_call(functools.partial(solve_kernel, float(documents)), out_sha...]
    pallas_call x3, Pallas kernels: 34.4 us -> 37.2 us  [stage(): pl.pallas_call(functools.partial(stage_kernel, old, new, last), out_shape...]
    ppermute x7, starting transfers between devices: 11.9 us -> 10 us  [the longest x6 10 us: per_device(): other = lax.ppermute(gram, axis, [(i, i ^ step) for i in range(size)])]
  transfers between devices with their start and end apart: 22 -> 22, of which waited for: 12 -> 11; matrix products, arithmetic and copies ran while one was open for 0% -> 0% of each run, Pallas kernels for 12% -> 15%
where the time goes in v3:
time: 161 us; the launch traced here: 160 us
  waiting for transfers between devices  71.3 us (44%)
  Pallas kernels  47 us (29%)
  starting transfers between devices  38.6 us (24%)
  local copies, waits for them, and re-layouts  1.94 us (1%)
    pallas_call x3, Pallas kernels, stage(): pl.pallas_call(functools.partial(stage_kernel, old, new, last), out_shape...  37.2 us
    ppermute x2, waiting for transfers between devices, gather(): minus_a = lax.ppermute(a, 'blk', shift(1))  21.2 us
    ppermute x2, waiting for transfers between devices, gather(): minus_b = lax.ppermute(b_next, 'blk', shift(1))  20.3 us
    ppermute x6, waiting for transfers between devices, per_device(): other = lax.ppermute(gram, axis, [(i, i ^ step) for i in range(size)])  19.3 us
    ppermute x6, starting transfers between devices, per_device(): other = lax.ppermute(gram, axis, [(i, i ^ step) for i in range(size)])  10 us
    ppermute x1, waiting for transfers between devices, per_device(): back_a = lax.ppermute(to_minus, 'blk', shift_z(-1))  7.43 us
    ppermute x2, starting transfers between devices, gather(): far_b = lax.ppermute(plus_next, 'blk', shift(-1))  5.54 us
    ppermute x2, starting transfers between devices, gather(): plus_a = lax.ppermute(a_next, 'blk', shift(-1))  5.13 us
  transfers between devices with their start and end apart: 22, of which 11 were waited for; matrix products, arithmetic and copies ran while one was open for 0% of the time, Pallas kernels for 15%

profile of v3, /device:TPU:0, one launch (start us, length us, event | category | flops | bytes accessed | tf_op | source)
XLA Modules:
  0.0 160.4 jit_solution(8669868869349665935)
XLA Ops:
  0.0 4.6 %prepare.1 = (bf16[528,1024]{1,0:T(8,128)(2,1)}, bf16[528,1024]{1,0:T(8,128)(2,1)}, bf16[560,1024]{1,0:T(8,128)(2,1)}, bf16[560,1024]{1,0:T(8,128)(2,1)}) custom-call(s32[4,16]{1,0:T(4,128)} %nbr_hbm.1, s32[4]{0:T(128)} %cnt_hbm.1, bf16[1024,1024]{1,0:T(8,128)(2,1)} %bitcast.37, f32[4,64,256]{2,1,0:T(8,128)} %bitcast.38, f32[4,256]{1,0:T(4,128)} %deg_ref.1), custom_call_target="tpu_custom_call" | custom-call | tf_op jit(solution)/shard_map/prepare/pallas_call | solution.py:110
  4.7 1.7 %collective-permute-start.6 = (bf16[560,1024]{1,0:T(8,128)(2,1)}, bf16[560,1024]{1,0:T(8,128)(2,1)S(1)}, u32[]{:S(2)}, u32[]{:S(2)}) collective-permute-start(bf16[560,1024]{1,0:T(8,128)(2,1)} %get-tuple-element.47.refs_5_.refs_7_.refs_9_), channel_id=1, source_target_pairs={{0,4},{1,5},{2,6},{3,7},{4,8},{5,9},{6,10},{7,11},{8,12},{9,13},{1... | collective-permute-start | bytes 3440648 | tf_op jit(solution)/shard_map/ppermute | solution.py:386
  6.4 1.6 collective-permute-start.7
  8.0 2.0 %collective-permute-start = (bf16[528,1024]{1,0:T(8,128)(2,1)}, bf16[528,1024]{1,0:T(8,128)(2,1)}, u32[]{:S(2)}, u32[]{:S(2)}) collective-permute-start(bf16[528,1024]{1,0:T(8,128)(2,1)} %get-tuple-element.37.refs_1_), channel_id=1, source_target_pairs={{0,1},{1,2},{2,3},{3,0},{4,5},{5,6},{6,7},{7,4},{8,9},{9,10},{10,1... | collective-permute-start | bytes 3244040 | tf_op jit(solution)/shard_map/ppermute | solution.py:386
  10.0 2.1 %collective-permute-start.1 = (bf16[528,1024]{1,0:T(8,128)(2,1)}, bf16[528,1024]{1,0:T(8,128)(2,1)}, u32[]{:S(2)}, u32[]{:S(2)}) collective-permute-start(bf16[528,1024]{1,0:T(8,128)(2,1)} %get-tuple-element.35.refs_2_), channel_id=1, source_target_pairs={{0,3},{1,0},{2,1},{3,2},{4,7},{5,4},{6,5},{7,6},{8,11},{9,8},{10,9... | collective-permute-start | bytes 3244040 | tf_op jit(solution)/shard_map/ppermute | solution.py:387
  12.1 21.2 %collective-permute-done.6.refs_7_.refs_9_.refs_11_ = bf16[560,1024]{1,0:T(8,128)(2,1)S(1)} collective-permute-done((bf16[560,1024]{1,0:T(8,128)(2,1)}, bf16[560,1024]{1,0:T(8,128)(2,1)S(1)}, u32[]{:S(2)}, u32[]{:S(2)}) %collective-permute-start.6) | collective-permute-done | bytes 1146912 | tf_op jit(solution)/shard_map/ppermute | solution.py:386
  33.3 0.0 copy-start.4
  33.3 0.3 collective-permute-start.8
  33.6 0.0 collective-permute-done.7.refs_8_.refs_10_.refs_12_
  33.6 2.9 %collective-permute-start.9 = (bf16[560,1024]{1,0:T(8,128)(2,1)}, bf16[560,1024]{1,0:T(8,128)(2,1)}, u32[]{:S(2)}, u32[]{:S(2)}) collective-permute-start(bf16[560,1024]{1,0:T(8,128)(2,1)} %get-tuple-element.47.refs_5_.refs_7_.refs_9_), channel_id=1, source_target_pairs={{0,12},{1,13},{2,14},{3,15},{4,0},{5,1},{6,2},{7,3},{8,4},{9,5},{1... | collective-permute-start | bytes 3440648 | tf_op jit(solution)/shard_map/ppermute | solution.py:391
  36.5 0.0 collective-permute-done.refs_3_
  36.5 1.9 %collective-permute-start.2 = (bf16[528,1024]{1,0:T(8,128)(2,1)}, bf16[528,1024]{1,0:T(8,128)(2,1)}, u32[]{:S(2)}, u32[]{:S(2)}) collective-permute-start(bf16[528,1024]{1,0:T(8,128)(2,1)} %get-tuple-element.35.refs_2_), channel_id=1, source_target_pairs={{0,1},{1,2},{2,3},{3,0},{4,5},{5,6},{6,7},{7,4},{8,9},{9,10},{10,1... | collective-permute-start | bytes 3244040 | tf_op jit(solution)/shard_map/ppermute | solution.py:390
  38.5 0.0 collective-permute-done.1.refs_4_
  38.5 2.2 %collective-permute-start.3 = (bf16[528,1024]{1,0:T(8,128)(2,1)}, bf16[528,1024]{1,0:T(8,128)(2,1)}, u32[]{:S(2)}, u32[]{:S(2)}) collective-permute-start(bf16[528,1024]{1,0:T(8,128)(2,1)} %get-tuple-element.37.refs_1_), channel_id=1, source_target_pairs={{0,3},{1,0},{2,1},{3,2},{4,7},{5,4},{6,5},{7,6},{8,11},{9,8},{10,9... | collective-permute-start | bytes 3244040 | tf_op jit(solution)/shard_map/ppermute | solution.py:391
  40.7 0.1 stack.127
  40.8 0.1 stack.145
  40.9 20.3 %collective-permute-done.8.refs_11_.refs_13_ = bf16[560,1024]{1,0:T(8,128)(2,1)S(1)} collective-permute-done((bf16[560,1024]{1,0:T(8,128)(2,1)}, bf16[560,1024]{1,0:T(8,128)(2,1)S(1)}, u32[]{:S(2)}, u32[]{:S(2)}) %collective-permute-start.8) | collective-permute-done | bytes 1146912 | tf_op jit(solution)/shard_map/ppermute | solution.py:390
  61.1 0.0 copy-start.5
  61.1 0.0 collective-permute-start.10
  61.1 0.0 collective-permute-done.9.refs_12_.refs_14_
  61.1 3.2 %collective-permute-start.11 = (bf16[560,1024]{1,0:T(8,128)(2,1)}, bf16[560,1024]{1,0:T(8,128)(2,1)}, u32[]{:S(2)}, u32[]{:S(2)}) collective-permute-start(bf16[560,1024]{1,0:T(8,128)(2,1)} %collective-permute-done.7.refs_8_.refs_10_.refs_12_), channel_id=1, source_target_pairs={{0,12},{1,13},{2,14},{3,15},{4,0},{5,1},{6,2},{7,3},{8,4},{9,5},{1... | collective-permute-start | bytes 3440648 | tf_op jit(solution)/shard_map/ppermute | solution.py:395
  64.4 0.6 pad_add_fusion.refs_0_
  65.0 0.0 copy-done.5
  65.0 0.0 collective-permute-done.2.refs_5_
  65.0 1.7 %collective-permute-start.4 = (bf16[528,1024]{1,0:T(8,128)(2,1)}, bf16[528,1024]{1,0:T(8,128)(2,1)}, u32[]{:S(2)}, u32[]{:S(2)}) collective-permute-start(bf16[528,1024]{1,0:T(8,128)(2,1)} %collective-permute-done.refs_3_), channel_id=1, source_target_pairs={{0,1},{1,2},{2,3},{3,0},{4,5},{5,6},{6,7},{7,4},{8,9},{9,10},{10,1... | collective-permute-start | bytes 3244040 | tf_op jit(solution)/shard_map/ppermute | solution.py:394
  66.7 0.0 collective-permute-done.3.refs_6_
  66.7 2.3 %collective-permute-start.5 = (bf16[528,1024]{1,0:T(8,128)(2,1)}, bf16[528,1024]{1,0:T(8,128)(2,1)}, u32[]{:S(2)}, u32[]{:S(2)}) collective-permute-start(bf16[528,1024]{1,0:T(8,128)(2,1)} %collective-permute-done.1.refs_4_), channel_id=1, source_target_pairs={{0,3},{1,0},{2,1},{3,2},{4,7},{5,4},{6,5},{7,6},{8,11},{9,8},{10,9... | collective-permute-start | bytes 3244040 | tf_op jit(solution)/shard_map/ppermute | solution.py:395
  69.0 0.0 copy-done.4
  69.0 11.0 %stage_4.1.refs_13_ = f32[16,64,256]{2,1,0:T(8,128)} custom-call(s32[2,16]{1,0:T(2,128)} %pad_add_fusion.refs_0_, bf16[528,1024]{1,0:T(8,128)(2,1)} %get-tuple-element.37.refs_1_, bf16[528,1024]{1,0:T(8,128)(2,1)} %get-tuple-element.35.refs_2_, bf16[528,1024]{1,0:T(8,128)(2,1)} %collective-permute-done.refs_3_, ...), custom_call_target="tpu_custom_call" | custom-call | flops 6000000000 | bytes 16777216 | tf_op jit(solution)/shard_map/stage_4/pallas_call | solution.py:277
  80.0 13.5 %stage_6.1.refs_17_ = f32[16,64,256]{2,1,0:T(8,128)} custom-call(s32[2,16]{1,0:T(2,128)} %pad_add_fusion.refs_0_, bf16[528,1024]{1,0:T(8,128)(2,1)} %get-tuple-element.37.refs_1_, bf16[528,1024]{1,0:T(8,128)(2,1)} %get-tuple-element.35.refs_2_, bf16[528,1024]{1,0:T(8,128)(2,1)} %collective-permute-done.refs_3_, ...), custom_call_target="tpu_custom_call" | custom-call | flops 6000000000 | bytes 16777216 | tf_op jit(solution)/shard_map/stage_6/pallas_call | solution.py:277
  93.6 0.0 collective-permute-done.4.refs_7_
  93.6 0.0 collective-permute-done.5.refs_8_
  93.6 0.0 collective-permute-done.10.refs_15_
  93.6 0.0 collective-permute-done.11.refs_16_
  93.6 12.6 %stage_8.1 = (f32[4,64,256]{2,1,0:T(8,128)}, f32[4,64,256]{2,1,0:T(8,128)}, f32[4,64,256]{2,1,0:T(8,128)}, f32[4,64,256]{2,1,0:T(8,128)}) custom-call(s32[2,16]{1,0:T(2,128)} %pad_add_fusion.refs_0_, bf16[528,1024]{1,0:T(8,128)(2,1)} %get-tuple-element.37.refs_1_, bf16[528,1024]{1,0:T(8,128)(2,1)} %get-tuple-element.35.refs_2_, ...), custom_call_target="tpu_custom_call" | custom-call | flops 6000000000 | bytes 16777216 | tf_op jit(solution)/shard_map/stage_8/pallas_call | solution.py:277
  106.3 5.0 %collective-permute-start.12 = (f32[4,64,256]{2,1,0:T(8,128)}, f32[4,64,256]{2,1,0:T(8,128)S(1)}, u32[]{:S(2)}, u32[]{:S(2)}) collective-permute-start(f32[4,64,256]{2,1,0:T(8,128)} %get-tuple-element.52), channel_id=1, source_target_pairs={{0,3},{1,0},{2,1},{3,2},{4,7},{5,4},{6,5},{7,6},{8,11},{9,8},{10,9... | collective-permute-start | bytes 786440 | tf_op jit(solution)/shard_map/ppermute | solution.py:403
  111.3 0.0 collective-permute-start.13
  111.3 1.5 collective-permute-start.14
  112.8 7.4 %collective-permute-done.12.a_ref = f32[4,64,256]{2,1,0:T(8,128)S(1)} collective-permute-done((f32[4,64,256]{2,1,0:T(8,128)}, f32[4,64,256]{2,1,0:T(8,128)S(1)}, u32[]{:S(2)}, u32[]{:S(2)}) %collective-permute-start.12) | collective-permute-done | bytes 262176 | tf_op jit(solution)/shard_map/ppermute | solution.py:403
  120.3 0.0 copy-start.1
  120.3 1.6 %collective-permute-done.13.b_ref = f32[4,64,256]{2,1,0:T(8,128)S(1)} collective-permute-done((f32[4,64,256]{2,1,0:T(8,128)}, f32[4,64,256]{2,1,0:T(8,128)S(1)}, u32[]{:S(2)}, u32[]{:S(2)}) %collective-permute-start.13) | collective-permute-done | bytes 262176 | tf_op jit(solution)/shard_map/ppermute | solution.py:404
  121.9 0.0 copy-start.2
  121.9 0.0 collective-permute-done.14.c_ref
  121.9 0.0 copy-done.1
  121.9 0.7 copy-done.2
  122.6 0.1 copy-done.3
  122.7 2.2 %finish.1 = (f32[64,1024]{1,0:T(8,128)}, f32[64,64]{1,0:T(8,128)}) custom-call(f32[4,256]{1,0:T(4,128)} %deg_ref.1, f32[4,64,256]{2,1,0:T(8,128)} %get-tuple-element.51.own_ref, f32[4,64,256]{2,1,0:T(8,128)} %copy-done.1, f32[4,64,256]{2,1,0:T(8,128)} %copy-done.2, f32[4,64,256]{2,1,0:T(8,128)} %copy-done.3), custom_call_target="tpu_custom_call" | custom-call | tf_op jit(solution)/shard_map/finish/pallas_call | solution.py:324
  124.9 0.0 collective-permute-start.15
  124.9 1.4 collective-permute-done.15
  126.3 0.8 add.298
  127.1 0.0 collective-permute-start.16
  127.1 3.9 %collective-permute-done.16 = f32[64,64]{1,0:T(8,128)S(1)} collective-permute-done((f32[64,64]{1,0:T(8,128)S(1)}, f32[64,64]{1,0:T(8,128)S(1)}, u32[]{:S(2)}, u32[]{:S(2)}) %collective-permute-start.16) | collective-permute-done | bytes 16416 | tf_op jit(solution)/shard_map/ppermute | solution.py:415
  131.0 4.7 %collective-permute-start.17 = (f32[64,64]{1,0:T(8,128)S(1)}, f32[64,64]{1,0:T(8,128)S(1)}, u32[]{:S(2)}, u32[]{:S(2)}) collective-permute-start(f32[64,64]{1,0:T(8,128)S(1)} %add.299), channel_id=1, source_target_pairs={{0,64},{16,80},{32,96},{48,112},{64,0},{80,16},{96,32},{112,48},{1... | collective-permute-start | bytes 49160 | tf_op jit(solution)/shard_map/ppermute | solution.py:415
  135.7 1.9 %collective-permute-done.17 = f32[64,64]{1,0:T(8,128)S(1)} collective-permute-done((f32[64,64]{1,0:T(8,128)S(1)}, f32[64,64]{1,0:T(8,128)S(1)}, u32[]{:S(2)}, u32[]{:S(2)}) %collective-permute-start.17) | collective-permute-done | bytes 16416 | tf_op jit(solution)/shard_map/ppermute | solution.py:415
  137.6 0.1 collective-permute-start.18
  137.8 3.8 %collective-permute-done.18 = f32[64,64]{1,0:T(8,128)S(1)} collective-permute-done((f32[64,64]{1,0:T(8,128)S(1)}, f32[64,64]{1,0:T(8,128)S(1)}, u32[]{:S(2)}, u32[]{:S(2)}) %collective-permute-start.18) | collective-permute-done | bytes 16416 | tf_op jit(solution)/shard_map/ppermute | solution.py:415
  141.6 1.8 %collective-permute-start.19 = (f32[64,64]{1,0:T(8,128)S(1)}, f32[64,64]{1,0:T(8,128)S(1)}, u32[]{:S(2)}, u32[]{:S(2)}) collective-permute-start(f32[64,64]{1,0:T(8,128)S(1)} %add.301), channel_id=1, source_target_pairs={{0,2},{1,3},{2,0},{3,1},{4,6},{5,7},{6,4},{7,5},{8,10},{9,11},{10,... | collective-permute-start | bytes 49160 | tf_op jit(solution)/shard_map/ppermute | solution.py:415
  143.4 3.6 %collective-permute-done.19 = f32[64,64]{1,0:T(8,128)S(1)} collective-permute-done((f32[64,64]{1,0:T(8,128)S(1)}, f32[64,64]{1,0:T(8,128)S(1)}, u32[]{:S(2)}, u32[]{:S(2)}) %collective-permute-start.19) | collective-permute-done | bytes 16416 | tf_op jit(solution)/shard_map/ppermute | solution.py:415
  147.0 0.0 collective-permute-start.20
  147.0 4.0 %collective-permute-done.20 = f32[64,64]{1,0:T(8,128)S(1)} collective-permute-done((f32[64,64]{1,0:T(8,128)S(1)}, f32[64,64]{1,0:T(8,128)S(1)}, u32[]{:S(2)}, u32[]{:S(2)}) %collective-permute-start.20) | collective-permute-done | bytes 16416 | tf_op jit(solution)/shard_map/ppermute | solution.py:415
  151.0 3.3 %collective-permute-start.21 = (f32[64,64]{1,0:T(8,128)S(1)}, f32[64,64]{1,0:T(8,128)S(1)}, u32[]{:S(2)}, u32[]{:S(2)}) collective-permute-start(f32[64,64]{1,0:T(8,128)S(1)} %add.303.gram_ref), channel_id=1, source_target_pairs={{0,8},{1,9},{2,10},{3,11},{4,12},{5,13},{6,14},{7,15},{8,0},{9,1},... | collective-permute-start | bytes 49160 | tf_op jit(solution)/shard_map/ppermute | solution.py:415
  154.4 2.1 %collective-permute-done.21.other_ref = f32[64,64]{1,0:T(8,128)S(1)} collective-permute-done((f32[64,64]{1,0:T(8,128)S(1)}, f32[64,64]{1,0:T(8,128)S(1)}, u32[]{:S(2)}, u32[]{:S(2)}) %collective-permute-start.21) | collective-permute-done | bytes 16416 | tf_op jit(solution)/shard_map/ppermute | solution.py:415
  156.5 0.9 copy-done
  157.4 3.0 %solve.1 = f32[4,64,256]{2,1,0:T(8,128)} custom-call(f32[64,64]{1,0:T(8,128)S(1)} %add.303.gram_ref, f32[64,64]{1,0:T(8,128)S(1)} %collective-permute-done.21.other_ref, f32[64,1024]{1,0:T(8,128)S(1)} %copy-done), custom_call_target="tpu_custom_call" | custom-call | tf_op jit(solution)/shard_map/solve/pallas_call | solution.py:360
  (7 shorter events, 0.0 us)
Async XLA Ops:
  4.7 28.6 %collective-permute-start.6 = (bf16[560,1024]{1,0:T(8,128)(2,1)}, bf16[560,1024]{1,0:T(8,128)(2,1)S(1)}, u32[]{:S(2)}, u32[]{:S(2)}) collective-permute-start(bf16[560,1024]{1,0:T(8,128)(2,1)} %get-tuple-element.47.refs_5_.refs_7_.refs_9_), channel_id=1, source_target_pairs={{0,4},{1,5},{2,6},{3,7},{4,8},{5,9},{6,10},{7,11},{8,12},{9,13},{1... | collective-permute-start | bytes 3440648 | tf_op jit(solution)/shard_map/ppermute | solution.py:386
  6.4 27.2 %collective-permute-start.7 = (bf16[560,1024]{1,0:T(8,128)(2,1)}, bf16[560,1024]{1,0:T(8,128)(2,1)}, u32[]{:S(2)}, u32[]{:S(2)}) collective-permute-start(bf16[560,1024]{1,0:T(8,128)(2,1)} %get-tuple-element.45.refs_6_.refs_8_.refs_10_), channel_id=1, source_target_pairs={{0,12},{1,13},{2,14},{3,15},{4,0},{5,1},{6,2},{7,3},{8,4},{9,5},{1... | collective-permute-start | bytes 3440648 | tf_op jit(solution)/shard_map/ppermute | solution.py:387
  8.0 28.6 %collective-permute-start = (bf16[528,1024]{1,0:T(8,128)(2,1)}, bf16[528,1024]{1,0:T(8,128)(2,1)}, u32[]{:S(2)}, u32[]{:S(2)}) collective-permute-start(bf16[528,1024]{1,0:T(8,128)(2,1)} %get-tuple-element.37.refs_1_), channel_id=1, source_target_pairs={{0,1},{1,2},{2,3},{3,0},{4,5},{5,6},{6,7},{7,4},{8,9},{9,10},{10,1... | collective-permute-start | bytes 3244040 | tf_op jit(solution)/shard_map/ppermute | solution.py:386
  10.0 28.5 %collective-permute-start.1 = (bf16[528,1024]{1,0:T(8,128)(2,1)}, bf16[528,1024]{1,0:T(8,128)(2,1)}, u32[]{:S(2)}, u32[]{:S(2)}) collective-permute-start(bf16[528,1024]{1,0:T(8,128)(2,1)} %get-tuple-element.35.refs_2_), channel_id=1, source_target_pairs={{0,3},{1,0},{2,1},{3,2},{4,7},{5,4},{6,5},{7,6},{8,11},{9,8},{10,9... | collective-permute-start | bytes 3244040 | tf_op jit(solution)/shard_map/ppermute | solution.py:387
  33.3 35.7 %copy-start.4 = (bf16[560,1024]{1,0:T(8,128)(2,1)}, bf16[560,1024]{1,0:T(8,128)(2,1)S(1)}, u32[]{:S(2)}) copy-start(bf16[560,1024]{1,0:T(8,128)(2,1)S(1)} %collective-permute-done.6.refs_7_.refs_9_.refs_11_) | copy-start | bytes 3440644
  33.3 27.8 %collective-permute-start.8 = (bf16[560,1024]{1,0:T(8,128)(2,1)}, bf16[560,1024]{1,0:T(8,128)(2,1)S(1)}, u32[]{:S(2)}, u32[]{:S(2)}) collective-permute-start(bf16[560,1024]{1,0:T(8,128)(2,1)} %get-tuple-element.45.refs_6_.refs_8_.refs_10_), channel_id=1, source_target_pairs={{0,4},{1,5},{2,6},{3,7},{4,8},{5,9},{6,10},{7,11},{8,12},{9,13},{1... | collective-permute-start | bytes 3440648 | tf_op jit(solution)/shard_map/ppermute | solution.py:390
  33.6 27.5 %collective-permute-start.9 = (bf16[560,1024]{1,0:T(8,128)(2,1)}, bf16[560,1024]{1,0:T(8,128)(2,1)}, u32[]{:S(2)}, u32[]{:S(2)}) collective-permute-start(bf16[560,1024]{1,0:T(8,128)(2,1)} %get-tuple-element.47.refs_5_.refs_7_.refs_9_), channel_id=1, source_target_pairs={{0,12},{1,13},{2,14},{3,15},{4,0},{5,1},{6,2},{7,3},{8,4},{9,5},{1... | collective-permute-start | bytes 3440648 | tf_op jit(solution)/shard_map/ppermute | solution.py:391
  36.5 28.4 %collective-permute-start.2 = (bf16[528,1024]{1,0:T(8,128)(2,1)}, bf16[528,1024]{1,0:T(8,128)(2,1)}, u32[]{:S(2)}, u32[]{:S(2)}) collective-permute-start(bf16[528,1024]{1,0:T(8,128)(2,1)} %get-tuple-element.35.refs_2_), channel_id=1, source_target_pairs={{0,1},{1,2},{2,3},{3,0},{4,5},{5,6},{6,7},{7,4},{8,9},{9,10},{10,1... | collective-permute-start | bytes 3244040 | tf_op jit(solution)/shard_map/ppermute | solution.py:390
  38.5 28.2 %collective-permute-start.3 = (bf16[528,1024]{1,0:T(8,128)(2,1)}, bf16[528,1024]{1,0:T(8,128)(2,1)}, u32[]{:S(2)}, u32[]{:S(2)}) collective-permute-start(bf16[528,1024]{1,0:T(8,128)(2,1)} %get-tuple-element.37.refs_1_), channel_id=1, source_target_pairs={{0,3},{1,0},{2,1},{3,2},{4,7},{5,4},{6,5},{7,6},{8,11},{9,8},{10,9... | collective-permute-start | bytes 3244040 | tf_op jit(solution)/shard_map/ppermute | solution.py:391
  61.1 3.8 %copy-start.5 = (bf16[560,1024]{1,0:T(8,128)(2,1)}, bf16[560,1024]{1,0:T(8,128)(2,1)S(1)}, u32[]{:S(2)}) copy-start(bf16[560,1024]{1,0:T(8,128)(2,1)S(1)} %collective-permute-done.8.refs_11_.refs_13_) | copy-start | bytes 3440644
  61.1 32.5 %collective-permute-start.10 = (bf16[560,1024]{1,0:T(8,128)(2,1)S(1)}, bf16[560,1024]{1,0:T(8,128)(2,1)}, u32[]{:S(2)}, u32[]{:S(2)}) collective-permute-start(bf16[560,1024]{1,0:T(8,128)(2,1)S(1)} %collective-permute-done.6.refs_7_.refs_9_.refs_11_), channel_id=1, source_target_pairs={{0,4},{1,5},{2,6},{3,7},{4,8},{5,9},{6,10},{7,11},{8,12},{9,13},{1... | collective-permute-start | bytes 3440648 | tf_op jit(solution)/shard_map/ppermute | solution.py:394
  61.1 32.5 %collective-permute-start.11 = (bf16[560,1024]{1,0:T(8,128)(2,1)}, bf16[560,1024]{1,0:T(8,128)(2,1)}, u32[]{:S(2)}, u32[]{:S(2)}) collective-permute-start(bf16[560,1024]{1,0:T(8,128)(2,1)} %collective-permute-done.7.refs_8_.refs_10_.refs_12_), channel_id=1, source_target_pairs={{0,12},{1,13},{2,14},{3,15},{4,0},{5,1},{6,2},{7,3},{8,4},{9,5},{1... | collective-permute-start | bytes 3440648 | tf_op jit(solution)/shard_map/ppermute | solution.py:395
  65.0 28.6 %collective-permute-start.4 = (bf16[528,1024]{1,0:T(8,128)(2,1)}, bf16[528,1024]{1,0:T(8,128)(2,1)}, u32[]{:S(2)}, u32[]{:S(2)}) collective-permute-start(bf16[528,1024]{1,0:T(8,128)(2,1)} %collective-permute-done.refs_3_), channel_id=1, source_target_pairs={{0,1},{1,2},{2,3},{3,0},{4,5},{5,6},{6,7},{7,4},{8,9},{9,10},{10,1... | collective-permute-start | bytes 3244040 | tf_op jit(solution)/shard_map/ppermute | solution.py:394
  66.7 26.9 %collective-permute-start.5 = (bf16[528,1024]{1,0:T(8,128)(2,1)}, bf16[528,1024]{1,0:T(8,128)(2,1)}, u32[]{:S(2)}, u32[]{:S(2)}) collective-permute-start(bf16[528,1024]{1,0:T(8,128)(2,1)} %collective-permute-done.1.refs_4_), channel_id=1, source_target_pairs={{0,3},{1,0},{2,1},{3,2},{4,7},{5,4},{6,5},{7,6},{8,11},{9,8},{10,9... | collective-permute-start | bytes 3244040 | tf_op jit(solution)/shard_map/ppermute | solution.py:395
  106.3 14.0 %collective-permute-start.12 = (f32[4,64,256]{2,1,0:T(8,128)}, f32[4,64,256]{2,1,0:T(8,128)S(1)}, u32[]{:S(2)}, u32[]{:S(2)}) collective-permute-start(f32[4,64,256]{2,1,0:T(8,128)} %get-tuple-element.52), channel_id=1, source_target_pairs={{0,3},{1,0},{2,1},{3,2},{4,7},{5,4},{6,5},{7,6},{8,11},{9,8},{10,9... | collective-permute-start | bytes 786440 | tf_op jit(solution)/shard_map/ppermute | solution.py:403
  111.3 10.6 %collective-permute-start.13 = (f32[4,64,256]{2,1,0:T(8,128)}, f32[4,64,256]{2,1,0:T(8,128)S(1)}, u32[]{:S(2)}, u32[]{:S(2)}) collective-permute-start(f32[4,64,256]{2,1,0:T(8,128)} %get-tuple-element.53), channel_id=1, source_target_pairs={{0,1},{1,2},{2,3},{3,0},{4,5},{5,6},{6,7},{7,4},{8,9},{9,10},{10,1... | collective-permute-start | bytes 786440 | tf_op jit(solution)/shard_map/ppermute | solution.py:404
  111.3 10.6 %collective-permute-start.14 = (f32[4,64,256]{2,1,0:T(8,128)}, f32[4,64,256]{2,1,0:T(8,128)S(1)}, u32[]{:S(2)}, u32[]{:S(2)}) collective-permute-start(f32[4,64,256]{2,1,0:T(8,128)} %get-tuple-element.54), channel_id=1, source_target_pairs={{0,2},{1,3},{2,0},{3,1},{4,6},{5,7},{6,4},{7,5},{8,10},{9,11},{10,... | collective-permute-start | bytes 786440 | tf_op jit(solution)/shard_map/ppermute | solution.py:405
  120.3 1.6 %copy-start.1 = (f32[4,64,256]{2,1,0:T(8,128)}, f32[4,64,256]{2,1,0:T(8,128)S(1)}, u32[]{:S(2)}) copy-start(f32[4,64,256]{2,1,0:T(8,128)S(1)} %collective-permute-done.12.a_ref) | copy-start | bytes 786436
  121.9 0.7 copy-start.2
  121.9 0.8 copy-start.3
  124.9 1.4 collective-permute-start.15
  127.1 3.9 %collective-permute-start.16 = (f32[64,64]{1,0:T(8,128)S(1)}, f32[64,64]{1,0:T(8,128)S(1)}, u32[]{:S(2)}, u32[]{:S(2)}) collective-permute-start(f32[64,64]{1,0:T(8,128)S(1)} %add.298), channel_id=1, source_target_pairs={{0,32},{16,48},{32,0},{48,16},{64,96},{80,112},{96,64},{112,80},{1... | collective-permute-start | bytes 49160 | tf_op jit(solution)/shard_map/ppermute | solution.py:415
  131.0 6.6 %collective-permute-start.17 = (f32[64,64]{1,0:T(8,128)S(1)}, f32[64,64]{1,0:T(8,128)S(1)}, u32[]{:S(2)}, u32[]{:S(2)}) collective-permute-start(f32[64,64]{1,0:T(8,128)S(1)} %add.299), channel_id=1, source_target_pairs={{0,64},{16,80},{32,96},{48,112},{64,0},{80,16},{96,32},{112,48},{1... | collective-permute-start | bytes 49160 | tf_op jit(solution)/shard_map/ppermute | solution.py:415
  137.6 3.9 %collective-permute-start.18 = (f32[64,64]{1,0:T(8,128)S(1)}, f32[64,64]{1,0:T(8,128)S(1)}, u32[]{:S(2)}, u32[]{:S(2)}) collective-permute-start(f32[64,64]{1,0:T(8,128)S(1)} %add.300), channel_id=1, source_target_pairs={{0,1},{1,0},{2,3},{3,2},{4,5},{5,4},{6,7},{7,6},{8,9},{9,8},{10,11... | collective-permute-start | bytes 49160 | tf_op jit(solution)/shard_map/ppermute | solution.py:415
  141.6 5.4 %collective-permute-start.19 = (f32[64,64]{1,0:T(8,128)S(1)}, f32[64,64]{1,0:T(8,128)S(1)}, u32[]{:S(2)}, u32[]{:S(2)}) collective-permute-start(f32[64,64]{1,0:T(8,128)S(1)} %add.301), channel_id=1, source_target_pairs={{0,2},{1,3},{2,0},{3,1},{4,6},{5,7},{6,4},{7,5},{8,10},{9,11},{10,... | collective-permute-start | bytes 49160 | tf_op jit(solution)/shard_map/ppermute | solution.py:415
  147.0 4.0 %collective-permute-start.20 = (f32[64,64]{1,0:T(8,128)S(1)}, f32[64,64]{1,0:T(8,128)S(1)}, u32[]{:S(2)}, u32[]{:S(2)}) collective-permute-start(f32[64,64]{1,0:T(8,128)S(1)} %add.302), channel_id=1, source_target_pairs={{0,4},{1,5},{2,6},{3,7},{4,0},{5,1},{6,2},{7,3},{8,12},{9,13},{10,... | collective-permute-start | bytes 49160 | tf_op jit(solution)/shard_map/ppermute | solution.py:415
  151.0 5.4 %collective-permute-start.21 = (f32[64,64]{1,0:T(8,128)S(1)}, f32[64,64]{1,0:T(8,128)S(1)}, u32[]{:S(2)}, u32[]{:S(2)}) collective-permute-start(f32[64,64]{1,0:T(8,128)S(1)} %add.303.gram_ref), channel_id=1, source_target_pairs={{0,8},{1,9},{2,10},{3,11},{4,12},{5,13},{6,14},{7,15},{8,0},{9,1},... | collective-permute-start | bytes 49160 | tf_op jit(solution)/shard_map/ppermute | solution.py:415
  156.5 1.0 copy-start

commit v4 on v3

--- a/solution.py
+++ b/solution.py
@@ -252,7 +252,7 @@
     if last:
         for out, order in zip(outs, ((0, 1, 2, 3), (4, 5, 8, 9), (10, 11, 6, 7), (12, 13, 14, 15))):
             for k, s in enumerate(order):
-                out[k] = acc[s]
+                out[k] = acc[s].astype(out.dtype)
     else:
         acc_out[...] = acc[...]
 
@@ -268,7 +268,9 @@
         operands.append(acc)
         in_specs.append(hbm)
     if last:
-        out_shape = tuple(jax.ShapeDtypeStruct((OWN, COLS, ROWS), jnp.float32) for _ in range(4))
+        out_shape = tuple(
+            jax.ShapeDtypeStruct((OWN, COLS, ROWS), kind) for kind in (jnp.float32,) * 4
+        )
         out_specs = (vmem,) * 4
     else:
         out_shape = jax.ShapeDtypeStruct((16, COLS, ROWS), jnp.float32)
@@ -312,12 +314,14 @@
     parts = []
     for b in range(OWN):
         inv = 1.0 / jnp.sqrt(deg_ref[b:b + 1, :])
-        parts.append((own_ref[b] + a_ref[b] + (b_ref[b] + c_ref[b])) * inv)
+        far = [ref[b].astype(jnp.float32) for ref in (a_ref, b_ref, c_ref)]
+        parts.append((own_ref[b] + far[0] + (far[1] + far[2])) * inv)
     image = jnp.concatenate(parts, axis=1)
     image_ref[...] = image
-    gram_ref[...] = lax.dot_general(
+    gram = lax.dot_general(
         image, image, NT, precision=lax.Precision.HIGHEST, preferred_element_type=jnp.float32
     )
+    gram_ref[...] = jnp.concatenate([gram[:COLS // 2], gram[COLS // 2:]], axis=1)
 
 
 def finish(degree, own, a, b, c):
@@ -325,15 +329,18 @@
         finish_kernel,
         out_shape=(
             jax.ShapeDtypeStruct((COLS, DOCS), jnp.float32),
-            jax.ShapeDtypeStruct((COLS, COLS), jnp.float32),
+            jax.ShapeDtypeStruct((COLS // 2, 2 * COLS), jnp.float32),
         ),
-        compiler_params=pltpu.CompilerParams(vmem_limit_bytes=VMEM_LIMIT),
+        compiler_params=pltpu.CompilerParams(vmem_limit_bytes=SMALL_LIMIT),
         name="finish",
     )(degree, own, a, b, c)
 
 
-def solve_kernel(documents, gram_ref, other_ref, image_ref, out_ref):
-    gram = (gram_ref[...] + other_ref[...]) / documents
+def solve_kernel(documents, gram_ref, other_ref, image_hbm, out_ref, image_ref, sem):
+    load = pltpu.make_async_copy(image_hbm, image_ref, sem)
+    load.start()
+    packed = (gram_ref[...] + other_ref[...]) / documents
+    gram = jnp.concatenate([packed[:, :COLS], packed[:, COLS:]], axis=0)
     row_id = lax.broadcasted_iota(jnp.int32, (COLS, 2 * COLS), 0)
     lane_id = lax.broadcasted_iota(jnp.int32, (COLS, 2 * COLS), 1)
     unit = (row_id[:, :COLS] == lane_id[:, :COLS]).astype(jnp.float32)
@@ -349,6 +356,7 @@
             work = work - factor * work[k:k + 1, :]
     pivots = jnp.sum(jnp.where(row_id == lane_id, work, 0.0), axis=1, keepdims=True)
     inverse = work[:, COLS:] / jnp.sqrt(pivots)
+    load.wait()
     for b in range(OWN):
         out_ref[b] = lax.dot_general(
             inverse, image_ref[:, b * ROWS:(b + 1) * ROWS], NN,
@@ -357,9 +365,12 @@
 
 
 def solve(documents, gram, other, image):
+    vmem = pl.BlockSpec(memory_space=pltpu.VMEM)
     return pl.pallas_call(
         functools.partial(solve_kernel, float(documents)),
         out_shape=jax.ShapeDtypeStruct((OWN, COLS, ROWS), jnp.float32),
+        in_specs=[vmem, vmem, pl.BlockSpec(memory_space=pltpu.HBM)],
+        scratch_shapes=[pltpu.VMEM((COLS, DOCS), jnp.float32), pltpu.SemaphoreType.DMA],
         compiler_params=pltpu.CompilerParams(vmem_limit_bytes=SMALL_LIMIT),
         name="solve",
     )(gram, other, image)

time: 161 us -> 157 us (0.975)
  starting transfers between devices: 38.6 us -> 33.2 us
  waiting for transfers between devices: 71.3 us -> 74.2 us
    ppermute x1, starting transfers between devices: 5.04 us -> 1.01 us  [per_device(): back_a = lax.ppermute(to_minus, 'blk', shift_z(-1))]
    ppermute x1, waiting for transfers between devices: 1.62 us -> 5.04 us  [per_device(): back_b = lax.ppermute(to_plus, 'blk', shift_z(1))]
    ppermute x1, waiting for transfers between devices: 7.43 us -> 4.35 us  [per_device(): back_a = lax.ppermute(to_minus, 'blk', shift_z(-1))]
    ppermute x6, starting transfers between devices: 10 us -> 7.45 us  [per_device(): other = lax.ppermute(gram, axis, [(i, i ^ step) for i in range(size)])]
    pallas_call x1, Pallas kernels: 2.2 us -> 0.46 us  [finish(): pl.pallas_call(finish_kernel, out_shape=(jax.ShapeDtypeStruct((COLS, DOCS...]
    ppermute x6, waiting for transfers between devices: 19.3 us -> 21 us  [per_device(): other = lax.ppermute(gram, axis, [(i, i ^ step) for i in range(size)])]
  transfers between devices with their start and end apart: 22 -> 22, of which waited for: 11 -> 12; matrix products, arithmetic and copies ran while one was open for 0% -> 0% of each run, Pallas kernels for 15% -> 13%
where the time goes in v4:
time: 157 us; the launch traced here: 156 us
  waiting for transfers between devices  74.2 us (47%)
  Pallas kernels  46.4 us (30%)
  starting transfers between devices  33.2 us (21%)
    pallas_call x3, Pallas kernels, stage(): pl.pallas_call(functools.partial(stage_kernel, old, new, last), out_shape...  38.3 us
    ppermute x2, waiting for transfers between devices, gather(): minus_a = lax.ppermute(a, 'blk', shift(1))  21.2 us
    ppermute x6, waiting for transfers between devices, per_device(): other = lax.ppermute(gram, axis, [(i, i ^ step) for i in range(size)])  21 us
    ppermute x2, waiting for transfers between devices, gather(): minus_b = lax.ppermute(b_next, 'blk', shift(1))  20.3 us
    ppermute x6, starting transfers between devices, per_device(): other = lax.ppermute(gram, axis, [(i, i ^ step) for i in range(size)])  7.45 us
    ppermute x2, starting transfers between devices, gather(): far_b = lax.ppermute(plus_next, 'blk', shift(-1))  5.54 us
    ppermute x2, starting transfers between devices, gather(): plus_a = lax.ppermute(a_next, 'blk', shift(-1))  5.13 us
    ppermute x1, waiting for transfers between devices, per_device(): back_b = lax.ppermute(to_plus, 'blk', shift_z(1))  5.04 us
  transfers between devices with their start and end apart: 22, of which 12 were waited for; matrix products, arithmetic and copies ran while one was open for 0% of the time, Pallas kernels for 13%

profile of v4, /device:TPU:0, one launch (start us, length us, event | category | flops | bytes accessed | tf_op | source)
XLA Modules:
  0.0 155.8 jit_solution(7495722542755794528)
XLA Ops:
  0.0 4.7 %prepare.1 = (bf16[528,1024]{1,0:T(8,128)(2,1)}, bf16[528,1024]{1,0:T(8,128)(2,1)}, bf16[560,1024]{1,0:T(8,128)(2,1)}, bf16[560,1024]{1,0:T(8,128)(2,1)}) custom-call(s32[4,16]{1,0:T(4,128)} %nbr_hbm.1, s32[4]{0:T(128)} %cnt_hbm.1, bf16[1024,1024]{1,0:T(8,128)(2,1)} %bitcast.37, f32[4,64,256]{2,1,0:T(8,128)} %bitcast.38, f32[4,256]{1,0:T(4,128)} %deg_ref.1), custom_call_target="tpu_custom_call" | custom-call | tf_op jit(solution)/shard_map/prepare/pallas_call | solution.py:110
  4.7 1.7 %collective-permute-start.6 = (bf16[560,1024]{1,0:T(8,128)(2,1)}, bf16[560,1024]{1,0:T(8,128)(2,1)S(1)}, u32[]{:S(2)}, u32[]{:S(2)}) collective-permute-start(bf16[560,1024]{1,0:T(8,128)(2,1)} %get-tuple-element.47.refs_5_.refs_7_.refs_9_), channel_id=1, source_target_pairs={{0,4},{1,5},{2,6},{3,7},{4,8},{5,9},{6,10},{7,11},{8,12},{9,13},{1... | collective-permute-start | bytes 3440648 | tf_op jit(solution)/shard_map/ppermute | solution.py:397
  6.4 1.6 %collective-permute-start.7 = (bf16[560,1024]{1,0:T(8,128)(2,1)}, bf16[560,1024]{1,0:T(8,128)(2,1)}, u32[]{:S(2)}, u32[]{:S(2)}) collective-permute-start(bf16[560,1024]{1,0:T(8,128)(2,1)} %get-tuple-element.45.refs_6_.refs_8_.refs_10_), channel_id=1, source_target_pairs={{0,12},{1,13},{2,14},{3,15},{4,0},{5,1},{6,2},{7,3},{8,4},{9,5},{1... | collective-permute-start | bytes 3440648 | tf_op jit(solution)/shard_map/ppermute | solution.py:398
  8.0 2.0 %collective-permute-start = (bf16[528,1024]{1,0:T(8,128)(2,1)}, bf16[528,1024]{1,0:T(8,128)(2,1)}, u32[]{:S(2)}, u32[]{:S(2)}) collective-permute-start(bf16[528,1024]{1,0:T(8,128)(2,1)} %get-tuple-element.37.refs_1_), channel_id=1, source_target_pairs={{0,1},{1,2},{2,3},{3,0},{4,5},{5,6},{6,7},{7,4},{8,9},{9,10},{10,1... | collective-permute-start | bytes 3244040 | tf_op jit(solution)/shard_map/ppermute | solution.py:397
  10.0 2.1 %collective-permute-start.1 = (bf16[528,1024]{1,0:T(8,128)(2,1)}, bf16[528,1024]{1,0:T(8,128)(2,1)}, u32[]{:S(2)}, u32[]{:S(2)}) collective-permute-start(bf16[528,1024]{1,0:T(8,128)(2,1)} %get-tuple-element.35.refs_2_), channel_id=1, source_target_pairs={{0,3},{1,0},{2,1},{3,2},{4,7},{5,4},{6,5},{7,6},{8,11},{9,8},{10,9... | collective-permute-start | bytes 3244040 | tf_op jit(solution)/shard_map/ppermute | solution.py:398
  12.1 21.2 %collective-permute-done.6.refs_7_.refs_9_.refs_11_ = bf16[560,1024]{1,0:T(8,128)(2,1)S(1)} collective-permute-done((bf16[560,1024]{1,0:T(8,128)(2,1)}, bf16[560,1024]{1,0:T(8,128)(2,1)S(1)}, u32[]{:S(2)}, u32[]{:S(2)}) %collective-permute-start.6) | collective-permute-done | bytes 1146912 | tf_op jit(solution)/shard_map/ppermute | solution.py:397
  33.3 0.0 copy-start.2
  33.3 0.3 collective-permute-start.8
  33.6 0.0 collective-permute-done.7.refs_8_.refs_10_.refs_12_
  33.6 2.9 %collective-permute-start.9 = (bf16[560,1024]{1,0:T(8,128)(2,1)}, bf16[560,1024]{1,0:T(8,128)(2,1)}, u32[]{:S(2)}, u32[]{:S(2)}) collective-permute-start(bf16[560,1024]{1,0:T(8,128)(2,1)} %get-tuple-element.47.refs_5_.refs_7_.refs_9_), channel_id=1, source_target_pairs={{0,12},{1,13},{2,14},{3,15},{4,0},{5,1},{6,2},{7,3},{8,4},{9,5},{1... | collective-permute-start | bytes 3440648 | tf_op jit(solution)/shard_map/ppermute | solution.py:402
  36.6 0.0 collective-permute-done.refs_3_
  36.6 1.9 %collective-permute-start.2 = (bf16[528,1024]{1,0:T(8,128)(2,1)}, bf16[528,1024]{1,0:T(8,128)(2,1)}, u32[]{:S(2)}, u32[]{:S(2)}) collective-permute-start(bf16[528,1024]{1,0:T(8,128)(2,1)} %get-tuple-element.35.refs_2_), channel_id=1, source_target_pairs={{0,1},{1,2},{2,3},{3,0},{4,5},{5,6},{6,7},{7,4},{8,9},{9,10},{10,1... | collective-permute-start | bytes 3244040 | tf_op jit(solution)/shard_map/ppermute | solution.py:401
  38.5 0.0 collective-permute-done.1.refs_4_
  38.5 2.2 %collective-permute-start.3 = (bf16[528,1024]{1,0:T(8,128)(2,1)}, bf16[528,1024]{1,0:T(8,128)(2,1)}, u32[]{:S(2)}, u32[]{:S(2)}) collective-permute-start(bf16[528,1024]{1,0:T(8,128)(2,1)} %get-tuple-element.37.refs_1_), channel_id=1, source_target_pairs={{0,3},{1,0},{2,1},{3,2},{4,7},{5,4},{6,5},{7,6},{8,11},{9,8},{10,9... | collective-permute-start | bytes 3244040 | tf_op jit(solution)/shard_map/ppermute | solution.py:402
  40.7 0.1 stack.127
  40.8 0.1 stack.145
  40.9 20.3 %collective-permute-done.8.refs_11_.refs_13_ = bf16[560,1024]{1,0:T(8,128)(2,1)S(1)} collective-permute-done((bf16[560,1024]{1,0:T(8,128)(2,1)}, bf16[560,1024]{1,0:T(8,128)(2,1)S(1)}, u32[]{:S(2)}, u32[]{:S(2)}) %collective-permute-start.8) | collective-permute-done | bytes 1146912 | tf_op jit(solution)/shard_map/ppermute | solution.py:401
  61.1 0.0 copy-start.3
  61.1 0.0 collective-permute-start.10
  61.1 0.0 collective-permute-done.9.refs_12_.refs_14_
  61.2 3.2 %collective-permute-start.11 = (bf16[560,1024]{1,0:T(8,128)(2,1)}, bf16[560,1024]{1,0:T(8,128)(2,1)}, u32[]{:S(2)}, u32[]{:S(2)}) collective-permute-start(bf16[560,1024]{1,0:T(8,128)(2,1)} %collective-permute-done.7.refs_8_.refs_10_.refs_12_), channel_id=1, source_target_pairs={{0,12},{1,13},{2,14},{3,15},{4,0},{5,1},{6,2},{7,3},{8,4},{9,5},{1... | collective-permute-start | bytes 3440648 | tf_op jit(solution)/shard_map/ppermute | solution.py:406
  64.4 0.6 pad_add_fusion.refs_0_
  65.0 0.0 copy-done.3
  65.0 0.0 collective-permute-done.2.refs_5_
  65.0 1.7 %collective-permute-start.4 = (bf16[528,1024]{1,0:T(8,128)(2,1)}, bf16[528,1024]{1,0:T(8,128)(2,1)}, u32[]{:S(2)}, u32[]{:S(2)}) collective-permute-start(bf16[528,1024]{1,0:T(8,128)(2,1)} %collective-permute-done.refs_3_), channel_id=1, source_target_pairs={{0,1},{1,2},{2,3},{3,0},{4,5},{5,6},{6,7},{7,4},{8,9},{9,10},{10,1... | collective-permute-start | bytes 3244040 | tf_op jit(solution)/shard_map/ppermute | solution.py:405
  66.7 0.0 collective-permute-done.3.refs_6_
  66.7 2.3 %collective-permute-start.5 = (bf16[528,1024]{1,0:T(8,128)(2,1)}, bf16[528,1024]{1,0:T(8,128)(2,1)}, u32[]{:S(2)}, u32[]{:S(2)}) collective-permute-start(bf16[528,1024]{1,0:T(8,128)(2,1)} %collective-permute-done.1.refs_4_), channel_id=1, source_target_pairs={{0,3},{1,0},{2,1},{3,2},{4,7},{5,4},{6,5},{7,6},{8,11},{9,8},{10,9... | collective-permute-start | bytes 3244040 | tf_op jit(solution)/shard_map/ppermute | solution.py:406
  69.0 0.0 copy-done.2
  69.0 9.2 %stage_4.1.refs_13_ = f32[16,64,256]{2,1,0:T(8,128)} custom-call(s32[2,16]{1,0:T(2,128)} %pad_add_fusion.refs_0_, bf16[528,1024]{1,0:T(8,128)(2,1)} %get-tuple-element.37.refs_1_, bf16[528,1024]{1,0:T(8,128)(2,1)} %get-tuple-element.35.refs_2_, bf16[528,1024]{1,0:T(8,128)(2,1)} %collective-permute-done.refs_3_, ...), custom_call_target="tpu_custom_call" | custom-call | flops 6000000000 | bytes 16777216 | tf_op jit(solution)/shard_map/stage_4/pallas_call | solution.py:279
  78.2 11.7 %stage_6.1.refs_17_ = f32[16,64,256]{2,1,0:T(8,128)} custom-call(s32[2,16]{1,0:T(2,128)} %pad_add_fusion.refs_0_, bf16[528,1024]{1,0:T(8,128)(2,1)} %get-tuple-element.37.refs_1_, bf16[528,1024]{1,0:T(8,128)(2,1)} %get-tuple-element.35.refs_2_, bf16[528,1024]{1,0:T(8,128)(2,1)} %collective-permute-done.refs_3_, ...), custom_call_target="tpu_custom_call" | custom-call | flops 6000000000 | bytes 16777216 | tf_op jit(solution)/shard_map/stage_6/pallas_call | solution.py:279
  89.9 0.0 copy-start.1
  89.9 1.1 collective-permute-done.4.refs_7_
  91.0 0.0 collective-permute-done.5.refs_8_
  91.0 0.0 collective-permute-done.10.refs_15_
  91.0 0.0 collective-permute-done.11.refs_16_
  91.0 17.4 %stage_8.1 = (f32[4,64,256]{2,1,0:T(8,128)}, f32[4,64,256]{2,1,0:T(8,128)}, f32[4,64,256]{2,1,0:T(8,128)}, f32[4,64,256]{2,1,0:T(8,128)}) custom-call(s32[2,16]{1,0:T(2,128)} %pad_add_fusion.refs_0_, bf16[528,1024]{1,0:T(8,128)(2,1)} %get-tuple-element.37.refs_1_, bf16[528,1024]{1,0:T(8,128)(2,1)} %get-tuple-element.35.refs_2_, ...), custom_call_target="tpu_custom_call" | custom-call | flops 6000000000 | bytes 16777216 | tf_op jit(solution)/shard_map/stage_8/pallas_call | solution.py:279
  108.4 1.0 collective-permute-start.12
  109.4 1.1 collective-permute-start.13
  110.5 1.6 %collective-permute-start.14 = (f32[4,64,256]{2,1,0:T(8,128)}, f32[4,64,256]{2,1,0:T(8,128)S(1)}, u32[]{:S(2)}, u32[]{:S(2)}) collective-permute-start(f32[4,64,256]{2,1,0:T(8,128)} %get-tuple-element.54), channel_id=1, source_target_pairs={{0,2},{1,3},{2,0},{3,1},{4,6},{5,7},{6,4},{7,5},{8,10},{9,11},{10,... | collective-permute-start | bytes 786440 | tf_op jit(solution)/shard_map/ppermute | solution.py:416
  112.1 4.3 %collective-permute-done.12.a_ref = f32[4,64,256]{2,1,0:T(8,128)S(1)} collective-permute-done((f32[4,64,256]{2,1,0:T(8,128)}, f32[4,64,256]{2,1,0:T(8,128)S(1)}, u32[]{:S(2)}, u32[]{:S(2)}) %collective-permute-start.12) | collective-permute-done | bytes 262176 | tf_op jit(solution)/shard_map/ppermute | solution.py:414
  116.4 5.0 %collective-permute-done.13.b_ref = f32[4,64,256]{2,1,0:T(8,128)S(1)} collective-permute-done((f32[4,64,256]{2,1,0:T(8,128)}, f32[4,64,256]{2,1,0:T(8,128)S(1)}, u32[]{:S(2)}, u32[]{:S(2)}) %collective-permute-start.13) | collective-permute-done | bytes 262176 | tf_op jit(solution)/shard_map/ppermute | solution.py:415
  121.5 0.0 collective-permute-done.14.c_ref
  121.5 0.0 copy-done.1
  121.5 0.0 copy-start
  121.5 0.9 copy-done
  122.4 0.5 finish.1
  122.9 0.0 collective-permute-start.15
  122.9 1.2 collective-permute-done.15
  124.1 3.5 %collective-permute-start.16 = (f32[32,128]{1,0:T(8,128)S(1)}, f32[32,128]{1,0:T(8,128)S(1)}, u32[]{:S(2)}, u32[]{:S(2)}) collective-permute-start(f32[32,128]{1,0:T(8,128)S(1)} %add.298), channel_id=1, source_target_pairs={{0,32},{16,48},{32,0},{48,16},{64,96},{80,112},{96,64},{112,80},{1... | collective-permute-start | bytes 49160 | tf_op jit(solution)/shard_map/ppermute | solution.py:426
  127.7 1.7 %collective-permute-done.16 = f32[32,128]{1,0:T(8,128)S(1)} collective-permute-done((f32[32,128]{1,0:T(8,128)S(1)}, f32[32,128]{1,0:T(8,128)S(1)}, u32[]{:S(2)}, u32[]{:S(2)}) %collective-permute-start.16) | collective-permute-done | bytes 16416 | tf_op jit(solution)/shard_map/ppermute | solution.py:426
  129.4 3.5 %collective-permute-start.17 = (f32[32,128]{1,0:T(8,128)S(1)}, f32[32,128]{1,0:T(8,128)S(1)}, u32[]{:S(2)}, u32[]{:S(2)}) collective-permute-start(f32[32,128]{1,0:T(8,128)S(1)} %add.299), channel_id=1, source_target_pairs={{0,64},{16,80},{32,96},{48,112},{64,0},{80,16},{96,32},{112,48},{1... | collective-permute-start | bytes 49160 | tf_op jit(solution)/shard_map/ppermute | solution.py:426
  132.9 1.7 %collective-permute-done.17 = f32[32,128]{1,0:T(8,128)S(1)} collective-permute-done((f32[32,128]{1,0:T(8,128)S(1)}, f32[32,128]{1,0:T(8,128)S(1)}, u32[]{:S(2)}, u32[]{:S(2)}) %collective-permute-start.17) | collective-permute-done | bytes 16416 | tf_op jit(solution)/shard_map/ppermute | solution.py:426
  134.6 0.0 collective-permute-start.18
  134.6 3.7 %collective-permute-done.18 = f32[32,128]{1,0:T(8,128)S(1)} collective-permute-done((f32[32,128]{1,0:T(8,128)S(1)}, f32[32,128]{1,0:T(8,128)S(1)}, u32[]{:S(2)}, u32[]{:S(2)}) %collective-permute-start.18) | collective-permute-done | bytes 16416 | tf_op jit(solution)/shard_map/ppermute | solution.py:426
  138.4 0.3 collective-permute-start.19
  138.7 5.0 %collective-permute-done.19 = f32[32,128]{1,0:T(8,128)S(1)} collective-permute-done((f32[32,128]{1,0:T(8,128)S(1)}, f32[32,128]{1,0:T(8,128)S(1)}, u32[]{:S(2)}, u32[]{:S(2)}) %collective-permute-start.19) | collective-permute-done | bytes 16416 | tf_op jit(solution)/shard_map/ppermute | solution.py:426
  143.6 0.1 collective-permute-start.20
  143.7 3.7 %collective-permute-done.20 = f32[32,128]{1,0:T(8,128)S(1)} collective-permute-done((f32[32,128]{1,0:T(8,128)S(1)}, f32[32,128]{1,0:T(8,128)S(1)}, u32[]{:S(2)}, u32[]{:S(2)}) %collective-permute-start.20) | collective-permute-done | bytes 16416 | tf_op jit(solution)/shard_map/ppermute | solution.py:426
  147.4 0.0 collective-permute-start.21
  147.4 5.2 %collective-permute-done.21.other_ref = f32[32,128]{1,0:T(8,128)S(1)} collective-permute-done((f32[32,128]{1,0:T(8,128)S(1)}, f32[32,128]{1,0:T(8,128)S(1)}, u32[]{:S(2)}, u32[]{:S(2)}) %collective-permute-start.21) | collective-permute-done | bytes 16416 | tf_op jit(solution)/shard_map/ppermute | solution.py:426
  152.6 3.0 %solve.1 = f32[4,64,256]{2,1,0:T(8,128)} custom-call(f32[32,128]{1,0:T(8,128)S(1)} %add.303.gram_ref, f32[32,128]{1,0:T(8,128)S(1)} %collective-permute-done.21.other_ref, f32[64,1024]{1,0:T(8,128)S(1)} %get-tuple-element.56.image_hbm), custom_call_target="tpu_custom_call" | custom-call | tf_op jit(solution)/shard_map/solve/pallas_call | solution.py:369
  (6 shorter events, 0.0 us)
Async XLA Ops:
  4.7 28.6 %collective-permute-start.6 = (bf16[560,1024]{1,0:T(8,128)(2,1)}, bf16[560,1024]{1,0:T(8,128)(2,1)S(1)}, u32[]{:S(2)}, u32[]{:S(2)}) collective-permute-start(bf16[560,1024]{1,0:T(8,128)(2,1)} %get-tuple-element.47.refs_5_.refs_7_.refs_9_), channel_id=1, source_target_pairs={{0,4},{1,5},{2,6},{3,7},{4,8},{5,9},{6,10},{7,11},{8,12},{9,13},{1... | collective-permute-start | bytes 3440648 | tf_op jit(solution)/shard_map/ppermute | solution.py:397
  6.4 27.2 %collective-permute-start.7 = (bf16[560,1024]{1,0:T(8,128)(2,1)}, bf16[560,1024]{1,0:T(8,128)(2,1)}, u32[]{:S(2)}, u32[]{:S(2)}) collective-permute-start(bf16[560,1024]{1,0:T(8,128)(2,1)} %get-tuple-element.45.refs_6_.refs_8_.refs_10_), channel_id=1, source_target_pairs={{0,12},{1,13},{2,14},{3,15},{4,0},{5,1},{6,2},{7,3},{8,4},{9,5},{1... | collective-permute-start | bytes 3440648 | tf_op jit(solution)/shard_map/ppermute | solution.py:398
  8.0 28.6 %collective-permute-start = (bf16[528,1024]{1,0:T(8,128)(2,1)}, bf16[528,1024]{1,0:T(8,128)(2,1)}, u32[]{:S(2)}, u32[]{:S(2)}) collective-permute-start(bf16[528,1024]{1,0:T(8,128)(2,1)} %get-tuple-element.37.refs_1_), channel_id=1, source_target_pairs={{0,1},{1,2},{2,3},{3,0},{4,5},{5,6},{6,7},{7,4},{8,9},{9,10},{10,1... | collective-permute-start | bytes 3244040 | tf_op jit(solution)/shard_map/ppermute | solution.py:397
  10.0 28.5 %collective-permute-start.1 = (bf16[528,1024]{1,0:T(8,128)(2,1)}, bf16[528,1024]{1,0:T(8,128)(2,1)}, u32[]{:S(2)}, u32[]{:S(2)}) collective-permute-start(bf16[528,1024]{1,0:T(8,128)(2,1)} %get-tuple-element.35.refs_2_), channel_id=1, source_target_pairs={{0,3},{1,0},{2,1},{3,2},{4,7},{5,4},{6,5},{7,6},{8,11},{9,8},{10,9... | collective-permute-start | bytes 3244040 | tf_op jit(solution)/shard_map/ppermute | solution.py:398
  33.3 35.7 %copy-start.2 = (bf16[560,1024]{1,0:T(8,128)(2,1)}, bf16[560,1024]{1,0:T(8,128)(2,1)S(1)}, u32[]{:S(2)}) copy-start(bf16[560,1024]{1,0:T(8,128)(2,1)S(1)} %collective-permute-done.6.refs_7_.refs_9_.refs_11_) | copy-start | bytes 3440644
  33.3 27.8 %collective-permute-start.8 = (bf16[560,1024]{1,0:T(8,128)(2,1)}, bf16[560,1024]{1,0:T(8,128)(2,1)S(1)}, u32[]{:S(2)}, u32[]{:S(2)}) collective-permute-start(bf16[560,1024]{1,0:T(8,128)(2,1)} %get-tuple-element.45.refs_6_.refs_8_.refs_10_), channel_id=1, source_target_pairs={{0,4},{1,5},{2,6},{3,7},{4,8},{5,9},{6,10},{7,11},{8,12},{9,13},{1... | collective-permute-start | bytes 3440648 | tf_op jit(solution)/shard_map/ppermute | solution.py:401
  33.6 27.5 %collective-permute-start.9 = (bf16[560,1024]{1,0:T(8,128)(2,1)}, bf16[560,1024]{1,0:T(8,128)(2,1)}, u32[]{:S(2)}, u32[]{:S(2)}) collective-permute-start(bf16[560,1024]{1,0:T(8,128)(2,1)} %get-tuple-element.47.refs_5_.refs_7_.refs_9_), channel_id=1, source_target_pairs={{0,12},{1,13},{2,14},{3,15},{4,0},{5,1},{6,2},{7,3},{8,4},{9,5},{1... | collective-permute-start | bytes 3440648 | tf_op jit(solution)/shard_map/ppermute | solution.py:402
  36.6 28.4 %collective-permute-start.2 = (bf16[528,1024]{1,0:T(8,128)(2,1)}, bf16[528,1024]{1,0:T(8,128)(2,1)}, u32[]{:S(2)}, u32[]{:S(2)}) collective-permute-start(bf16[528,1024]{1,0:T(8,128)(2,1)} %get-tuple-element.35.refs_2_), channel_id=1, source_target_pairs={{0,1},{1,2},{2,3},{3,0},{4,5},{5,6},{6,7},{7,4},{8,9},{9,10},{10,1... | collective-permute-start | bytes 3244040 | tf_op jit(solution)/shard_map/ppermute | solution.py:401
  38.5 28.2 %collective-permute-start.3 = (bf16[528,1024]{1,0:T(8,128)(2,1)}, bf16[528,1024]{1,0:T(8,128)(2,1)}, u32[]{:S(2)}, u32[]{:S(2)}) collective-permute-start(bf16[528,1024]{1,0:T(8,128)(2,1)} %get-tuple-element.37.refs_1_), channel_id=1, source_target_pairs={{0,3},{1,0},{2,1},{3,2},{4,7},{5,4},{6,5},{7,6},{8,11},{9,8},{10,9... | collective-permute-start | bytes 3244040 | tf_op jit(solution)/shard_map/ppermute | solution.py:402
  61.1 3.8 %copy-start.3 = (bf16[560,1024]{1,0:T(8,128)(2,1)}, bf16[560,1024]{1,0:T(8,128)(2,1)S(1)}, u32[]{:S(2)}) copy-start(bf16[560,1024]{1,0:T(8,128)(2,1)S(1)} %collective-permute-done.8.refs_11_.refs_13_) | copy-start | bytes 3440644
  61.1 29.9 %collective-permute-start.10 = (bf16[560,1024]{1,0:T(8,128)(2,1)S(1)}, bf16[560,1024]{1,0:T(8,128)(2,1)}, u32[]{:S(2)}, u32[]{:S(2)}) collective-permute-start(bf16[560,1024]{1,0:T(8,128)(2,1)S(1)} %collective-permute-done.6.refs_7_.refs_9_.refs_11_), channel_id=1, source_target_pairs={{0,4},{1,5},{2,6},{3,7},{4,8},{5,9},{6,10},{7,11},{8,12},{9,13},{1... | collective-permute-start | bytes 3440648 | tf_op jit(solution)/shard_map/ppermute | solution.py:405
  61.2 29.9 %collective-permute-start.11 = (bf16[560,1024]{1,0:T(8,128)(2,1)}, bf16[560,1024]{1,0:T(8,128)(2,1)}, u32[]{:S(2)}, u32[]{:S(2)}) collective-permute-start(bf16[560,1024]{1,0:T(8,128)(2,1)} %collective-permute-done.7.refs_8_.refs_10_.refs_12_), channel_id=1, source_target_pairs={{0,12},{1,13},{2,14},{3,15},{4,0},{5,1},{6,2},{7,3},{8,4},{9,5},{1... | collective-permute-start | bytes 3440648 | tf_op jit(solution)/shard_map/ppermute | solution.py:406
  65.0 26.0 %collective-permute-start.4 = (bf16[528,1024]{1,0:T(8,128)(2,1)}, bf16[528,1024]{1,0:T(8,128)(2,1)}, u32[]{:S(2)}, u32[]{:S(2)}) collective-permute-start(bf16[528,1024]{1,0:T(8,128)(2,1)} %collective-permute-done.refs_3_), channel_id=1, source_target_pairs={{0,1},{1,2},{2,3},{3,0},{4,5},{5,6},{6,7},{7,4},{8,9},{9,10},{10,1... | collective-permute-start | bytes 3244040 | tf_op jit(solution)/shard_map/ppermute | solution.py:405
  66.7 24.3 %collective-permute-start.5 = (bf16[528,1024]{1,0:T(8,128)(2,1)}, bf16[528,1024]{1,0:T(8,128)(2,1)}, u32[]{:S(2)}, u32[]{:S(2)}) collective-permute-start(bf16[528,1024]{1,0:T(8,128)(2,1)} %collective-permute-done.1.refs_4_), channel_id=1, source_target_pairs={{0,3},{1,0},{2,1},{3,2},{4,7},{5,4},{6,5},{7,6},{8,11},{9,8},{10,9... | collective-permute-start | bytes 3244040 | tf_op jit(solution)/shard_map/ppermute | solution.py:406
  89.9 31.5 %copy-start.1 = (f32[4,256]{1,0:T(4,128)S(1)}, f32[4,256]{1,0:T(4,128)}, u32[]{:S(2)}) copy-start(f32[4,256]{1,0:T(4,128)} %deg_ref.1) | copy-start | bytes 12292
  108.4 8.0 %collective-permute-start.12 = (f32[4,64,256]{2,1,0:T(8,128)}, f32[4,64,256]{2,1,0:T(8,128)S(1)}, u32[]{:S(2)}, u32[]{:S(2)}) collective-permute-start(f32[4,64,256]{2,1,0:T(8,128)} %get-tuple-element.52), channel_id=1, source_target_pairs={{0,3},{1,0},{2,1},{3,2},{4,7},{5,4},{6,5},{7,6},{8,11},{9,8},{10,9... | collective-permute-start | bytes 786440 | tf_op jit(solution)/shard_map/ppermute | solution.py:414
  109.4 12.1 %collective-permute-start.13 = (f32[4,64,256]{2,1,0:T(8,128)}, f32[4,64,256]{2,1,0:T(8,128)S(1)}, u32[]{:S(2)}, u32[]{:S(2)}) collective-permute-start(f32[4,64,256]{2,1,0:T(8,128)} %get-tuple-element.53), channel_id=1, source_target_pairs={{0,1},{1,2},{2,3},{3,0},{4,5},{5,6},{6,7},{7,4},{8,9},{9,10},{10,1... | collective-permute-start | bytes 786440 | tf_op jit(solution)/shard_map/ppermute | solution.py:415
  110.5 11.0 %collective-permute-start.14 = (f32[4,64,256]{2,1,0:T(8,128)}, f32[4,64,256]{2,1,0:T(8,128)S(1)}, u32[]{:S(2)}, u32[]{:S(2)}) collective-permute-start(f32[4,64,256]{2,1,0:T(8,128)} %get-tuple-element.54), channel_id=1, source_target_pairs={{0,2},{1,3},{2,0},{3,1},{4,6},{5,7},{6,4},{7,5},{8,10},{9,11},{10,... | collective-permute-start | bytes 786440 | tf_op jit(solution)/shard_map/ppermute | solution.py:416
  121.5 1.0 copy-start
  122.9 1.2 collective-permute-start.15
  124.1 5.3 %collective-permute-start.16 = (f32[32,128]{1,0:T(8,128)S(1)}, f32[32,128]{1,0:T(8,128)S(1)}, u32[]{:S(2)}, u32[]{:S(2)}) collective-permute-start(f32[32,128]{1,0:T(8,128)S(1)} %add.298), channel_id=1, source_target_pairs={{0,32},{16,48},{32,0},{48,16},{64,96},{80,112},{96,64},{112,80},{1... | collective-permute-start | bytes 49160 | tf_op jit(solution)/shard_map/ppermute | solution.py:426
  129.4 5.3 %collective-permute-start.17 = (f32[32,128]{1,0:T(8,128)S(1)}, f32[32,128]{1,0:T(8,128)S(1)}, u32[]{:S(2)}, u32[]{:S(2)}) collective-permute-start(f32[32,128]{1,0:T(8,128)S(1)} %add.299), channel_id=1, source_target_pairs={{0,64},{16,80},{32,96},{48,112},{64,0},{80,16},{96,32},{112,48},{1... | collective-permute-start | bytes 49160 | tf_op jit(solution)/shard_map/ppermute | solution.py:426
  134.6 3.7 %collective-permute-start.18 = (f32[32,128]{1,0:T(8,128)S(1)}, f32[32,128]{1,0:T(8,128)S(1)}, u32[]{:S(2)}, u32[]{:S(2)}) collective-permute-start(f32[32,128]{1,0:T(8,128)S(1)} %add.300), channel_id=1, source_target_pairs={{0,1},{1,0},{2,3},{3,2},{4,5},{5,4},{6,7},{7,6},{8,9},{9,8},{10,11... | collective-permute-start | bytes 49160 | tf_op jit(solution)/shard_map/ppermute | solution.py:426
  138.4 5.2 %collective-permute-start.19 = (f32[32,128]{1,0:T(8,128)S(1)}, f32[32,128]{1,0:T(8,128)S(1)}, u32[]{:S(2)}, u32[]{:S(2)}) collective-permute-start(f32[32,128]{1,0:T(8,128)S(1)} %add.301), channel_id=1, source_target_pairs={{0,2},{1,3},{2,0},{3,1},{4,6},{5,7},{6,4},{7,5},{8,10},{9,11},{10,... | collective-permute-start | bytes 49160 | tf_op jit(solution)/shard_map/ppermute | solution.py:426
  143.6 3.7 %collective-permute-start.20 = (f32[32,128]{1,0:T(8,128)S(1)}, f32[32,128]{1,0:T(8,128)S(1)}, u32[]{:S(2)}, u32[]{:S(2)}) collective-permute-start(f32[32,128]{1,0:T(8,128)S(1)} %add.302), channel_id=1, source_target_pairs={{0,4},{1,5},{2,6},{3,7},{4,0},{5,1},{6,2},{7,3},{8,12},{9,13},{10,... | collective-permute-start | bytes 49160 | tf_op jit(solution)/shard_map/ppermute | solution.py:426
  147.4 5.2 %collective-permute-start.21 = (f32[32,128]{1,0:T(8,128)S(1)}, f32[32,128]{1,0:T(8,128)S(1)}, u32[]{:S(2)}, u32[]{:S(2)}) collective-permute-start(f32[32,128]{1,0:T(8,128)S(1)} %add.303.gram_ref), channel_id=1, source_target_pairs={{0,8},{1,9},{2,10},{3,11},{4,12},{5,13},{6,14},{7,15},{8,0},{9,1},... | collective-permute-start | bytes 49160 | tf_op jit(solution)/shard_map/ppermute | solution.py:426

commit v5 on v4

--- a/solution.py
+++ b/solution.py
@@ -22,7 +22,7 @@
 Z_ROWS = META + HALF
 Y_X = SCALED + META
 Y_ROWS = Y_X + HALF
-GROUPED = 4
+GROUPED = 8
 VMEM_LIMIT = 62 * 2**20
 SMALL_LIMIT = 16 * 2**20
 PANEL = 8
@@ -154,14 +154,19 @@
         c_copies.append(pltpu.make_async_copy(y_refs[u].at[pl.ds(Y_X, HALF)], c_x.at[u], sem_c.at[u]))
     if old:
         acc_copy = pltpu.make_async_copy(acc_in, acc, sem_a.at[2])
+    if old:
+        sweeps = [
+            ((0, old_slots, old_slots, slots), r_copies[old:] + c_copies[:old]),
+            ((old_slots, slots, 0, slots), c_copies[old:] + r_copies[:old]),
+        ]
+    else:
+        sweeps = [((0, slots, 0, slots), c_copies + r_copies)]
     for copy in meta_copies:
         copy.start()
-    for copy in r_copies[old:] + c_copies[:old] + pack_copies:
+    for copy in sweeps[0][1] + pack_copies:
         copy.start()
     if old:
         acc_copy.start()
-    for copy in c_copies[old:] + r_copies[:old]:
-        copy.start()
 
     for copy in meta_copies:
         copy.wait()
@@ -234,20 +239,18 @@
         lax.fori_loop(0, (count + GROUPED - 1) // GROUPED, step, 0)
 
     if old:
-        count = list_tiles(0, old_slots, old_slots, slots)
-        for copy in [acc_copy] + r_copies[old:] + c_copies[:old]:
-            copy.wait()
-        run_tiles(count)
-        count = list_tiles(old_slots, slots, 0, slots)
-        for copy in c_copies[old:] + r_copies[:old]:
-            copy.wait()
-        run_tiles(count)
+        acc_copy.wait()
     else:
         acc[...] = jnp.zeros_like(acc)
-        count = list_tiles(0, slots, 0, slots)
-        for copy in c_copies + r_copies:
+    for which, (span, loads) in enumerate(sweeps):
+        count = list_tiles(*span)
+        for copy in loads:
             copy.wait()
-        form([(s, s, None) for s in range(OWN)], True)
+        if which + 1 < len(sweeps):
+            for copy in sweeps[which + 1][1]:
+                copy.start()
+        if not old:
+            form([(s, s, None) for s in range(OWN)], True)
         run_tiles(count)
     if last:
         for out, order in zip(outs, ((0, 1, 2, 3), (4, 5, 8, 9), (10, 11, 6, 7), (12, 13, 14, 15))):

time: 157 us -> 153 us (0.975)
  Pallas kernels: 46.4 us -> 40.7 us
  starting transfers between devices: 33.2 us -> 37.2 us
  waiting for transfers between devices: 74.2 us -> 71 us
    pallas_call x3, Pallas kernels: 38.3 us -> 32.5 us  [stage(): pl.pallas_call(functools.partial(stage_kernel, old, new, last), out_shape...]
    ppermute x6, waiting for transfers between devices: 21 us -> 17.2 us  [per_device(): other = lax.ppermute(gram, axis, [(i, i ^ step) for i in range(size)])]
    ppermute x1, waiting for transfers between devices: 4.35 us -> 7.32 us  [per_device(): back_a = lax.ppermute(to_minus, 'blk', shift_z(-1))]
    ppermute x6, starting transfers between devices: 7.45 us -> 10.1 us  [per_device(): other = lax.ppermute(gram, axis, [(i, i ^ step) for i in range(size)])]
    ppermute x1, waiting for transfers between devices: 5.04 us -> 2.58 us  [per_device(): back_b = lax.ppermute(to_plus, 'blk', shift_z(1))]
    ppermute x1, starting transfers between devices: 1.01 us -> 3.09 us  [per_device(): back_a = lax.ppermute(to_minus, 'blk', shift_z(-1))]
  transfers between devices with their start and end apart: 22 -> 22, of which waited for: 12 -> 12; matrix products, arithmetic and copies ran while one was open for 0% -> 1% of each run, Pallas kernels for 13% -> 14%
where the time goes in v5:
time: 153 us; the launch traced here: 151 us
  waiting for transfers between devices  71 us (46%)
  Pallas kernels  40.7 us (27%)
  starting transfers between devices  37.2 us (24%)
    pallas_call x3, Pallas kernels, stage(): pl.pallas_call(functools.partial(stage_kernel, old, new, last), out_shape...  32.5 us
    ppermute x2, waiting for transfers between devices, gather(): minus_a = lax.ppermute(a, 'blk', shift(1))  21.2 us
    ppermute x2, waiting for transfers between devices, gather(): minus_b = lax.ppermute(b_next, 'blk', shift(1))  20.3 us
    ppermute x6, waiting for transfers between devices, per_device(): other = lax.ppermute(gram, axis, [(i, i ^ step) for i in range(size)])  17.2 us
    ppermute x6, starting transfers between devices, per_device(): other = lax.ppermute(gram, axis, [(i, i ^ step) for i in range(size)])  10.1 us
    ppermute x1, waiting for transfers between devices, per_device(): back_a = lax.ppermute(to_minus, 'blk', shift_z(-1))  7.32 us
    ppermute x2, starting transfers between devices, gather(): far_b = lax.ppermute(plus_next, 'blk', shift(-1))  5.54 us
    ppermute x2, starting transfers between devices, gather(): plus_a = lax.ppermute(a_next, 'blk', shift(-1))  5.13 us
  transfers between devices with their start and end apart: 22, of which 12 were waited for; matrix products, arithmetic and copies ran while one was open for 1% of the time, Pallas kernels for 14%

profile of v5, /device:TPU:0, one launch (start us, length us, event | category | flops | bytes accessed | tf_op | source)
XLA Modules:
  0.0 150.9 jit_solution(7658592114618511130)
XLA Ops:
  0.0 4.7 %prepare.1 = (bf16[528,1024]{1,0:T(8,128)(2,1)}, bf16[528,1024]{1,0:T(8,128)(2,1)}, bf16[560,1024]{1,0:T(8,128)(2,1)}, bf16[560,1024]{1,0:T(8,128)(2,1)}) custom-call(s32[4,16]{1,0:T(4,128)} %nbr_hbm.1, s32[4]{0:T(128)} %cnt_hbm.1, bf16[1024,1024]{1,0:T(8,128)(2,1)} %bitcast.37, f32[4,64,256]{2,1,0:T(8,128)} %bitcast.38, f32[4,256]{1,0:T(4,128)} %deg_ref.1), custom_call_target="tpu_custom_call" | custom-call | tf_op jit(solution)/shard_map/prepare/pallas_call | solution.py:110
  4.7 1.7 %collective-permute-start.6 = (bf16[560,1024]{1,0:T(8,128)(2,1)}, bf16[560,1024]{1,0:T(8,128)(2,1)S(1)}, u32[]{:S(2)}, u32[]{:S(2)}) collective-permute-start(bf16[560,1024]{1,0:T(8,128)(2,1)} %get-tuple-element.47.refs_5_.refs_7_.refs_9_), channel_id=1, source_target_pairs={{0,4},{1,5},{2,6},{3,7},{4,8},{5,9},{6,10},{7,11},{8,12},{9,13},{1... | collective-permute-start | bytes 3440648 | tf_op jit(solution)/shard_map/ppermute | solution.py:400
  6.4 1.6 %collective-permute-start.7 = (bf16[560,1024]{1,0:T(8,128)(2,1)}, bf16[560,1024]{1,0:T(8,128)(2,1)}, u32[]{:S(2)}, u32[]{:S(2)}) collective-permute-start(bf16[560,1024]{1,0:T(8,128)(2,1)} %get-tuple-element.45.refs_6_.refs_8_.refs_10_), channel_id=1, source_target_pairs={{0,12},{1,13},{2,14},{3,15},{4,0},{5,1},{6,2},{7,3},{8,4},{9,5},{1... | collective-permute-start | bytes 3440648 | tf_op jit(solution)/shard_map/ppermute | solution.py:401
  8.0 2.0 %collective-permute-start = (bf16[528,1024]{1,0:T(8,128)(2,1)}, bf16[528,1024]{1,0:T(8,128)(2,1)}, u32[]{:S(2)}, u32[]{:S(2)}) collective-permute-start(bf16[528,1024]{1,0:T(8,128)(2,1)} %get-tuple-element.37.refs_1_), channel_id=1, source_target_pairs={{0,1},{1,2},{2,3},{3,0},{4,5},{5,6},{6,7},{7,4},{8,9},{9,10},{10,1... | collective-permute-start | bytes 3244040 | tf_op jit(solution)/shard_map/ppermute | solution.py:400
  10.0 2.1 %collective-permute-start.1 = (bf16[528,1024]{1,0:T(8,128)(2,1)}, bf16[528,1024]{1,0:T(8,128)(2,1)}, u32[]{:S(2)}, u32[]{:S(2)}) collective-permute-start(bf16[528,1024]{1,0:T(8,128)(2,1)} %get-tuple-element.35.refs_2_), channel_id=1, source_target_pairs={{0,3},{1,0},{2,1},{3,2},{4,7},{5,4},{6,5},{7,6},{8,11},{9,8},{10,9... | collective-permute-start | bytes 3244040 | tf_op jit(solution)/shard_map/ppermute | solution.py:401
  12.1 21.2 %collective-permute-done.6.refs_7_.refs_9_.refs_11_ = bf16[560,1024]{1,0:T(8,128)(2,1)S(1)} collective-permute-done((bf16[560,1024]{1,0:T(8,128)(2,1)}, bf16[560,1024]{1,0:T(8,128)(2,1)S(1)}, u32[]{:S(2)}, u32[]{:S(2)}) %collective-permute-start.6) | collective-permute-done | bytes 1146912 | tf_op jit(solution)/shard_map/ppermute | solution.py:400
  33.3 0.0 copy-start.2
  33.3 0.3 collective-permute-start.8
  33.6 0.0 collective-permute-done.7.refs_8_.refs_10_.refs_12_
  33.6 2.9 %collective-permute-start.9 = (bf16[560,1024]{1,0:T(8,128)(2,1)}, bf16[560,1024]{1,0:T(8,128)(2,1)}, u32[]{:S(2)}, u32[]{:S(2)}) collective-permute-start(bf16[560,1024]{1,0:T(8,128)(2,1)} %get-tuple-element.47.refs_5_.refs_7_.refs_9_), channel_id=1, source_target_pairs={{0,12},{1,13},{2,14},{3,15},{4,0},{5,1},{6,2},{7,3},{8,4},{9,5},{1... | collective-permute-start | bytes 3440648 | tf_op jit(solution)/shard_map/ppermute | solution.py:405
  36.6 0.0 collective-permute-done.refs_3_
  36.6 1.9 %collective-permute-start.2 = (bf16[528,1024]{1,0:T(8,128)(2,1)}, bf16[528,1024]{1,0:T(8,128)(2,1)}, u32[]{:S(2)}, u32[]{:S(2)}) collective-permute-start(bf16[528,1024]{1,0:T(8,128)(2,1)} %get-tuple-element.35.refs_2_), channel_id=1, source_target_pairs={{0,1},{1,2},{2,3},{3,0},{4,5},{5,6},{6,7},{7,4},{8,9},{9,10},{10,1... | collective-permute-start | bytes 3244040 | tf_op jit(solution)/shard_map/ppermute | solution.py:404
  38.5 0.0 collective-permute-done.1.refs_4_
  38.5 2.2 %collective-permute-start.3 = (bf16[528,1024]{1,0:T(8,128)(2,1)}, bf16[528,1024]{1,0:T(8,128)(2,1)}, u32[]{:S(2)}, u32[]{:S(2)}) collective-permute-start(bf16[528,1024]{1,0:T(8,128)(2,1)} %get-tuple-element.37.refs_1_), channel_id=1, source_target_pairs={{0,3},{1,0},{2,1},{3,2},{4,7},{5,4},{6,5},{7,6},{8,11},{9,8},{10,9... | collective-permute-start | bytes 3244040 | tf_op jit(solution)/shard_map/ppermute | solution.py:405
  40.7 0.1 stack.127
  40.8 0.1 stack.145
  40.9 20.3 %collective-permute-done.8.refs_11_.refs_13_ = bf16[560,1024]{1,0:T(8,128)(2,1)S(1)} collective-permute-done((bf16[560,1024]{1,0:T(8,128)(2,1)}, bf16[560,1024]{1,0:T(8,128)(2,1)S(1)}, u32[]{:S(2)}, u32[]{:S(2)}) %collective-permute-start.8) | collective-permute-done | bytes 1146912 | tf_op jit(solution)/shard_map/ppermute | solution.py:404
  61.1 0.0 copy-start.3
  61.1 0.0 collective-permute-start.10
  61.1 0.0 collective-permute-done.9.refs_12_.refs_14_
  61.2 3.2 %collective-permute-start.11 = (bf16[560,1024]{1,0:T(8,128)(2,1)}, bf16[560,1024]{1,0:T(8,128)(2,1)}, u32[]{:S(2)}, u32[]{:S(2)}) collective-permute-start(bf16[560,1024]{1,0:T(8,128)(2,1)} %collective-permute-done.7.refs_8_.refs_10_.refs_12_), channel_id=1, source_target_pairs={{0,12},{1,13},{2,14},{3,15},{4,0},{5,1},{6,2},{7,3},{8,4},{9,5},{1... | collective-permute-start | bytes 3440648 | tf_op jit(solution)/shard_map/ppermute | solution.py:409
  64.4 0.6 pad_add_fusion.refs_0_
  65.0 0.0 copy-done.3
  65.0 0.0 collective-permute-done.2.refs_5_
  65.0 1.7 %collective-permute-start.4 = (bf16[528,1024]{1,0:T(8,128)(2,1)}, bf16[528,1024]{1,0:T(8,128)(2,1)}, u32[]{:S(2)}, u32[]{:S(2)}) collective-permute-start(bf16[528,1024]{1,0:T(8,128)(2,1)} %collective-permute-done.refs_3_), channel_id=1, source_target_pairs={{0,1},{1,2},{2,3},{3,0},{4,5},{5,6},{6,7},{7,4},{8,9},{9,10},{10,1... | collective-permute-start | bytes 3244040 | tf_op jit(solution)/shard_map/ppermute | solution.py:408
  66.7 0.0 collective-permute-done.3.refs_6_
  66.7 2.3 %collective-permute-start.5 = (bf16[528,1024]{1,0:T(8,128)(2,1)}, bf16[528,1024]{1,0:T(8,128)(2,1)}, u32[]{:S(2)}, u32[]{:S(2)}) collective-permute-start(bf16[528,1024]{1,0:T(8,128)(2,1)} %collective-permute-done.1.refs_4_), channel_id=1, source_target_pairs={{0,3},{1,0},{2,1},{3,2},{4,7},{5,4},{6,5},{7,6},{8,11},{9,8},{10,9... | collective-permute-start | bytes 3244040 | tf_op jit(solution)/shard_map/ppermute | solution.py:409
  69.0 0.0 copy-done.2
  69.0 8.9 %stage_4.1.refs_13_ = f32[16,64,256]{2,1,0:T(8,128)} custom-call(s32[2,16]{1,0:T(2,128)} %pad_add_fusion.refs_0_, bf16[528,1024]{1,0:T(8,128)(2,1)} %get-tuple-element.37.refs_1_, bf16[528,1024]{1,0:T(8,128)(2,1)} %get-tuple-element.35.refs_2_, bf16[528,1024]{1,0:T(8,128)(2,1)} %collective-permute-done.refs_3_, ...), custom_call_target="tpu_custom_call" | custom-call | flops 6000000000 | bytes 16777216 | tf_op jit(solution)/shard_map/stage_4/pallas_call | solution.py:282
  77.9 11.8 %stage_6.1.refs_17_ = f32[16,64,256]{2,1,0:T(8,128)} custom-call(s32[2,16]{1,0:T(2,128)} %pad_add_fusion.refs_0_, bf16[528,1024]{1,0:T(8,128)(2,1)} %get-tuple-element.37.refs_1_, bf16[528,1024]{1,0:T(8,128)(2,1)} %get-tuple-element.35.refs_2_, bf16[528,1024]{1,0:T(8,128)(2,1)} %collective-permute-done.refs_3_, ...), custom_call_target="tpu_custom_call" | custom-call | flops 6000000000 | bytes 16777216 | tf_op jit(solution)/shard_map/stage_6/pallas_call | solution.py:282
  89.7 0.0 copy-start.1
  89.7 1.3 collective-permute-done.4.refs_7_
  91.0 0.0 collective-permute-done.5.refs_8_
  91.0 0.0 collective-permute-done.10.refs_15_
  91.0 0.0 collective-permute-done.11.refs_16_
  91.0 11.8 %stage_8.1 = (f32[4,64,256]{2,1,0:T(8,128)}, f32[4,64,256]{2,1,0:T(8,128)}, f32[4,64,256]{2,1,0:T(8,128)}, f32[4,64,256]{2,1,0:T(8,128)}) custom-call(s32[2,16]{1,0:T(2,128)} %pad_add_fusion.refs_0_, bf16[528,1024]{1,0:T(8,128)(2,1)} %get-tuple-element.37.refs_1_, bf16[528,1024]{1,0:T(8,128)(2,1)} %get-tuple-element.35.refs_2_, ...), custom_call_target="tpu_custom_call" | custom-call | flops 6000000000 | bytes 16777216 | tf_op jit(solution)/shard_map/stage_8/pallas_call | solution.py:282
  102.9 3.1 %collective-permute-start.12 = (f32[4,64,256]{2,1,0:T(8,128)}, f32[4,64,256]{2,1,0:T(8,128)S(1)}, u32[]{:S(2)}, u32[]{:S(2)}) collective-permute-start(f32[4,64,256]{2,1,0:T(8,128)} %get-tuple-element.52), channel_id=1, source_target_pairs={{0,3},{1,0},{2,1},{3,2},{4,7},{5,4},{6,5},{7,6},{8,11},{9,8},{10,9... | collective-permute-start | bytes 786440 | tf_op jit(solution)/shard_map/ppermute | solution.py:417
  106.0 0.0 collective-permute-start.13
  106.0 1.9 %collective-permute-start.14 = (f32[4,64,256]{2,1,0:T(8,128)}, f32[4,64,256]{2,1,0:T(8,128)S(1)}, u32[]{:S(2)}, u32[]{:S(2)}) collective-permute-start(f32[4,64,256]{2,1,0:T(8,128)} %get-tuple-element.54), channel_id=1, source_target_pairs={{0,2},{1,3},{2,0},{3,1},{4,6},{5,7},{6,4},{7,5},{8,10},{9,11},{10,... | collective-permute-start | bytes 786440 | tf_op jit(solution)/shard_map/ppermute | solution.py:419
  107.9 7.3 %collective-permute-done.12.a_ref = f32[4,64,256]{2,1,0:T(8,128)S(1)} collective-permute-done((f32[4,64,256]{2,1,0:T(8,128)}, f32[4,64,256]{2,1,0:T(8,128)S(1)}, u32[]{:S(2)}, u32[]{:S(2)}) %collective-permute-start.12) | collective-permute-done | bytes 262176 | tf_op jit(solution)/shard_map/ppermute | solution.py:417
  115.2 2.6 %collective-permute-done.13.b_ref = f32[4,64,256]{2,1,0:T(8,128)S(1)} collective-permute-done((f32[4,64,256]{2,1,0:T(8,128)}, f32[4,64,256]{2,1,0:T(8,128)S(1)}, u32[]{:S(2)}, u32[]{:S(2)}) %collective-permute-start.13) | collective-permute-done | bytes 262176 | tf_op jit(solution)/shard_map/ppermute | solution.py:418
  117.8 0.0 collective-permute-done.14.c_ref
  117.8 0.0 copy-done.1
  117.8 0.0 copy-start
  117.8 0.9 copy-done
  118.7 0.5 finish.1
  119.2 0.0 collective-permute-start.15
  119.2 1.2 collective-permute-done.15
  120.4 1.8 %collective-permute-start.16 = (f32[32,128]{1,0:T(8,128)S(1)}, f32[32,128]{1,0:T(8,128)S(1)}, u32[]{:S(2)}, u32[]{:S(2)}) collective-permute-start(f32[32,128]{1,0:T(8,128)S(1)} %add.298), channel_id=1, source_target_pairs={{0,32},{16,48},{32,0},{48,16},{64,96},{80,112},{96,64},{112,80},{1... | collective-permute-start | bytes 49160 | tf_op jit(solution)/shard_map/ppermute | solution.py:429
  122.2 2.0 %collective-permute-done.16 = f32[32,128]{1,0:T(8,128)S(1)} collective-permute-done((f32[32,128]{1,0:T(8,128)S(1)}, f32[32,128]{1,0:T(8,128)S(1)}, u32[]{:S(2)}, u32[]{:S(2)}) %collective-permute-start.16) | collective-permute-done | bytes 16416 | tf_op jit(solution)/shard_map/ppermute | solution.py:429
  124.2 3.8 %collective-permute-start.17 = (f32[32,128]{1,0:T(8,128)S(1)}, f32[32,128]{1,0:T(8,128)S(1)}, u32[]{:S(2)}, u32[]{:S(2)}) collective-permute-start(f32[32,128]{1,0:T(8,128)S(1)} %add.299), channel_id=1, source_target_pairs={{0,64},{16,80},{32,96},{48,112},{64,0},{80,16},{96,32},{112,48},{1... | collective-permute-start | bytes 49160 | tf_op jit(solution)/shard_map/ppermute | solution.py:429
  128.0 1.7 %collective-permute-done.17 = f32[32,128]{1,0:T(8,128)S(1)} collective-permute-done((f32[32,128]{1,0:T(8,128)S(1)}, f32[32,128]{1,0:T(8,128)S(1)}, u32[]{:S(2)}, u32[]{:S(2)}) %collective-permute-start.17) | collective-permute-done | bytes 16416 | tf_op jit(solution)/shard_map/ppermute | solution.py:429
  129.7 0.0 collective-permute-start.18
  129.7 3.7 %collective-permute-done.18 = f32[32,128]{1,0:T(8,128)S(1)} collective-permute-done((f32[32,128]{1,0:T(8,128)S(1)}, f32[32,128]{1,0:T(8,128)S(1)}, u32[]{:S(2)}, u32[]{:S(2)}) %collective-permute-start.18) | collective-permute-done | bytes 16416 | tf_op jit(solution)/shard_map/ppermute | solution.py:429
  133.4 1.0 collective-permute-start.19
  134.4 4.3 %collective-permute-done.19 = f32[32,128]{1,0:T(8,128)S(1)} collective-permute-done((f32[32,128]{1,0:T(8,128)S(1)}, f32[32,128]{1,0:T(8,128)S(1)}, u32[]{:S(2)}, u32[]{:S(2)}) %collective-permute-start.19) | collective-permute-done | bytes 16416 | tf_op jit(solution)/shard_map/ppermute | solution.py:429
  138.7 2.1 %collective-permute-start.20 = (f32[32,128]{1,0:T(8,128)S(1)}, f32[32,128]{1,0:T(8,128)S(1)}, u32[]{:S(2)}, u32[]{:S(2)}) collective-permute-start(f32[32,128]{1,0:T(8,128)S(1)} %add.302), channel_id=1, source_target_pairs={{0,4},{1,5},{2,6},{3,7},{4,0},{5,1},{6,2},{7,3},{8,12},{9,13},{10,... | collective-permute-start | bytes 49160 | tf_op jit(solution)/shard_map/ppermute | solution.py:429
  140.8 1.7 %collective-permute-done.20 = f32[32,128]{1,0:T(8,128)S(1)} collective-permute-done((f32[32,128]{1,0:T(8,128)S(1)}, f32[32,128]{1,0:T(8,128)S(1)}, u32[]{:S(2)}, u32[]{:S(2)}) %collective-permute-start.20) | collective-permute-done | bytes 16416 | tf_op jit(solution)/shard_map/ppermute | solution.py:429
  142.5 1.5 collective-permute-start.21
  144.0 3.7 %collective-permute-done.21.other_ref = f32[32,128]{1,0:T(8,128)S(1)} collective-permute-done((f32[32,128]{1,0:T(8,128)S(1)}, f32[32,128]{1,0:T(8,128)S(1)}, u32[]{:S(2)}, u32[]{:S(2)}) %collective-permute-start.21) | collective-permute-done | bytes 16416 | tf_op jit(solution)/shard_map/ppermute | solution.py:429
  147.8 3.0 %solve.1 = f32[4,64,256]{2,1,0:T(8,128)} custom-call(f32[32,128]{1,0:T(8,128)S(1)} %add.303.gram_ref, f32[32,128]{1,0:T(8,128)S(1)} %collective-permute-done.21.other_ref, f32[64,1024]{1,0:T(8,128)S(1)} %get-tuple-element.56.image_hbm), custom_call_target="tpu_custom_call" | custom-call | tf_op jit(solution)/shard_map/solve/pallas_call | solution.py:372
  (6 shorter events, 0.0 us)
Async XLA Ops:
  4.7 28.6 %collective-permute-start.6 = (bf16[560,1024]{1,0:T(8,128)(2,1)}, bf16[560,1024]{1,0:T(8,128)(2,1)S(1)}, u32[]{:S(2)}, u32[]{:S(2)}) collective-permute-start(bf16[560,1024]{1,0:T(8,128)(2,1)} %get-tuple-element.47.refs_5_.refs_7_.refs_9_), channel_id=1, source_target_pairs={{0,4},{1,5},{2,6},{3,7},{4,8},{5,9},{6,10},{7,11},{8,12},{9,13},{1... | collective-permute-start | bytes 3440648 | tf_op jit(solution)/shard_map/ppermute | solution.py:400
  6.4 27.2 %collective-permute-start.7 = (bf16[560,1024]{1,0:T(8,128)(2,1)}, bf16[560,1024]{1,0:T(8,128)(2,1)}, u32[]{:S(2)}, u32[]{:S(2)}) collective-permute-start(bf16[560,1024]{1,0:T(8,128)(2,1)} %get-tuple-element.45.refs_6_.refs_8_.refs_10_), channel_id=1, source_target_pairs={{0,12},{1,13},{2,14},{3,15},{4,0},{5,1},{6,2},{7,3},{8,4},{9,5},{1... | collective-permute-start | bytes 3440648 | tf_op jit(solution)/shard_map/ppermute | solution.py:401
  8.0 28.6 %collective-permute-start = (bf16[528,1024]{1,0:T(8,128)(2,1)}, bf16[528,1024]{1,0:T(8,128)(2,1)}, u32[]{:S(2)}, u32[]{:S(2)}) collective-permute-start(bf16[528,1024]{1,0:T(8,128)(2,1)} %get-tuple-element.37.refs_1_), channel_id=1, source_target_pairs={{0,1},{1,2},{2,3},{3,0},{4,5},{5,6},{6,7},{7,4},{8,9},{9,10},{10,1... | collective-permute-start | bytes 3244040 | tf_op jit(solution)/shard_map/ppermute | solution.py:400
  10.0 28.5 %collective-permute-start.1 = (bf16[528,1024]{1,0:T(8,128)(2,1)}, bf16[528,1024]{1,0:T(8,128)(2,1)}, u32[]{:S(2)}, u32[]{:S(2)}) collective-permute-start(bf16[528,1024]{1,0:T(8,128)(2,1)} %get-tuple-element.35.refs_2_), channel_id=1, source_target_pairs={{0,3},{1,0},{2,1},{3,2},{4,7},{5,4},{6,5},{7,6},{8,11},{9,8},{10,9... | collective-permute-start | bytes 3244040 | tf_op jit(solution)/shard_map/ppermute | solution.py:401
  33.3 35.7 %copy-start.2 = (bf16[560,1024]{1,0:T(8,128)(2,1)}, bf16[560,1024]{1,0:T(8,128)(2,1)S(1)}, u32[]{:S(2)}) copy-start(bf16[560,1024]{1,0:T(8,128)(2,1)S(1)} %collective-permute-done.6.refs_7_.refs_9_.refs_11_) | copy-start | bytes 3440644
  33.3 27.8 %collective-permute-start.8 = (bf16[560,1024]{1,0:T(8,128)(2,1)}, bf16[560,1024]{1,0:T(8,128)(2,1)S(1)}, u32[]{:S(2)}, u32[]{:S(2)}) collective-permute-start(bf16[560,1024]{1,0:T(8,128)(2,1)} %get-tuple-element.45.refs_6_.refs_8_.refs_10_), channel_id=1, source_target_pairs={{0,4},{1,5},{2,6},{3,7},{4,8},{5,9},{6,10},{7,11},{8,12},{9,13},{1... | collective-permute-start | bytes 3440648 | tf_op jit(solution)/shard_map/ppermute | solution.py:404
  33.6 27.5 %collective-permute-start.9 = (bf16[560,1024]{1,0:T(8,128)(2,1)}, bf16[560,1024]{1,0:T(8,128)(2,1)}, u32[]{:S(2)}, u32[]{:S(2)}) collective-permute-start(bf16[560,1024]{1,0:T(8,128)(2,1)} %get-tuple-element.47.refs_5_.refs_7_.refs_9_), channel_id=1, source_target_pairs={{0,12},{1,13},{2,14},{3,15},{4,0},{5,1},{6,2},{7,3},{8,4},{9,5},{1... | collective-permute-start | bytes 3440648 | tf_op jit(solution)/shard_map/ppermute | solution.py:405
  36.6 28.4 %collective-permute-start.2 = (bf16[528,1024]{1,0:T(8,128)(2,1)}, bf16[528,1024]{1,0:T(8,128)(2,1)}, u32[]{:S(2)}, u32[]{:S(2)}) collective-permute-start(bf16[528,1024]{1,0:T(8,128)(2,1)} %get-tuple-element.35.refs_2_), channel_id=1, source_target_pairs={{0,1},{1,2},{2,3},{3,0},{4,5},{5,6},{6,7},{7,4},{8,9},{9,10},{10,1... | collective-permute-start | bytes 3244040 | tf_op jit(solution)/shard_map/ppermute | solution.py:404
  38.5 28.2 %collective-permute-start.3 = (bf16[528,1024]{1,0:T(8,128)(2,1)}, bf16[528,1024]{1,0:T(8,128)(2,1)}, u32[]{:S(2)}, u32[]{:S(2)}) collective-permute-start(bf16[528,1024]{1,0:T(8,128)(2,1)} %get-tuple-element.37.refs_1_), channel_id=1, source_target_pairs={{0,3},{1,0},{2,1},{3,2},{4,7},{5,4},{6,5},{7,6},{8,11},{9,8},{10,9... | collective-permute-start | bytes 3244040 | tf_op jit(solution)/shard_map/ppermute | solution.py:405
  61.1 3.8 %copy-start.3 = (bf16[560,1024]{1,0:T(8,128)(2,1)}, bf16[560,1024]{1,0:T(8,128)(2,1)S(1)}, u32[]{:S(2)}) copy-start(bf16[560,1024]{1,0:T(8,128)(2,1)S(1)} %collective-permute-done.8.refs_11_.refs_13_) | copy-start | bytes 3440644
  61.1 29.9 %collective-permute-start.10 = (bf16[560,1024]{1,0:T(8,128)(2,1)S(1)}, bf16[560,1024]{1,0:T(8,128)(2,1)}, u32[]{:S(2)}, u32[]{:S(2)}) collective-permute-start(bf16[560,1024]{1,0:T(8,128)(2,1)S(1)} %collective-permute-done.6.refs_7_.refs_9_.refs_11_), channel_id=1, source_target_pairs={{0,4},{1,5},{2,6},{3,7},{4,8},{5,9},{6,10},{7,11},{8,12},{9,13},{1... | collective-permute-start | bytes 3440648 | tf_op jit(solution)/shard_map/ppermute | solution.py:408
  61.2 29.9 %collective-permute-start.11 = (bf16[560,1024]{1,0:T(8,128)(2,1)}, bf16[560,1024]{1,0:T(8,128)(2,1)}, u32[]{:S(2)}, u32[]{:S(2)}) collective-permute-start(bf16[560,1024]{1,0:T(8,128)(2,1)} %collective-permute-done.7.refs_8_.refs_10_.refs_12_), channel_id=1, source_target_pairs={{0,12},{1,13},{2,14},{3,15},{4,0},{5,1},{6,2},{7,3},{8,4},{9,5},{1... | collective-permute-start | bytes 3440648 | tf_op jit(solution)/shard_map/ppermute | solution.py:409
  65.0 26.0 %collective-permute-start.4 = (bf16[528,1024]{1,0:T(8,128)(2,1)}, bf16[528,1024]{1,0:T(8,128)(2,1)}, u32[]{:S(2)}, u32[]{:S(2)}) collective-permute-start(bf16[528,1024]{1,0:T(8,128)(2,1)} %collective-permute-done.refs_3_), channel_id=1, source_target_pairs={{0,1},{1,2},{2,3},{3,0},{4,5},{5,6},{6,7},{7,4},{8,9},{9,10},{10,1... | collective-permute-start | bytes 3244040 | tf_op jit(solution)/shard_map/ppermute | solution.py:408
  66.7 24.3 %collective-permute-start.5 = (bf16[528,1024]{1,0:T(8,128)(2,1)}, bf16[528,1024]{1,0:T(8,128)(2,1)}, u32[]{:S(2)}, u32[]{:S(2)}) collective-permute-start(bf16[528,1024]{1,0:T(8,128)(2,1)} %collective-permute-done.1.refs_4_), channel_id=1, source_target_pairs={{0,3},{1,0},{2,1},{3,2},{4,7},{5,4},{6,5},{7,6},{8,11},{9,8},{10,9... | collective-permute-start | bytes 3244040 | tf_op jit(solution)/shard_map/ppermute | solution.py:409
  89.7 28.1 %copy-start.1 = (f32[4,256]{1,0:T(4,128)S(1)}, f32[4,256]{1,0:T(4,128)}, u32[]{:S(2)}) copy-start(f32[4,256]{1,0:T(4,128)} %deg_ref.1) | copy-start | bytes 12292
  102.9 12.3 %collective-permute-start.12 = (f32[4,64,256]{2,1,0:T(8,128)}, f32[4,64,256]{2,1,0:T(8,128)S(1)}, u32[]{:S(2)}, u32[]{:S(2)}) collective-permute-start(f32[4,64,256]{2,1,0:T(8,128)} %get-tuple-element.52), channel_id=1, source_target_pairs={{0,3},{1,0},{2,1},{3,2},{4,7},{5,4},{6,5},{7,6},{8,11},{9,8},{10,9... | collective-permute-start | bytes 786440 | tf_op jit(solution)/shard_map/ppermute | solution.py:417
  106.0 11.8 %collective-permute-start.13 = (f32[4,64,256]{2,1,0:T(8,128)}, f32[4,64,256]{2,1,0:T(8,128)S(1)}, u32[]{:S(2)}, u32[]{:S(2)}) collective-permute-start(f32[4,64,256]{2,1,0:T(8,128)} %get-tuple-element.53), channel_id=1, source_target_pairs={{0,1},{1,2},{2,3},{3,0},{4,5},{5,6},{6,7},{7,4},{8,9},{9,10},{10,1... | collective-permute-start | bytes 786440 | tf_op jit(solution)/shard_map/ppermute | solution.py:418
  106.0 11.8 %collective-permute-start.14 = (f32[4,64,256]{2,1,0:T(8,128)}, f32[4,64,256]{2,1,0:T(8,128)S(1)}, u32[]{:S(2)}, u32[]{:S(2)}) collective-permute-start(f32[4,64,256]{2,1,0:T(8,128)} %get-tuple-element.54), channel_id=1, source_target_pairs={{0,2},{1,3},{2,0},{3,1},{4,6},{5,7},{6,4},{7,5},{8,10},{9,11},{10,... | collective-permute-start | bytes 786440 | tf_op jit(solution)/shard_map/ppermute | solution.py:419
  117.8 1.0 copy-start
  119.2 1.2 collective-permute-start.15
  120.4 3.7 %collective-permute-start.16 = (f32[32,128]{1,0:T(8,128)S(1)}, f32[32,128]{1,0:T(8,128)S(1)}, u32[]{:S(2)}, u32[]{:S(2)}) collective-permute-start(f32[32,128]{1,0:T(8,128)S(1)} %add.298), channel_id=1, source_target_pairs={{0,32},{16,48},{32,0},{48,16},{64,96},{80,112},{96,64},{112,80},{1... | collective-permute-start | bytes 49160 | tf_op jit(solution)/shard_map/ppermute | solution.py:429
  124.2 5.5 %collective-permute-start.17 = (f32[32,128]{1,0:T(8,128)S(1)}, f32[32,128]{1,0:T(8,128)S(1)}, u32[]{:S(2)}, u32[]{:S(2)}) collective-permute-start(f32[32,128]{1,0:T(8,128)S(1)} %add.299), channel_id=1, source_target_pairs={{0,64},{16,80},{32,96},{48,112},{64,0},{80,16},{96,32},{112,48},{1... | collective-permute-start | bytes 49160 | tf_op jit(solution)/shard_map/ppermute | solution.py:429
  129.7 3.7 %collective-permute-start.18 = (f32[32,128]{1,0:T(8,128)S(1)}, f32[32,128]{1,0:T(8,128)S(1)}, u32[]{:S(2)}, u32[]{:S(2)}) collective-permute-start(f32[32,128]{1,0:T(8,128)S(1)} %add.300), channel_id=1, source_target_pairs={{0,1},{1,0},{2,3},{3,2},{4,5},{5,4},{6,7},{7,6},{8,9},{9,8},{10,11... | collective-permute-start | bytes 49160 | tf_op jit(solution)/shard_map/ppermute | solution.py:429
  133.4 5.2 %collective-permute-start.19 = (f32[32,128]{1,0:T(8,128)S(1)}, f32[32,128]{1,0:T(8,128)S(1)}, u32[]{:S(2)}, u32[]{:S(2)}) collective-permute-start(f32[32,128]{1,0:T(8,128)S(1)} %add.301), channel_id=1, source_target_pairs={{0,2},{1,3},{2,0},{3,1},{4,6},{5,7},{6,4},{7,5},{8,10},{9,11},{10,... | collective-permute-start | bytes 49160 | tf_op jit(solution)/shard_map/ppermute | solution.py:429
  138.7 3.8 %collective-permute-start.20 = (f32[32,128]{1,0:T(8,128)S(1)}, f32[32,128]{1,0:T(8,128)S(1)}, u32[]{:S(2)}, u32[]{:S(2)}) collective-permute-start(f32[32,128]{1,0:T(8,128)S(1)} %add.302), channel_id=1, source_target_pairs={{0,4},{1,5},{2,6},{3,7},{4,0},{5,1},{6,2},{7,3},{8,12},{9,13},{10,... | collective-permute-start | bytes 49160 | tf_op jit(solution)/shard_map/ppermute | solution.py:429
  142.5 5.2 %collective-permute-start.21 = (f32[32,128]{1,0:T(8,128)S(1)}, f32[32,128]{1,0:T(8,128)S(1)}, u32[]{:S(2)}, u32[]{:S(2)}) collective-permute-start(f32[32,128]{1,0:T(8,128)S(1)} %add.303.gram_ref), channel_id=1, source_target_pairs={{0,8},{1,9},{2,10},{3,11},{4,12},{5,13},{6,14},{7,15},{8,0},{9,1},... | collective-permute-start | bytes 49160 | tf_op jit(solution)/shard_map/ppermute | solution.py:429

commit v6 on v5

--- a/solution.py
+++ b/solution.py
@@ -128,17 +128,16 @@
 
 
 def stage_kernel(old, new, last, *refs):
-    idx_ref = refs[0]
-    z_refs = refs[1:1 + new]
-    y_refs = refs[1 + new:1 + 2 * new]
-    rest = refs[1 + 2 * new:]
+    z_refs = refs[:new]
+    y_refs = refs[new:2 * new]
+    rest = refs[2 * new:]
     if old:
         acc_in, rest = rest[0], rest[1:]
     if last:
         outs, rest = rest[:4], rest[4:]
     else:
         acc_out, rest = rest[0], rest[1:]
-    (r_x, c_x, c_s, c_pack, meta_r, meta_c, sq_r, sq_c, col, adj_vmem, adj_r, adj_c, codes, edge_list, acc,
+    (r_x, c_x, c_s, c_pack, meta_r, meta_c, sq_r, sq_c, col, adj_vmem, adj_r, adj_c, idx_ref, codes, edge_list, acc,
      sem_r, sem_c, sem_s, sem_m, sem_n, sem_a) = rest
     old_slots, slots = UNIT * old, UNIT * new
 
@@ -167,6 +166,15 @@
         copy.start()
     if old:
         acc_copy.start()
+
+    position = lax.axis_index("blk")
+    y, z = lax.div(position, SIDE), lax.rem(position, SIDE)
+    for u in range(new):
+        offset, half = ARRIVAL[u]
+        for i in range(UNIT):
+            place = UNIT * half + i
+            idx_ref[0, u * UNIT + i] = (y * SIDE + lax.rem(z + offset + SIDE, SIDE)) * OWN + place
+            idx_ref[1, u * UNIT + i] = (lax.rem(y + offset + SIDE, SIDE) * SIDE + z) * OWN + place
 
     for copy in meta_copies:
         copy.wait()
@@ -260,13 +268,12 @@
         acc_out[...] = acc[...]
 
 
-def stage(old, new, index, z_parts, y_parts, acc=None):
-    smem = pl.BlockSpec(memory_space=pltpu.SMEM)
+def stage(old, new, z_parts, y_parts, acc=None):
     vmem = pl.BlockSpec(memory_space=pltpu.VMEM)
     hbm = pl.BlockSpec(memory_space=pltpu.HBM)
     last = new == UNITS
-    operands = [index, *z_parts[:new], *y_parts[:new]]
-    in_specs = [smem] + [hbm] * (2 * new)
+    operands = [*z_parts[:new], *y_parts[:new]]
+    in_specs = [hbm] * (2 * new)
     if old:
         operands.append(acc)
         in_specs.append(hbm)
@@ -297,6 +304,7 @@
             pltpu.VMEM((2, 16, 128), jnp.int32),
             pltpu.SMEM((16, 128), jnp.int32),
             pltpu.SMEM((16, 128), jnp.int32),
+            pltpu.SMEM((2, 16), jnp.int32),
             pltpu.SMEM((264,), jnp.int32),
             pltpu.SMEM((264,), jnp.int32),
             pltpu.VMEM((16, COLS, ROWS), jnp.float32),
@@ -388,12 +396,6 @@
 
 
 def per_device(embedding, subspace, degree, neighbours, counts):
-    position = lax.axis_index("blk")
-    y, z = position // SIDE, position % SIDE
-    row_ids = jnp.stack([(y * SIDE + (z + k) % SIDE) * OWN + UNIT * h + i for k, h in ARRIVAL for i in range(UNIT)])
-    col_ids = jnp.stack([((y + k) % SIDE * SIDE + z) * OWN + UNIT * h + i for k, h in ARRIVAL for i in range(UNIT)])
-    index = jnp.stack([row_ids, col_ids]).astype(jnp.int32)
-
     z_a, z_b, y_a, y_b = prepare(embedding, subspace, degree, neighbours, counts)
 
     def gather(a, b, shift):
@@ -411,9 +413,9 @@
 
     z_parts = gather(z_a, z_b, shift_z)
     y_parts = gather(y_a, y_b, shift_y)
-    acc = stage(0, 4, index, z_parts, y_parts)
-    acc = stage(4, 6, index, z_parts, y_parts, acc)
-    own, to_minus, to_plus, to_far = stage(6, 8, index, z_parts, y_parts, acc)
+    acc = stage(0, 4, z_parts, y_parts)
+    acc = stage(4, 6, z_parts, y_parts, acc)
+    own, to_minus, to_plus, to_far = stage(6, 8, z_parts, y_parts, acc)
     back_a = lax.ppermute(to_minus, "blk", shift_z(-1))
     back_b = lax.ppermute(to_plus, "blk", shift_z(1))
     back_c = lax.ppermute(to_far, "blk", shift_z(2))

time: 153 us -> 152 us (level)
  Pallas kernels: 40.7 us -> 38.5 us
  starting transfers between devices: 37.2 us -> 39 us
    ppermute x1, waiting for transfers between devices: 7.32 us -> 3.25 us  [per_device(): back_a = lax.ppermute(to_minus, 'blk', shift_z(-1))]
    ppermute x1, waiting for transfers between devices: 2.58 us -> 5.04 us  [per_device(): back_b = lax.ppermute(to_plus, 'blk', shift_z(1))]
    pallas_call x3, Pallas kernels: 32.5 us -> 30.4 us  [stage(): pl.pallas_call(functools.partial(stage_kernel, old, new, last), out_shape...]
  transfers between devices with their start and end apart: 22 -> 22, of which waited for: 12 -> 12; matrix products, arithmetic and copies ran while one was open for 1% -> 0% of each run, Pallas kernels for 14% -> 13%
where the time goes in v6:
time: 152 us; the launch traced here: 150 us
  waiting for transfers between devices  71.4 us (47%)
  starting transfers between devices  39 us (26%)
  Pallas kernels  38.5 us (25%)
    pallas_call x3, Pallas kernels, stage(): pl.pallas_call(functools.partial(stage_kernel, old, new, last), out_shape...  30.4 us
    ppermute x2, waiting for transfers between devices, gather(): minus_a = lax.ppermute(a, 'blk', shift(1))  21.2 us
    ppermute x2, waiting for transfers between devices, gather(): minus_b = lax.ppermute(b_next, 'blk', shift(1))  20.6 us
    ppermute x6, waiting for transfers between devices, per_device(): other = lax.ppermute(gram, axis, [(i, i ^ step) for i in range(size)])  17.5 us
    ppermute x6, starting transfers between devices, per_device(): other = lax.ppermute(gram, axis, [(i, i ^ step) for i in range(size)])  10.4 us
    ppermute x2, starting transfers between devices, gather(): far_b = lax.ppermute(plus_next, 'blk', shift(-1))  5.53 us
    ppermute x2, starting transfers between devices, gather(): plus_a = lax.ppermute(a_next, 'blk', shift(-1))  5.13 us
    ppermute x1, waiting for transfers between devices, per_device(): back_b = lax.ppermute(to_plus, 'blk', shift_z(1))  5.04 us
  transfers between devices with their start and end apart: 22, of which 12 were waited for; matrix products, arithmetic and copies ran while one was open for 0% of the time, Pallas kernels for 13%

profile of v6, /device:TPU:0, one launch (start us, length us, event | category | flops | bytes accessed | tf_op | source)
XLA Modules:
  0.0 150.1 jit_solution(13978117347594347161)
XLA Ops:
  0.0 4.6 %prepare.1 = (bf16[528,1024]{1,0:T(8,128)(2,1)}, bf16[528,1024]{1,0:T(8,128)(2,1)}, bf16[560,1024]{1,0:T(8,128)(2,1)}, bf16[560,1024]{1,0:T(8,128)(2,1)}) custom-call(s32[4,16]{1,0:T(4,128)} %nbr_hbm.1, s32[4]{0:T(128)} %cnt_hbm.1, bf16[1024,1024]{1,0:T(8,128)(2,1)} %bitcast.3, f32[4,64,256]{2,1,0:T(8,128)} %bitcast.4, f32[4,256]{1,0:T(4,128)} %deg_ref.1), custom_call_target="tpu_custom_call" | custom-call | tf_op jit(solution)/shard_map/prepare/pallas_call | solution.py:110
  4.6 1.7 %collective-permute-start.6 = (bf16[560,1024]{1,0:T(8,128)(2,1)}, bf16[560,1024]{1,0:T(8,128)(2,1)S(1)}, u32[]{:S(2)}, u32[]{:S(2)}) collective-permute-start(bf16[560,1024]{1,0:T(8,128)(2,1)} %get-tuple-element.47.refs_4_.refs_6_.refs_8_), channel_id=1, source_target_pairs={{0,4},{1,5},{2,6},{3,7},{4,8},{5,9},{6,10},{7,11},{8,12},{9,13},{1... | collective-permute-start | bytes 3440648 | tf_op jit(solution)/shard_map/ppermute | solution.py:402
  6.4 1.6 %collective-permute-start.7 = (bf16[560,1024]{1,0:T(8,128)(2,1)}, bf16[560,1024]{1,0:T(8,128)(2,1)}, u32[]{:S(2)}, u32[]{:S(2)}) collective-permute-start(bf16[560,1024]{1,0:T(8,128)(2,1)} %get-tuple-element.45.refs_5_.refs_7_.refs_9_), channel_id=1, source_target_pairs={{0,12},{1,13},{2,14},{3,15},{4,0},{5,1},{6,2},{7,3},{8,4},{9,5},{1... | collective-permute-start | bytes 3440648 | tf_op jit(solution)/shard_map/ppermute | solution.py:403
  8.0 2.0 %collective-permute-start = (bf16[528,1024]{1,0:T(8,128)(2,1)}, bf16[528,1024]{1,0:T(8,128)(2,1)}, u32[]{:S(2)}, u32[]{:S(2)}) collective-permute-start(bf16[528,1024]{1,0:T(8,128)(2,1)} %get-tuple-element.37.refs_0_), channel_id=1, source_target_pairs={{0,1},{1,2},{2,3},{3,0},{4,5},{5,6},{6,7},{7,4},{8,9},{9,10},{10,1... | collective-permute-start | bytes 3244040 | tf_op jit(solution)/shard_map/ppermute | solution.py:402
  10.0 2.1 %collective-permute-start.1 = (bf16[528,1024]{1,0:T(8,128)(2,1)}, bf16[528,1024]{1,0:T(8,128)(2,1)}, u32[]{:S(2)}, u32[]{:S(2)}) collective-permute-start(bf16[528,1024]{1,0:T(8,128)(2,1)} %get-tuple-element.35.refs_1_), channel_id=1, source_target_pairs={{0,3},{1,0},{2,1},{3,2},{4,7},{5,4},{6,5},{7,6},{8,11},{9,8},{10,9... | collective-permute-start | bytes 3244040 | tf_op jit(solution)/shard_map/ppermute | solution.py:403
  12.1 21.2 %collective-permute-done.6.refs_6_.refs_8_.refs_10_ = bf16[560,1024]{1,0:T(8,128)(2,1)S(1)} collective-permute-done((bf16[560,1024]{1,0:T(8,128)(2,1)}, bf16[560,1024]{1,0:T(8,128)(2,1)S(1)}, u32[]{:S(2)}, u32[]{:S(2)}) %collective-permute-start.6) | collective-permute-done | bytes 1146912 | tf_op jit(solution)/shard_map/ppermute | solution.py:402
  33.3 0.0 copy-start.2
  33.3 0.3 collective-permute-start.8
  33.6 0.0 collective-permute-done.7.refs_7_.refs_9_.refs_11_
  33.6 2.9 %collective-permute-start.9 = (bf16[560,1024]{1,0:T(8,128)(2,1)}, bf16[560,1024]{1,0:T(8,128)(2,1)}, u32[]{:S(2)}, u32[]{:S(2)}) collective-permute-start(bf16[560,1024]{1,0:T(8,128)(2,1)} %get-tuple-element.47.refs_4_.refs_6_.refs_8_), channel_id=1, source_target_pairs={{0,12},{1,13},{2,14},{3,15},{4,0},{5,1},{6,2},{7,3},{8,4},{9,5},{1... | collective-permute-start | bytes 3440648 | tf_op jit(solution)/shard_map/ppermute | solution.py:407
  36.5 0.0 collective-permute-done.refs_2_
  36.5 1.9 %collective-permute-start.2 = (bf16[528,1024]{1,0:T(8,128)(2,1)}, bf16[528,1024]{1,0:T(8,128)(2,1)}, u32[]{:S(2)}, u32[]{:S(2)}) collective-permute-start(bf16[528,1024]{1,0:T(8,128)(2,1)} %get-tuple-element.35.refs_1_), channel_id=1, source_target_pairs={{0,1},{1,2},{2,3},{3,0},{4,5},{5,6},{6,7},{7,4},{8,9},{9,10},{10,1... | collective-permute-start | bytes 3244040 | tf_op jit(solution)/shard_map/ppermute | solution.py:406
  38.5 0.0 collective-permute-done.1.refs_3_
  38.5 2.2 %collective-permute-start.3 = (bf16[528,1024]{1,0:T(8,128)(2,1)}, bf16[528,1024]{1,0:T(8,128)(2,1)}, u32[]{:S(2)}, u32[]{:S(2)}) collective-permute-start(bf16[528,1024]{1,0:T(8,128)(2,1)} %get-tuple-element.37.refs_0_), channel_id=1, source_target_pairs={{0,3},{1,0},{2,1},{3,2},{4,7},{5,4},{6,5},{7,6},{8,11},{9,8},{10,9... | collective-permute-start | bytes 3244040 | tf_op jit(solution)/shard_map/ppermute | solution.py:407
  40.6 20.6 %collective-permute-done.8.refs_10_.refs_12_ = bf16[560,1024]{1,0:T(8,128)(2,1)} collective-permute-done((bf16[560,1024]{1,0:T(8,128)(2,1)}, bf16[560,1024]{1,0:T(8,128)(2,1)}, u32[]{:S(2)}, u32[]{:S(2)}) %collective-permute-start.8) | collective-permute-done | bytes 1146912 | tf_op jit(solution)/shard_map/ppermute | solution.py:406
  61.2 0.0 collective-permute-start.10
  61.2 0.0 collective-permute-done.9.refs_11_.refs_13_
  61.2 3.2 %collective-permute-start.11 = (bf16[560,1024]{1,0:T(8,128)(2,1)}, bf16[560,1024]{1,0:T(8,128)(2,1)}, u32[]{:S(2)}, u32[]{:S(2)}) collective-permute-start(bf16[560,1024]{1,0:T(8,128)(2,1)} %collective-permute-done.7.refs_7_.refs_9_.refs_11_), channel_id=1, source_target_pairs={{0,12},{1,13},{2,14},{3,15},{4,0},{5,1},{6,2},{7,3},{8,4},{9,5},{1... | collective-permute-start | bytes 3440648 | tf_op jit(solution)/shard_map/ppermute | solution.py:411
  64.5 0.0 collective-permute-done.2.refs_4_
  64.5 1.7 %collective-permute-start.4 = (bf16[528,1024]{1,0:T(8,128)(2,1)}, bf16[528,1024]{1,0:T(8,128)(2,1)}, u32[]{:S(2)}, u32[]{:S(2)}) collective-permute-start(bf16[528,1024]{1,0:T(8,128)(2,1)} %collective-permute-done.refs_2_), channel_id=1, source_target_pairs={{0,1},{1,2},{2,3},{3,0},{4,5},{5,6},{6,7},{7,4},{8,9},{9,10},{10,1... | collective-permute-start | bytes 3244040 | tf_op jit(solution)/shard_map/ppermute | solution.py:410
  66.2 0.0 collective-permute-done.3.refs_5_
  66.2 2.3 %collective-permute-start.5 = (bf16[528,1024]{1,0:T(8,128)(2,1)}, bf16[528,1024]{1,0:T(8,128)(2,1)}, u32[]{:S(2)}, u32[]{:S(2)}) collective-permute-start(bf16[528,1024]{1,0:T(8,128)(2,1)} %collective-permute-done.1.refs_3_), channel_id=1, source_target_pairs={{0,3},{1,0},{2,1},{3,2},{4,7},{5,4},{6,5},{7,6},{8,11},{9,8},{10,9... | collective-permute-start | bytes 3244040 | tf_op jit(solution)/shard_map/ppermute | solution.py:411
  68.5 0.0 copy-done.2
  68.5 9.7 %stage_4.1.refs_12_ = f32[16,64,256]{2,1,0:T(8,128)} custom-call(bf16[528,1024]{1,0:T(8,128)(2,1)} %get-tuple-element.37.refs_0_, bf16[528,1024]{1,0:T(8,128)(2,1)} %get-tuple-element.35.refs_1_, bf16[528,1024]{1,0:T(8,128)(2,1)} %collective-permute-done.refs_2_, bf16[528,1024]{1,0:T(8,128)(2,1)} %collective-permute-done.1.refs_3_, ...), custom_call_target="tpu_custom_call" | custom-call | flops 6000000000 | bytes 16777216 | tf_op jit(solution)/shard_map/stage_4/pallas_call | solution.py:289
  78.2 9.6 %stage_6.1.refs_16_ = f32[16,64,256]{2,1,0:T(8,128)} custom-call(bf16[528,1024]{1,0:T(8,128)(2,1)} %get-tuple-element.37.refs_0_, bf16[528,1024]{1,0:T(8,128)(2,1)} %get-tuple-element.35.refs_1_, bf16[528,1024]{1,0:T(8,128)(2,1)} %collective-permute-done.refs_2_, bf16[528,1024]{1,0:T(8,128)(2,1)} %collective-permute-done.1.refs_3_, ...), custom_call_target="tpu_custom_call" | custom-call | flops 6000000000 | bytes 16777216 | tf_op jit(solution)/shard_map/stage_6/pallas_call | solution.py:289
  87.8 0.0 copy-start.1
  87.8 2.6 %collective-permute-done.4.refs_6_ = bf16[528,1024]{1,0:T(8,128)(2,1)} collective-permute-done((bf16[528,1024]{1,0:T(8,128)(2,1)}, bf16[528,1024]{1,0:T(8,128)(2,1)}, u32[]{:S(2)}, u32[]{:S(2)}) %collective-permute-start.4) | collective-permute-done | bytes 1081376 | tf_op jit(solution)/shard_map/ppermute | solution.py:410
  90.4 0.0 collective-permute-done.5.refs_7_
  90.4 0.0 collective-permute-done.10.refs_14_
  90.4 0.0 collective-permute-done.11.refs_15_
  90.4 11.1 %stage_8.1 = (f32[4,64,256]{2,1,0:T(8,128)}, f32[4,64,256]{2,1,0:T(8,128)}, f32[4,64,256]{2,1,0:T(8,128)}, f32[4,64,256]{2,1,0:T(8,128)}) custom-call(bf16[528,1024]{1,0:T(8,128)(2,1)} %get-tuple-element.37.refs_0_, bf16[528,1024]{1,0:T(8,128)(2,1)} %get-tuple-element.35.refs_1_, bf16[528,1024]{1,0:T(8,128)(2,1)} %collective-permute-done.refs_2_, ...), custom_call_target="tpu_custom_call" | custom-call | flops 6000000000 | bytes 16777216 | tf_op jit(solution)/shard_map/stage_8/pallas_call | solution.py:289
  101.6 3.1 %collective-permute-start.12 = (f32[4,64,256]{2,1,0:T(8,128)}, f32[4,64,256]{2,1,0:T(8,128)S(1)}, u32[]{:S(2)}, u32[]{:S(2)}) collective-permute-start(f32[4,64,256]{2,1,0:T(8,128)} %get-tuple-element.52), channel_id=1, source_target_pairs={{0,3},{1,0},{2,1},{3,2},{4,7},{5,4},{6,5},{7,6},{8,11},{9,8},{10,9... | collective-permute-start | bytes 786440 | tf_op jit(solution)/shard_map/ppermute | solution.py:419
  104.7 1.2 collective-permute-start.13
  105.8 2.2 %collective-permute-start.14 = (f32[4,64,256]{2,1,0:T(8,128)}, f32[4,64,256]{2,1,0:T(8,128)S(1)}, u32[]{:S(2)}, u32[]{:S(2)}) collective-permute-start(f32[4,64,256]{2,1,0:T(8,128)} %get-tuple-element.54), channel_id=1, source_target_pairs={{0,2},{1,3},{2,0},{3,1},{4,6},{5,7},{6,4},{7,5},{8,10},{9,11},{10,... | collective-permute-start | bytes 786440 | tf_op jit(solution)/shard_map/ppermute | solution.py:421
  108.1 3.3 %collective-permute-done.12.a_ref = f32[4,64,256]{2,1,0:T(8,128)S(1)} collective-permute-done((f32[4,64,256]{2,1,0:T(8,128)}, f32[4,64,256]{2,1,0:T(8,128)S(1)}, u32[]{:S(2)}, u32[]{:S(2)}) %collective-permute-start.12) | collective-permute-done | bytes 262176 | tf_op jit(solution)/shard_map/ppermute | solution.py:419
  111.3 5.0 %collective-permute-done.13.b_ref = f32[4,64,256]{2,1,0:T(8,128)S(1)} collective-permute-done((f32[4,64,256]{2,1,0:T(8,128)}, f32[4,64,256]{2,1,0:T(8,128)S(1)}, u32[]{:S(2)}, u32[]{:S(2)}) %collective-permute-start.13) | collective-permute-done | bytes 262176 | tf_op jit(solution)/shard_map/ppermute | solution.py:420
  116.4 0.0 collective-permute-done.14.c_ref
  116.4 0.0 copy-done.1
  116.4 0.0 copy-start
  116.4 0.9 copy-done
  117.3 0.5 finish.1
  117.8 0.0 collective-permute-start.15
  117.8 1.2 collective-permute-done.15
  119.0 2.1 %collective-permute-start.16 = (f32[32,128]{1,0:T(8,128)S(1)}, f32[32,128]{1,0:T(8,128)S(1)}, u32[]{:S(2)}, u32[]{:S(2)}) collective-permute-start(f32[32,128]{1,0:T(8,128)S(1)} %add.18), channel_id=1, source_target_pairs={{0,32},{16,48},{32,0},{48,16},{64,96},{80,112},{96,64},{112,80},{1... | collective-permute-start | bytes 49160 | tf_op jit(solution)/shard_map/ppermute | solution.py:431
  121.1 1.7 %collective-permute-done.16 = f32[32,128]{1,0:T(8,128)S(1)} collective-permute-done((f32[32,128]{1,0:T(8,128)S(1)}, f32[32,128]{1,0:T(8,128)S(1)}, u32[]{:S(2)}, u32[]{:S(2)}) %collective-permute-start.16) | collective-permute-done | bytes 16416 | tf_op jit(solution)/shard_map/ppermute | solution.py:431
  122.8 4.5 %collective-permute-start.17 = (f32[32,128]{1,0:T(8,128)S(1)}, f32[32,128]{1,0:T(8,128)S(1)}, u32[]{:S(2)}, u32[]{:S(2)}) collective-permute-start(f32[32,128]{1,0:T(8,128)S(1)} %add.19), channel_id=1, source_target_pairs={{0,64},{16,80},{32,96},{48,112},{64,0},{80,16},{96,32},{112,48},{1... | collective-permute-start | bytes 49160 | tf_op jit(solution)/shard_map/ppermute | solution.py:431
  127.2 1.7 %collective-permute-done.17 = f32[32,128]{1,0:T(8,128)S(1)} collective-permute-done((f32[32,128]{1,0:T(8,128)S(1)}, f32[32,128]{1,0:T(8,128)S(1)}, u32[]{:S(2)}, u32[]{:S(2)}) %collective-permute-start.17) | collective-permute-done | bytes 16416 | tf_op jit(solution)/shard_map/ppermute | solution.py:431
  129.0 0.0 collective-permute-start.18
  129.0 3.7 %collective-permute-done.18 = f32[32,128]{1,0:T(8,128)S(1)} collective-permute-done((f32[32,128]{1,0:T(8,128)S(1)}, f32[32,128]{1,0:T(8,128)S(1)}, u32[]{:S(2)}, u32[]{:S(2)}) %collective-permute-start.18) | collective-permute-done | bytes 16416 | tf_op jit(solution)/shard_map/ppermute | solution.py:431
  132.7 1.1 collective-permute-start.19
  133.8 4.2 %collective-permute-done.19 = f32[32,128]{1,0:T(8,128)S(1)} collective-permute-done((f32[32,128]{1,0:T(8,128)S(1)}, f32[32,128]{1,0:T(8,128)S(1)}, u32[]{:S(2)}, u32[]{:S(2)}) %collective-permute-start.19) | collective-permute-done | bytes 16416 | tf_op jit(solution)/shard_map/ppermute | solution.py:431
  138.0 0.0 collective-permute-start.20
  138.0 3.7 %collective-permute-done.20 = f32[32,128]{1,0:T(8,128)S(1)} collective-permute-done((f32[32,128]{1,0:T(8,128)S(1)}, f32[32,128]{1,0:T(8,128)S(1)}, u32[]{:S(2)}, u32[]{:S(2)}) %collective-permute-start.20) | collective-permute-done | bytes 16416 | tf_op jit(solution)/shard_map/ppermute | solution.py:431
  141.7 2.8 %collective-permute-start.21 = (f32[32,128]{1,0:T(8,128)S(1)}, f32[32,128]{1,0:T(8,128)S(1)}, u32[]{:S(2)}, u32[]{:S(2)}) collective-permute-start(f32[32,128]{1,0:T(8,128)S(1)} %add.23.gram_ref), channel_id=1, source_target_pairs={{0,8},{1,9},{2,10},{3,11},{4,12},{5,13},{6,14},{7,15},{8,0},{9,1},... | collective-permute-start | bytes 49160 | tf_op jit(solution)/shard_map/ppermute | solution.py:431
  144.5 2.5 %collective-permute-done.21.other_ref = f32[32,128]{1,0:T(8,128)S(1)} collective-permute-done((f32[32,128]{1,0:T(8,128)S(1)}, f32[32,128]{1,0:T(8,128)S(1)}, u32[]{:S(2)}, u32[]{:S(2)}) %collective-permute-start.21) | collective-permute-done | bytes 16416 | tf_op jit(solution)/shard_map/ppermute | solution.py:431
  146.9 3.0 %solve.1 = f32[4,64,256]{2,1,0:T(8,128)} custom-call(f32[32,128]{1,0:T(8,128)S(1)} %add.23.gram_ref, f32[32,128]{1,0:T(8,128)S(1)} %collective-permute-done.21.other_ref, f32[64,1024]{1,0:T(8,128)S(1)} %get-tuple-element.56.image_hbm), custom_call_target="tpu_custom_call" | custom-call | tf_op jit(solution)/shard_map/solve/pallas_call | solution.py:380
  (6 shorter events, 0.0 us)
Async XLA Ops:
  4.6 28.6 %collective-permute-start.6 = (bf16[560,1024]{1,0:T(8,128)(2,1)}, bf16[560,1024]{1,0:T(8,128)(2,1)S(1)}, u32[]{:S(2)}, u32[]{:S(2)}) collective-permute-start(bf16[560,1024]{1,0:T(8,128)(2,1)} %get-tuple-element.47.refs_4_.refs_6_.refs_8_), channel_id=1, source_target_pairs={{0,4},{1,5},{2,6},{3,7},{4,8},{5,9},{6,10},{7,11},{8,12},{9,13},{1... | collective-permute-start | bytes 3440648 | tf_op jit(solution)/shard_map/ppermute | solution.py:402
  6.4 27.2 %collective-permute-start.7 = (bf16[560,1024]{1,0:T(8,128)(2,1)}, bf16[560,1024]{1,0:T(8,128)(2,1)}, u32[]{:S(2)}, u32[]{:S(2)}) collective-permute-start(bf16[560,1024]{1,0:T(8,128)(2,1)} %get-tuple-element.45.refs_5_.refs_7_.refs_9_), channel_id=1, source_target_pairs={{0,12},{1,13},{2,14},{3,15},{4,0},{5,1},{6,2},{7,3},{8,4},{9,5},{1... | collective-permute-start | bytes 3440648 | tf_op jit(solution)/shard_map/ppermute | solution.py:403
  8.0 28.6 %collective-permute-start = (bf16[528,1024]{1,0:T(8,128)(2,1)}, bf16[528,1024]{1,0:T(8,128)(2,1)}, u32[]{:S(2)}, u32[]{:S(2)}) collective-permute-start(bf16[528,1024]{1,0:T(8,128)(2,1)} %get-tuple-element.37.refs_0_), channel_id=1, source_target_pairs={{0,1},{1,2},{2,3},{3,0},{4,5},{5,6},{6,7},{7,4},{8,9},{9,10},{10,1... | collective-permute-start | bytes 3244040 | tf_op jit(solution)/shard_map/ppermute | solution.py:402
  10.0 28.5 %collective-permute-start.1 = (bf16[528,1024]{1,0:T(8,128)(2,1)}, bf16[528,1024]{1,0:T(8,128)(2,1)}, u32[]{:S(2)}, u32[]{:S(2)}) collective-permute-start(bf16[528,1024]{1,0:T(8,128)(2,1)} %get-tuple-element.35.refs_1_), channel_id=1, source_target_pairs={{0,3},{1,0},{2,1},{3,2},{4,7},{5,4},{6,5},{7,6},{8,11},{9,8},{10,9... | collective-permute-start | bytes 3244040 | tf_op jit(solution)/shard_map/ppermute | solution.py:403
  33.3 35.2 %copy-start.2 = (bf16[560,1024]{1,0:T(8,128)(2,1)}, bf16[560,1024]{1,0:T(8,128)(2,1)S(1)}, u32[]{:S(2)}) copy-start(bf16[560,1024]{1,0:T(8,128)(2,1)S(1)} %collective-permute-done.6.refs_6_.refs_8_.refs_10_) | copy-start | bytes 3440644
  33.3 27.9 %collective-permute-start.8 = (bf16[560,1024]{1,0:T(8,128)(2,1)}, bf16[560,1024]{1,0:T(8,128)(2,1)}, u32[]{:S(2)}, u32[]{:S(2)}) collective-permute-start(bf16[560,1024]{1,0:T(8,128)(2,1)} %get-tuple-element.45.refs_5_.refs_7_.refs_9_), channel_id=1, source_target_pairs={{0,4},{1,5},{2,6},{3,7},{4,8},{5,9},{6,10},{7,11},{8,12},{9,13},{1... | collective-permute-start | bytes 3440648 | tf_op jit(solution)/shard_map/ppermute | solution.py:406
  33.6 27.6 %collective-permute-start.9 = (bf16[560,1024]{1,0:T(8,128)(2,1)}, bf16[560,1024]{1,0:T(8,128)(2,1)}, u32[]{:S(2)}, u32[]{:S(2)}) collective-permute-start(bf16[560,1024]{1,0:T(8,128)(2,1)} %get-tuple-element.47.refs_4_.refs_6_.refs_8_), channel_id=1, source_target_pairs={{0,12},{1,13},{2,14},{3,15},{4,0},{5,1},{6,2},{7,3},{8,4},{9,5},{1... | collective-permute-start | bytes 3440648 | tf_op jit(solution)/shard_map/ppermute | solution.py:407
  36.5 27.9 %collective-permute-start.2 = (bf16[528,1024]{1,0:T(8,128)(2,1)}, bf16[528,1024]{1,0:T(8,128)(2,1)}, u32[]{:S(2)}, u32[]{:S(2)}) collective-permute-start(bf16[528,1024]{1,0:T(8,128)(2,1)} %get-tuple-element.35.refs_1_), channel_id=1, source_target_pairs={{0,1},{1,2},{2,3},{3,0},{4,5},{5,6},{6,7},{7,4},{8,9},{9,10},{10,1... | collective-permute-start | bytes 3244040 | tf_op jit(solution)/shard_map/ppermute | solution.py:406
  38.5 27.7 %collective-permute-start.3 = (bf16[528,1024]{1,0:T(8,128)(2,1)}, bf16[528,1024]{1,0:T(8,128)(2,1)}, u32[]{:S(2)}, u32[]{:S(2)}) collective-permute-start(bf16[528,1024]{1,0:T(8,128)(2,1)} %get-tuple-element.37.refs_0_), channel_id=1, source_target_pairs={{0,3},{1,0},{2,1},{3,2},{4,7},{5,4},{6,5},{7,6},{8,11},{9,8},{10,9... | collective-permute-start | bytes 3244040 | tf_op jit(solution)/shard_map/ppermute | solution.py:407
  61.2 29.2 %collective-permute-start.10 = (bf16[560,1024]{1,0:T(8,128)(2,1)S(1)}, bf16[560,1024]{1,0:T(8,128)(2,1)}, u32[]{:S(2)}, u32[]{:S(2)}) collective-permute-start(bf16[560,1024]{1,0:T(8,128)(2,1)S(1)} %collective-permute-done.6.refs_6_.refs_8_.refs_10_), channel_id=1, source_target_pairs={{0,4},{1,5},{2,6},{3,7},{4,8},{5,9},{6,10},{7,11},{8,12},{9,13},{1... | collective-permute-start | bytes 3440648 | tf_op jit(solution)/shard_map/ppermute | solution.py:410
  61.2 29.2 %collective-permute-start.11 = (bf16[560,1024]{1,0:T(8,128)(2,1)}, bf16[560,1024]{1,0:T(8,128)(2,1)}, u32[]{:S(2)}, u32[]{:S(2)}) collective-permute-start(bf16[560,1024]{1,0:T(8,128)(2,1)} %collective-permute-done.7.refs_7_.refs_9_.refs_11_), channel_id=1, source_target_pairs={{0,12},{1,13},{2,14},{3,15},{4,0},{5,1},{6,2},{7,3},{8,4},{9,5},{1... | collective-permute-start | bytes 3440648 | tf_op jit(solution)/shard_map/ppermute | solution.py:411
  64.5 25.9 %collective-permute-start.4 = (bf16[528,1024]{1,0:T(8,128)(2,1)}, bf16[528,1024]{1,0:T(8,128)(2,1)}, u32[]{:S(2)}, u32[]{:S(2)}) collective-permute-start(bf16[528,1024]{1,0:T(8,128)(2,1)} %collective-permute-done.refs_2_), channel_id=1, source_target_pairs={{0,1},{1,2},{2,3},{3,0},{4,5},{5,6},{6,7},{7,4},{8,9},{9,10},{10,1... | collective-permute-start | bytes 3244040 | tf_op jit(solution)/shard_map/ppermute | solution.py:410
  66.2 24.2 %collective-permute-start.5 = (bf16[528,1024]{1,0:T(8,128)(2,1)}, bf16[528,1024]{1,0:T(8,128)(2,1)}, u32[]{:S(2)}, u32[]{:S(2)}) collective-permute-start(bf16[528,1024]{1,0:T(8,128)(2,1)} %collective-permute-done.1.refs_3_), channel_id=1, source_target_pairs={{0,3},{1,0},{2,1},{3,2},{4,7},{5,4},{6,5},{7,6},{8,11},{9,8},{10,9... | collective-permute-start | bytes 3244040 | tf_op jit(solution)/shard_map/ppermute | solution.py:411
  87.8 28.6 %copy-start.1 = (f32[4,256]{1,0:T(4,128)S(1)}, f32[4,256]{1,0:T(4,128)}, u32[]{:S(2)}) copy-start(f32[4,256]{1,0:T(4,128)} %deg_ref.1) | copy-start | bytes 12292
  101.6 9.7 %collective-permute-start.12 = (f32[4,64,256]{2,1,0:T(8,128)}, f32[4,64,256]{2,1,0:T(8,128)S(1)}, u32[]{:S(2)}, u32[]{:S(2)}) collective-permute-start(f32[4,64,256]{2,1,0:T(8,128)} %get-tuple-element.52), channel_id=1, source_target_pairs={{0,3},{1,0},{2,1},{3,2},{4,7},{5,4},{6,5},{7,6},{8,11},{9,8},{10,9... | collective-permute-start | bytes 786440 | tf_op jit(solution)/shard_map/ppermute | solution.py:419
  104.7 11.7 %collective-permute-start.13 = (f32[4,64,256]{2,1,0:T(8,128)}, f32[4,64,256]{2,1,0:T(8,128)S(1)}, u32[]{:S(2)}, u32[]{:S(2)}) collective-permute-start(f32[4,64,256]{2,1,0:T(8,128)} %get-tuple-element.53), channel_id=1, source_target_pairs={{0,1},{1,2},{2,3},{3,0},{4,5},{5,6},{6,7},{7,4},{8,9},{9,10},{10,1... | collective-permute-start | bytes 786440 | tf_op jit(solution)/shard_map/ppermute | solution.py:420
  105.8 10.5 %collective-permute-start.14 = (f32[4,64,256]{2,1,0:T(8,128)}, f32[4,64,256]{2,1,0:T(8,128)S(1)}, u32[]{:S(2)}, u32[]{:S(2)}) collective-permute-start(f32[4,64,256]{2,1,0:T(8,128)} %get-tuple-element.54), channel_id=1, source_target_pairs={{0,2},{1,3},{2,0},{3,1},{4,6},{5,7},{6,4},{7,5},{8,10},{9,11},{10,... | collective-permute-start | bytes 786440 | tf_op jit(solution)/shard_map/ppermute | solution.py:421
  116.4 1.0 copy-start
  117.8 1.2 collective-permute-start.15
  119.0 3.8 %collective-permute-start.16 = (f32[32,128]{1,0:T(8,128)S(1)}, f32[32,128]{1,0:T(8,128)S(1)}, u32[]{:S(2)}, u32[]{:S(2)}) collective-permute-start(f32[32,128]{1,0:T(8,128)S(1)} %add.18), channel_id=1, source_target_pairs={{0,32},{16,48},{32,0},{48,16},{64,96},{80,112},{96,64},{112,80},{1... | collective-permute-start | bytes 49160 | tf_op jit(solution)/shard_map/ppermute | solution.py:431
  122.8 6.2 %collective-permute-start.17 = (f32[32,128]{1,0:T(8,128)S(1)}, f32[32,128]{1,0:T(8,128)S(1)}, u32[]{:S(2)}, u32[]{:S(2)}) collective-permute-start(f32[32,128]{1,0:T(8,128)S(1)} %add.19), channel_id=1, source_target_pairs={{0,64},{16,80},{32,96},{48,112},{64,0},{80,16},{96,32},{112,48},{1... | collective-permute-start | bytes 49160 | tf_op jit(solution)/shard_map/ppermute | solution.py:431
  129.0 3.7 %collective-permute-start.18 = (f32[32,128]{1,0:T(8,128)S(1)}, f32[32,128]{1,0:T(8,128)S(1)}, u32[]{:S(2)}, u32[]{:S(2)}) collective-permute-start(f32[32,128]{1,0:T(8,128)S(1)} %add.20), channel_id=1, source_target_pairs={{0,1},{1,0},{2,3},{3,2},{4,5},{5,4},{6,7},{7,6},{8,9},{9,8},{10,11... | collective-permute-start | bytes 49160 | tf_op jit(solution)/shard_map/ppermute | solution.py:431
  132.7 5.2 %collective-permute-start.19 = (f32[32,128]{1,0:T(8,128)S(1)}, f32[32,128]{1,0:T(8,128)S(1)}, u32[]{:S(2)}, u32[]{:S(2)}) collective-permute-start(f32[32,128]{1,0:T(8,128)S(1)} %add.21), channel_id=1, source_target_pairs={{0,2},{1,3},{2,0},{3,1},{4,6},{5,7},{6,4},{7,5},{8,10},{9,11},{10,... | collective-permute-start | bytes 49160 | tf_op jit(solution)/shard_map/ppermute | solution.py:431
  138.0 3.7 %collective-permute-start.20 = (f32[32,128]{1,0:T(8,128)S(1)}, f32[32,128]{1,0:T(8,128)S(1)}, u32[]{:S(2)}, u32[]{:S(2)}) collective-permute-start(f32[32,128]{1,0:T(8,128)S(1)} %add.22), channel_id=1, source_target_pairs={{0,4},{1,5},{2,6},{3,7},{4,0},{5,1},{6,2},{7,3},{8,12},{9,13},{10,... | collective-permute-start | bytes 49160 | tf_op jit(solution)/shard_map/ppermute | solution.py:431
  141.7 5.2 %collective-permute-start.21 = (f32[32,128]{1,0:T(8,128)S(1)}, f32[32,128]{1,0:T(8,128)S(1)}, u32[]{:S(2)}, u32[]{:S(2)}) collective-permute-start(f32[32,128]{1,0:T(8,128)S(1)} %add.23.gram_ref), channel_id=1, source_target_pairs={{0,8},{1,9},{2,10},{3,11},{4,12},{5,13},{6,14},{7,15},{8,0},{9,1},... | collective-permute-start | bytes 49160 | tf_op jit(solution)/shard_map/ppermute | solution.py:431

commit v7 on v6

--- a/solution.py
+++ b/solution.py
@@ -25,7 +25,7 @@
 GROUPED = 8
 VMEM_LIMIT = 62 * 2**20
 SMALL_LIMIT = 16 * 2**20
-PANEL = 8
+PANEL = 16
 ARRIVAL = ((0, 0), (0, 1), (-1, 0), (1, 1), (-1, 1), (1, 0), (2, 0), (2, 1))
 LOG2E = 1.4426950408889634
 GAIN = 2.0 * LOG2E / (4.0 * math.sqrt(FEAT))

time: 152 us -> 151 us (level)
  Pallas kernels: 38.5 us -> 40.6 us
  waiting for transfers between devices: 71.4 us -> 69.7 us
    pallas_call x3, Pallas kernels: 30.4 us -> 32.8 us  [stage(): pl.pallas_call(functools.partial(stage_kernel, old, new, last), out_shape...]
    ppermute x2, waiting for transfers between devices: 2.59 us -> 0.26 us  [gather(): far_a = lax.ppermute(minus_next, 'blk', shift(1))]
  transfers between devices with their start and end apart: 22 -> 22, of which waited for: 12 -> 12; matrix products, arithmetic and copies ran while one was open for 0% -> 0% of each run, Pallas kernels for 13% -> 14%
where the time goes in v7:
time: 151 us; the launch traced here: 150 us
  waiting for transfers between devices  69.7 us (46%)
  Pallas kernels  40.6 us (27%)
  starting transfers between devices  38.4 us (25%)
    pallas_call x3, Pallas kernels, stage(): pl.pallas_call(functools.partial(stage_kernel, old, new, last), out_shape...  32.8 us
    ppermute x2, waiting for transfers between devices, gather(): minus_a = lax.ppermute(a, 'blk', shift(1))  21.2 us
    ppermute x2, waiting for transfers between devices, gather(): minus_b = lax.ppermute(b_next, 'blk', shift(1))  20.6 us
    ppermute x6, waiting for transfers between devices, per_device(): other = lax.ppermute(gram, axis, [(i, i ^ step) for i in range(size)])  18.2 us
    ppermute x6, starting transfers between devices, per_device(): other = lax.ppermute(gram, axis, [(i, i ^ step) for i in range(size)])  9.83 us
    ppermute x2, starting transfers between devices, gather(): far_b = lax.ppermute(plus_next, 'blk', shift(-1))  5.53 us
    ppermute x2, starting transfers between devices, gather(): plus_a = lax.ppermute(a_next, 'blk', shift(-1))  5.13 us
    ppermute x1, waiting for transfers between devices, per_device(): back_b = lax.ppermute(to_plus, 'blk', shift_z(1))  5.04 us
  transfers between devices with their start and end apart: 22, of which 12 were waited for; matrix products, arithmetic and copies ran while one was open for 0% of the time, Pallas kernels for 14%

profile of v7, /device:TPU:0, one launch (start us, length us, event | category | flops | bytes accessed | tf_op | source)
XLA Modules:
  0.0 149.9 jit_solution(8456845400630062265)
XLA Ops:
  0.0 4.6 %prepare.1 = (bf16[528,1024]{1,0:T(8,128)(2,1)}, bf16[528,1024]{1,0:T(8,128)(2,1)}, bf16[560,1024]{1,0:T(8,128)(2,1)}, bf16[560,1024]{1,0:T(8,128)(2,1)}) custom-call(s32[4,16]{1,0:T(4,128)} %nbr_hbm.1, s32[4]{0:T(128)} %cnt_hbm.1, bf16[1024,1024]{1,0:T(8,128)(2,1)} %bitcast.3, f32[4,64,256]{2,1,0:T(8,128)} %bitcast.4, f32[4,256]{1,0:T(4,128)} %deg_ref.1), custom_call_target="tpu_custom_call" | custom-call | tf_op jit(solution)/shard_map/prepare/pallas_call | solution.py:110
  4.6 1.7 %collective-permute-start.6 = (bf16[560,1024]{1,0:T(8,128)(2,1)}, bf16[560,1024]{1,0:T(8,128)(2,1)S(1)}, u32[]{:S(2)}, u32[]{:S(2)}) collective-permute-start(bf16[560,1024]{1,0:T(8,128)(2,1)} %get-tuple-element.47.refs_4_.refs_6_.refs_8_), channel_id=1, source_target_pairs={{0,4},{1,5},{2,6},{3,7},{4,8},{5,9},{6,10},{7,11},{8,12},{9,13},{1... | collective-permute-start | bytes 3440648 | tf_op jit(solution)/shard_map/ppermute | solution.py:402
  6.4 1.6 %collective-permute-start.7 = (bf16[560,1024]{1,0:T(8,128)(2,1)}, bf16[560,1024]{1,0:T(8,128)(2,1)}, u32[]{:S(2)}, u32[]{:S(2)}) collective-permute-start(bf16[560,1024]{1,0:T(8,128)(2,1)} %get-tuple-element.45.refs_5_.refs_7_.refs_9_), channel_id=1, source_target_pairs={{0,12},{1,13},{2,14},{3,15},{4,0},{5,1},{6,2},{7,3},{8,4},{9,5},{1... | collective-permute-start | bytes 3440648 | tf_op jit(solution)/shard_map/ppermute | solution.py:403
  8.0 2.0 %collective-permute-start = (bf16[528,1024]{1,0:T(8,128)(2,1)}, bf16[528,1024]{1,0:T(8,128)(2,1)}, u32[]{:S(2)}, u32[]{:S(2)}) collective-permute-start(bf16[528,1024]{1,0:T(8,128)(2,1)} %get-tuple-element.37.refs_0_), channel_id=1, source_target_pairs={{0,1},{1,2},{2,3},{3,0},{4,5},{5,6},{6,7},{7,4},{8,9},{9,10},{10,1... | collective-permute-start | bytes 3244040 | tf_op jit(solution)/shard_map/ppermute | solution.py:402
  10.0 2.1 %collective-permute-start.1 = (bf16[528,1024]{1,0:T(8,128)(2,1)}, bf16[528,1024]{1,0:T(8,128)(2,1)}, u32[]{:S(2)}, u32[]{:S(2)}) collective-permute-start(bf16[528,1024]{1,0:T(8,128)(2,1)} %get-tuple-element.35.refs_1_), channel_id=1, source_target_pairs={{0,3},{1,0},{2,1},{3,2},{4,7},{5,4},{6,5},{7,6},{8,11},{9,8},{10,9... | collective-permute-start | bytes 3244040 | tf_op jit(solution)/shard_map/ppermute | solution.py:403
  12.1 21.2 %collective-permute-done.6.refs_6_.refs_8_.refs_10_ = bf16[560,1024]{1,0:T(8,128)(2,1)S(1)} collective-permute-done((bf16[560,1024]{1,0:T(8,128)(2,1)}, bf16[560,1024]{1,0:T(8,128)(2,1)S(1)}, u32[]{:S(2)}, u32[]{:S(2)}) %collective-permute-start.6) | collective-permute-done | bytes 1146912 | tf_op jit(solution)/shard_map/ppermute | solution.py:402
  33.3 0.0 copy-start.2
  33.3 0.3 collective-permute-start.8
  33.6 0.0 collective-permute-done.7.refs_7_.refs_9_.refs_11_
  33.6 2.9 %collective-permute-start.9 = (bf16[560,1024]{1,0:T(8,128)(2,1)}, bf16[560,1024]{1,0:T(8,128)(2,1)}, u32[]{:S(2)}, u32[]{:S(2)}) collective-permute-start(bf16[560,1024]{1,0:T(8,128)(2,1)} %get-tuple-element.47.refs_4_.refs_6_.refs_8_), channel_id=1, source_target_pairs={{0,12},{1,13},{2,14},{3,15},{4,0},{5,1},{6,2},{7,3},{8,4},{9,5},{1... | collective-permute-start | bytes 3440648 | tf_op jit(solution)/shard_map/ppermute | solution.py:407
  36.5 0.0 collective-permute-done.refs_2_
  36.5 1.9 %collective-permute-start.2 = (bf16[528,1024]{1,0:T(8,128)(2,1)}, bf16[528,1024]{1,0:T(8,128)(2,1)}, u32[]{:S(2)}, u32[]{:S(2)}) collective-permute-start(bf16[528,1024]{1,0:T(8,128)(2,1)} %get-tuple-element.35.refs_1_), channel_id=1, source_target_pairs={{0,1},{1,2},{2,3},{3,0},{4,5},{5,6},{6,7},{7,4},{8,9},{9,10},{10,1... | collective-permute-start | bytes 3244040 | tf_op jit(solution)/shard_map/ppermute | solution.py:406
  38.5 0.0 collective-permute-done.1.refs_3_
  38.5 2.2 %collective-permute-start.3 = (bf16[528,1024]{1,0:T(8,128)(2,1)}, bf16[528,1024]{1,0:T(8,128)(2,1)}, u32[]{:S(2)}, u32[]{:S(2)}) collective-permute-start(bf16[528,1024]{1,0:T(8,128)(2,1)} %get-tuple-element.37.refs_0_), channel_id=1, source_target_pairs={{0,3},{1,0},{2,1},{3,2},{4,7},{5,4},{6,5},{7,6},{8,11},{9,8},{10,9... | collective-permute-start | bytes 3244040 | tf_op jit(solution)/shard_map/ppermute | solution.py:407
  40.6 20.6 %collective-permute-done.8.refs_10_.refs_12_ = bf16[560,1024]{1,0:T(8,128)(2,1)} collective-permute-done((bf16[560,1024]{1,0:T(8,128)(2,1)}, bf16[560,1024]{1,0:T(8,128)(2,1)}, u32[]{:S(2)}, u32[]{:S(2)}) %collective-permute-start.8) | collective-permute-done | bytes 1146912 | tf_op jit(solution)/shard_map/ppermute | solution.py:406
  61.2 0.0 collective-permute-start.10
  61.2 0.0 collective-permute-done.9.refs_11_.refs_13_
  61.2 3.2 %collective-permute-start.11 = (bf16[560,1024]{1,0:T(8,128)(2,1)}, bf16[560,1024]{1,0:T(8,128)(2,1)}, u32[]{:S(2)}, u32[]{:S(2)}) collective-permute-start(bf16[560,1024]{1,0:T(8,128)(2,1)} %collective-permute-done.7.refs_7_.refs_9_.refs_11_), channel_id=1, source_target_pairs={{0,12},{1,13},{2,14},{3,15},{4,0},{5,1},{6,2},{7,3},{8,4},{9,5},{1... | collective-permute-start | bytes 3440648 | tf_op jit(solution)/shard_map/ppermute | solution.py:411
  64.5 0.0 collective-permute-done.2.refs_4_
  64.5 1.7 %collective-permute-start.4 = (bf16[528,1024]{1,0:T(8,128)(2,1)}, bf16[528,1024]{1,0:T(8,128)(2,1)}, u32[]{:S(2)}, u32[]{:S(2)}) collective-permute-start(bf16[528,1024]{1,0:T(8,128)(2,1)} %collective-permute-done.refs_2_), channel_id=1, source_target_pairs={{0,1},{1,2},{2,3},{3,0},{4,5},{5,6},{6,7},{7,4},{8,9},{9,10},{10,1... | collective-permute-start | bytes 3244040 | tf_op jit(solution)/shard_map/ppermute | solution.py:410
  66.2 0.0 collective-permute-done.3.refs_5_
  66.2 2.3 %collective-permute-start.5 = (bf16[528,1024]{1,0:T(8,128)(2,1)}, bf16[528,1024]{1,0:T(8,128)(2,1)}, u32[]{:S(2)}, u32[]{:S(2)}) collective-permute-start(bf16[528,1024]{1,0:T(8,128)(2,1)} %collective-permute-done.1.refs_3_), channel_id=1, source_target_pairs={{0,3},{1,0},{2,1},{3,2},{4,7},{5,4},{6,5},{7,6},{8,11},{9,8},{10,9... | collective-permute-start | bytes 3244040 | tf_op jit(solution)/shard_map/ppermute | solution.py:411
  68.5 0.0 copy-done.2
  68.5 9.7 %stage_4.1.refs_12_ = f32[16,64,256]{2,1,0:T(8,128)} custom-call(bf16[528,1024]{1,0:T(8,128)(2,1)} %get-tuple-element.37.refs_0_, bf16[528,1024]{1,0:T(8,128)(2,1)} %get-tuple-element.35.refs_1_, bf16[528,1024]{1,0:T(8,128)(2,1)} %collective-permute-done.refs_2_, bf16[528,1024]{1,0:T(8,128)(2,1)} %collective-permute-done.1.refs_3_, ...), custom_call_target="tpu_custom_call" | custom-call | flops 6000000000 | bytes 16777216 | tf_op jit(solution)/shard_map/stage_4/pallas_call | solution.py:289
  78.2 11.9 %stage_6.1.refs_16_ = f32[16,64,256]{2,1,0:T(8,128)} custom-call(bf16[528,1024]{1,0:T(8,128)(2,1)} %get-tuple-element.37.refs_0_, bf16[528,1024]{1,0:T(8,128)(2,1)} %get-tuple-element.35.refs_1_, bf16[528,1024]{1,0:T(8,128)(2,1)} %collective-permute-done.refs_2_, bf16[528,1024]{1,0:T(8,128)(2,1)} %collective-permute-done.1.refs_3_, ...), custom_call_target="tpu_custom_call" | custom-call | flops 6000000000 | bytes 16777216 | tf_op jit(solution)/shard_map/stage_6/pallas_call | solution.py:289
  90.1 0.0 copy-start.1
  90.1 0.3 collective-permute-done.4.refs_6_
  90.4 0.0 collective-permute-done.5.refs_7_
  90.4 0.0 collective-permute-done.10.refs_14_
  90.4 0.0 collective-permute-done.11.refs_15_
  90.4 11.1 %stage_8.1 = (f32[4,64,256]{2,1,0:T(8,128)}, f32[4,64,256]{2,1,0:T(8,128)}, f32[4,64,256]{2,1,0:T(8,128)}, f32[4,64,256]{2,1,0:T(8,128)}) custom-call(bf16[528,1024]{1,0:T(8,128)(2,1)} %get-tuple-element.37.refs_0_, bf16[528,1024]{1,0:T(8,128)(2,1)} %get-tuple-element.35.refs_1_, bf16[528,1024]{1,0:T(8,128)(2,1)} %collective-permute-done.refs_2_, ...), custom_call_target="tpu_custom_call" | custom-call | flops 6000000000 | bytes 16777216 | tf_op jit(solution)/shard_map/stage_8/pallas_call | solution.py:289
  101.6 3.1 %collective-permute-start.12 = (f32[4,64,256]{2,1,0:T(8,128)}, f32[4,64,256]{2,1,0:T(8,128)S(1)}, u32[]{:S(2)}, u32[]{:S(2)}) collective-permute-start(f32[4,64,256]{2,1,0:T(8,128)} %get-tuple-element.52), channel_id=1, source_target_pairs={{0,3},{1,0},{2,1},{3,2},{4,7},{5,4},{6,5},{7,6},{8,11},{9,8},{10,9... | collective-permute-start | bytes 786440 | tf_op jit(solution)/shard_map/ppermute | solution.py:419
  104.7 1.2 collective-permute-start.13
  105.8 2.3 %collective-permute-start.14 = (f32[4,64,256]{2,1,0:T(8,128)}, f32[4,64,256]{2,1,0:T(8,128)S(1)}, u32[]{:S(2)}, u32[]{:S(2)}) collective-permute-start(f32[4,64,256]{2,1,0:T(8,128)} %get-tuple-element.54), channel_id=1, source_target_pairs={{0,2},{1,3},{2,0},{3,1},{4,6},{5,7},{6,4},{7,5},{8,10},{9,11},{10,... | collective-permute-start | bytes 786440 | tf_op jit(solution)/shard_map/ppermute | solution.py:421
  108.1 3.2 %collective-permute-done.12.a_ref = f32[4,64,256]{2,1,0:T(8,128)S(1)} collective-permute-done((f32[4,64,256]{2,1,0:T(8,128)}, f32[4,64,256]{2,1,0:T(8,128)S(1)}, u32[]{:S(2)}, u32[]{:S(2)}) %collective-permute-start.12) | collective-permute-done | bytes 262176 | tf_op jit(solution)/shard_map/ppermute | solution.py:419
  111.3 5.0 %collective-permute-done.13.b_ref = f32[4,64,256]{2,1,0:T(8,128)S(1)} collective-permute-done((f32[4,64,256]{2,1,0:T(8,128)}, f32[4,64,256]{2,1,0:T(8,128)S(1)}, u32[]{:S(2)}, u32[]{:S(2)}) %collective-permute-start.13) | collective-permute-done | bytes 262176 | tf_op jit(solution)/shard_map/ppermute | solution.py:420
  116.4 0.0 collective-permute-done.14.c_ref
  116.4 0.0 copy-done.1
  116.4 0.0 copy-start
  116.4 0.9 copy-done
  117.3 0.5 finish.1
  117.8 0.0 collective-permute-start.15
  117.8 1.2 collective-permute-done.15
  119.0 1.5 collective-permute-start.16
  120.5 2.2 %collective-permute-done.16 = f32[32,128]{1,0:T(8,128)S(1)} collective-permute-done((f32[32,128]{1,0:T(8,128)S(1)}, f32[32,128]{1,0:T(8,128)S(1)}, u32[]{:S(2)}, u32[]{:S(2)}) %collective-permute-start.16) | collective-permute-done | bytes 16416 | tf_op jit(solution)/shard_map/ppermute | solution.py:431
  122.7 4.5 %collective-permute-start.17 = (f32[32,128]{1,0:T(8,128)S(1)}, f32[32,128]{1,0:T(8,128)S(1)}, u32[]{:S(2)}, u32[]{:S(2)}) collective-permute-start(f32[32,128]{1,0:T(8,128)S(1)} %add.19), channel_id=1, source_target_pairs={{0,64},{16,80},{32,96},{48,112},{64,0},{80,16},{96,32},{112,48},{1... | collective-permute-start | bytes 49160 | tf_op jit(solution)/shard_map/ppermute | solution.py:431
  127.2 1.7 %collective-permute-done.17 = f32[32,128]{1,0:T(8,128)S(1)} collective-permute-done((f32[32,128]{1,0:T(8,128)S(1)}, f32[32,128]{1,0:T(8,128)S(1)}, u32[]{:S(2)}, u32[]{:S(2)}) %collective-permute-start.17) | collective-permute-done | bytes 16416 | tf_op jit(solution)/shard_map/ppermute | solution.py:431
  129.0 0.0 collective-permute-start.18
  129.0 3.7 %collective-permute-done.18 = f32[32,128]{1,0:T(8,128)S(1)} collective-permute-done((f32[32,128]{1,0:T(8,128)S(1)}, f32[32,128]{1,0:T(8,128)S(1)}, u32[]{:S(2)}, u32[]{:S(2)}) %collective-permute-start.18) | collective-permute-done | bytes 16416 | tf_op jit(solution)/shard_map/ppermute | solution.py:431
  132.7 0.6 collective-permute-start.19
  133.3 4.7 %collective-permute-done.19 = f32[32,128]{1,0:T(8,128)S(1)} collective-permute-done((f32[32,128]{1,0:T(8,128)S(1)}, f32[32,128]{1,0:T(8,128)S(1)}, u32[]{:S(2)}, u32[]{:S(2)}) %collective-permute-start.19) | collective-permute-done | bytes 16416 | tf_op jit(solution)/shard_map/ppermute | solution.py:431
  138.0 0.0 collective-permute-start.20
  138.0 3.8 %collective-permute-done.20 = f32[32,128]{1,0:T(8,128)S(1)} collective-permute-done((f32[32,128]{1,0:T(8,128)S(1)}, f32[32,128]{1,0:T(8,128)S(1)}, u32[]{:S(2)}, u32[]{:S(2)}) %collective-permute-start.20) | collective-permute-done | bytes 16416 | tf_op jit(solution)/shard_map/ppermute | solution.py:431
  141.8 3.2 %collective-permute-start.21 = (f32[32,128]{1,0:T(8,128)S(1)}, f32[32,128]{1,0:T(8,128)S(1)}, u32[]{:S(2)}, u32[]{:S(2)}) collective-permute-start(f32[32,128]{1,0:T(8,128)S(1)} %add.23.gram_ref), channel_id=1, source_target_pairs={{0,8},{1,9},{2,10},{3,11},{4,12},{5,13},{6,14},{7,15},{8,0},{9,1},... | collective-permute-start | bytes 49160 | tf_op jit(solution)/shard_map/ppermute | solution.py:431
  145.0 2.0 %collective-permute-done.21.other_ref = f32[32,128]{1,0:T(8,128)S(1)} collective-permute-done((f32[32,128]{1,0:T(8,128)S(1)}, f32[32,128]{1,0:T(8,128)S(1)}, u32[]{:S(2)}, u32[]{:S(2)}) %collective-permute-start.21) | collective-permute-done | bytes 16416 | tf_op jit(solution)/shard_map/ppermute | solution.py:431
  147.0 2.8 %solve.1 = f32[4,64,256]{2,1,0:T(8,128)} custom-call(f32[32,128]{1,0:T(8,128)S(1)} %add.23.gram_ref, f32[32,128]{1,0:T(8,128)S(1)} %collective-permute-done.21.other_ref, f32[64,1024]{1,0:T(8,128)S(1)} %get-tuple-element.56.image_hbm), custom_call_target="tpu_custom_call" | custom-call | tf_op jit(solution)/shard_map/solve/pallas_call | solution.py:380
  (6 shorter events, 0.0 us)
Async XLA Ops:
  4.6 28.6 %collective-permute-start.6 = (bf16[560,1024]{1,0:T(8,128)(2,1)}, bf16[560,1024]{1,0:T(8,128)(2,1)S(1)}, u32[]{:S(2)}, u32[]{:S(2)}) collective-permute-start(bf16[560,1024]{1,0:T(8,128)(2,1)} %get-tuple-element.47.refs_4_.refs_6_.refs_8_), channel_id=1, source_target_pairs={{0,4},{1,5},{2,6},{3,7},{4,8},{5,9},{6,10},{7,11},{8,12},{9,13},{1... | collective-permute-start | bytes 3440648 | tf_op jit(solution)/shard_map/ppermute | solution.py:402
  6.4 27.2 %collective-permute-start.7 = (bf16[560,1024]{1,0:T(8,128)(2,1)}, bf16[560,1024]{1,0:T(8,128)(2,1)}, u32[]{:S(2)}, u32[]{:S(2)}) collective-permute-start(bf16[560,1024]{1,0:T(8,128)(2,1)} %get-tuple-element.45.refs_5_.refs_7_.refs_9_), channel_id=1, source_target_pairs={{0,12},{1,13},{2,14},{3,15},{4,0},{5,1},{6,2},{7,3},{8,4},{9,5},{1... | collective-permute-start | bytes 3440648 | tf_op jit(solution)/shard_map/ppermute | solution.py:403
  8.0 28.6 %collective-permute-start = (bf16[528,1024]{1,0:T(8,128)(2,1)}, bf16[528,1024]{1,0:T(8,128)(2,1)}, u32[]{:S(2)}, u32[]{:S(2)}) collective-permute-start(bf16[528,1024]{1,0:T(8,128)(2,1)} %get-tuple-element.37.refs_0_), channel_id=1, source_target_pairs={{0,1},{1,2},{2,3},{3,0},{4,5},{5,6},{6,7},{7,4},{8,9},{9,10},{10,1... | collective-permute-start | bytes 3244040 | tf_op jit(solution)/shard_map/ppermute | solution.py:402
  10.0 28.5 %collective-permute-start.1 = (bf16[528,1024]{1,0:T(8,128)(2,1)}, bf16[528,1024]{1,0:T(8,128)(2,1)}, u32[]{:S(2)}, u32[]{:S(2)}) collective-permute-start(bf16[528,1024]{1,0:T(8,128)(2,1)} %get-tuple-element.35.refs_1_), channel_id=1, source_target_pairs={{0,3},{1,0},{2,1},{3,2},{4,7},{5,4},{6,5},{7,6},{8,11},{9,8},{10,9... | collective-permute-start | bytes 3244040 | tf_op jit(solution)/shard_map/ppermute | solution.py:403
  33.3 35.2 %copy-start.2 = (bf16[560,1024]{1,0:T(8,128)(2,1)}, bf16[560,1024]{1,0:T(8,128)(2,1)S(1)}, u32[]{:S(2)}) copy-start(bf16[560,1024]{1,0:T(8,128)(2,1)S(1)} %collective-permute-done.6.refs_6_.refs_8_.refs_10_) | copy-start | bytes 3440644
  33.3 27.9 %collective-permute-start.8 = (bf16[560,1024]{1,0:T(8,128)(2,1)}, bf16[560,1024]{1,0:T(8,128)(2,1)}, u32[]{:S(2)}, u32[]{:S(2)}) collective-permute-start(bf16[560,1024]{1,0:T(8,128)(2,1)} %get-tuple-element.45.refs_5_.refs_7_.refs_9_), channel_id=1, source_target_pairs={{0,4},{1,5},{2,6},{3,7},{4,8},{5,9},{6,10},{7,11},{8,12},{9,13},{1... | collective-permute-start | bytes 3440648 | tf_op jit(solution)/shard_map/ppermute | solution.py:406
  33.6 27.6 %collective-permute-start.9 = (bf16[560,1024]{1,0:T(8,128)(2,1)}, bf16[560,1024]{1,0:T(8,128)(2,1)}, u32[]{:S(2)}, u32[]{:S(2)}) collective-permute-start(bf16[560,1024]{1,0:T(8,128)(2,1)} %get-tuple-element.47.refs_4_.refs_6_.refs_8_), channel_id=1, source_target_pairs={{0,12},{1,13},{2,14},{3,15},{4,0},{5,1},{6,2},{7,3},{8,4},{9,5},{1... | collective-permute-start | bytes 3440648 | tf_op jit(solution)/shard_map/ppermute | solution.py:407
  36.5 27.9 %collective-permute-start.2 = (bf16[528,1024]{1,0:T(8,128)(2,1)}, bf16[528,1024]{1,0:T(8,128)(2,1)}, u32[]{:S(2)}, u32[]{:S(2)}) collective-permute-start(bf16[528,1024]{1,0:T(8,128)(2,1)} %get-tuple-element.35.refs_1_), channel_id=1, source_target_pairs={{0,1},{1,2},{2,3},{3,0},{4,5},{5,6},{6,7},{7,4},{8,9},{9,10},{10,1... | collective-permute-start | bytes 3244040 | tf_op jit(solution)/shard_map/ppermute | solution.py:406
  38.5 27.7 %collective-permute-start.3 = (bf16[528,1024]{1,0:T(8,128)(2,1)}, bf16[528,1024]{1,0:T(8,128)(2,1)}, u32[]{:S(2)}, u32[]{:S(2)}) collective-permute-start(bf16[528,1024]{1,0:T(8,128)(2,1)} %get-tuple-element.37.refs_0_), channel_id=1, source_target_pairs={{0,3},{1,0},{2,1},{3,2},{4,7},{5,4},{6,5},{7,6},{8,11},{9,8},{10,9... | collective-permute-start | bytes 3244040 | tf_op jit(solution)/shard_map/ppermute | solution.py:407
  61.2 29.2 %collective-permute-start.10 = (bf16[560,1024]{1,0:T(8,128)(2,1)S(1)}, bf16[560,1024]{1,0:T(8,128)(2,1)}, u32[]{:S(2)}, u32[]{:S(2)}) collective-permute-start(bf16[560,1024]{1,0:T(8,128)(2,1)S(1)} %collective-permute-done.6.refs_6_.refs_8_.refs_10_), channel_id=1, source_target_pairs={{0,4},{1,5},{2,6},{3,7},{4,8},{5,9},{6,10},{7,11},{8,12},{9,13},{1... | collective-permute-start | bytes 3440648 | tf_op jit(solution)/shard_map/ppermute | solution.py:410
  61.2 29.2 %collective-permute-start.11 = (bf16[560,1024]{1,0:T(8,128)(2,1)}, bf16[560,1024]{1,0:T(8,128)(2,1)}, u32[]{:S(2)}, u32[]{:S(2)}) collective-permute-start(bf16[560,1024]{1,0:T(8,128)(2,1)} %collective-permute-done.7.refs_7_.refs_9_.refs_11_), channel_id=1, source_target_pairs={{0,12},{1,13},{2,14},{3,15},{4,0},{5,1},{6,2},{7,3},{8,4},{9,5},{1... | collective-permute-start | bytes 3440648 | tf_op jit(solution)/shard_map/ppermute | solution.py:411
  64.5 25.9 %collective-permute-start.4 = (bf16[528,1024]{1,0:T(8,128)(2,1)}, bf16[528,1024]{1,0:T(8,128)(2,1)}, u32[]{:S(2)}, u32[]{:S(2)}) collective-permute-start(bf16[528,1024]{1,0:T(8,128)(2,1)} %collective-permute-done.refs_2_), channel_id=1, source_target_pairs={{0,1},{1,2},{2,3},{3,0},{4,5},{5,6},{6,7},{7,4},{8,9},{9,10},{10,1... | collective-permute-start | bytes 3244040 | tf_op jit(solution)/shard_map/ppermute | solution.py:410
  66.2 24.2 %collective-permute-start.5 = (bf16[528,1024]{1,0:T(8,128)(2,1)}, bf16[528,1024]{1,0:T(8,128)(2,1)}, u32[]{:S(2)}, u32[]{:S(2)}) collective-permute-start(bf16[528,1024]{1,0:T(8,128)(2,1)} %collective-permute-done.1.refs_3_), channel_id=1, source_target_pairs={{0,3},{1,0},{2,1},{3,2},{4,7},{5,4},{6,5},{7,6},{8,11},{9,8},{10,9... | collective-permute-start | bytes 3244040 | tf_op jit(solution)/shard_map/ppermute | solution.py:411
  90.1 26.2 %copy-start.1 = (f32[4,256]{1,0:T(4,128)S(1)}, f32[4,256]{1,0:T(4,128)}, u32[]{:S(2)}) copy-start(f32[4,256]{1,0:T(4,128)} %deg_ref.1) | copy-start | bytes 12292
  101.6 9.7 %collective-permute-start.12 = (f32[4,64,256]{2,1,0:T(8,128)}, f32[4,64,256]{2,1,0:T(8,128)S(1)}, u32[]{:S(2)}, u32[]{:S(2)}) collective-permute-start(f32[4,64,256]{2,1,0:T(8,128)} %get-tuple-element.52), channel_id=1, source_target_pairs={{0,3},{1,0},{2,1},{3,2},{4,7},{5,4},{6,5},{7,6},{8,11},{9,8},{10,9... | collective-permute-start | bytes 786440 | tf_op jit(solution)/shard_map/ppermute | solution.py:419
  104.7 11.7 %collective-permute-start.13 = (f32[4,64,256]{2,1,0:T(8,128)}, f32[4,64,256]{2,1,0:T(8,128)S(1)}, u32[]{:S(2)}, u32[]{:S(2)}) collective-permute-start(f32[4,64,256]{2,1,0:T(8,128)} %get-tuple-element.53), channel_id=1, source_target_pairs={{0,1},{1,2},{2,3},{3,0},{4,5},{5,6},{6,7},{7,4},{8,9},{9,10},{10,1... | collective-permute-start | bytes 786440 | tf_op jit(solution)/shard_map/ppermute | solution.py:420
  105.8 10.5 %collective-permute-start.14 = (f32[4,64,256]{2,1,0:T(8,128)}, f32[4,64,256]{2,1,0:T(8,128)S(1)}, u32[]{:S(2)}, u32[]{:S(2)}) collective-permute-start(f32[4,64,256]{2,1,0:T(8,128)} %get-tuple-element.54), channel_id=1, source_target_pairs={{0,2},{1,3},{2,0},{3,1},{4,6},{5,7},{6,4},{7,5},{8,10},{9,11},{10,... | collective-permute-start | bytes 786440 | tf_op jit(solution)/shard_map/ppermute | solution.py:421
  116.4 1.0 copy-start
  117.8 1.2 collective-permute-start.15
  119.0 3.7 %collective-permute-start.16 = (f32[32,128]{1,0:T(8,128)S(1)}, f32[32,128]{1,0:T(8,128)S(1)}, u32[]{:S(2)}, u32[]{:S(2)}) collective-permute-start(f32[32,128]{1,0:T(8,128)S(1)} %add.18), channel_id=1, source_target_pairs={{0,32},{16,48},{32,0},{48,16},{64,96},{80,112},{96,64},{112,80},{1... | collective-permute-start | bytes 49160 | tf_op jit(solution)/shard_map/ppermute | solution.py:431
  122.7 6.2 %collective-permute-start.17 = (f32[32,128]{1,0:T(8,128)S(1)}, f32[32,128]{1,0:T(8,128)S(1)}, u32[]{:S(2)}, u32[]{:S(2)}) collective-permute-start(f32[32,128]{1,0:T(8,128)S(1)} %add.19), channel_id=1, source_target_pairs={{0,64},{16,80},{32,96},{48,112},{64,0},{80,16},{96,32},{112,48},{1... | collective-permute-start | bytes 49160 | tf_op jit(solution)/shard_map/ppermute | solution.py:431
  129.0 3.7 %collective-permute-start.18 = (f32[32,128]{1,0:T(8,128)S(1)}, f32[32,128]{1,0:T(8,128)S(1)}, u32[]{:S(2)}, u32[]{:S(2)}) collective-permute-start(f32[32,128]{1,0:T(8,128)S(1)} %add.20), channel_id=1, source_target_pairs={{0,1},{1,0},{2,3},{3,2},{4,5},{5,4},{6,7},{7,6},{8,9},{9,8},{10,11... | collective-permute-start | bytes 49160 | tf_op jit(solution)/shard_map/ppermute | solution.py:431
  132.7 5.2 %collective-permute-start.19 = (f32[32,128]{1,0:T(8,128)S(1)}, f32[32,128]{1,0:T(8,128)S(1)}, u32[]{:S(2)}, u32[]{:S(2)}) collective-permute-start(f32[32,128]{1,0:T(8,128)S(1)} %add.21), channel_id=1, source_target_pairs={{0,2},{1,3},{2,0},{3,1},{4,6},{5,7},{6,4},{7,5},{8,10},{9,11},{10,... | collective-permute-start | bytes 49160 | tf_op jit(solution)/shard_map/ppermute | solution.py:431
  138.0 3.8 %collective-permute-start.20 = (f32[32,128]{1,0:T(8,128)S(1)}, f32[32,128]{1,0:T(8,128)S(1)}, u32[]{:S(2)}, u32[]{:S(2)}) collective-permute-start(f32[32,128]{1,0:T(8,128)S(1)} %add.22), channel_id=1, source_target_pairs={{0,4},{1,5},{2,6},{3,7},{4,0},{5,1},{6,2},{7,3},{8,12},{9,13},{10,... | collective-permute-start | bytes 49160 | tf_op jit(solution)/shard_map/ppermute | solution.py:431
  141.8 5.2 %collective-permute-start.21 = (f32[32,128]{1,0:T(8,128)S(1)}, f32[32,128]{1,0:T(8,128)S(1)}, u32[]{:S(2)}, u32[]{:S(2)}) collective-permute-start(f32[32,128]{1,0:T(8,128)S(1)} %add.23.gram_ref), channel_id=1, source_target_pairs={{0,8},{1,9},{2,10},{3,11},{4,12},{5,13},{6,14},{7,15},{8,0},{9,1},... | collective-permute-start | bytes 49160 | tf_op jit(solution)/shard_map/ppermute | solution.py:431
